TPU v7x, 32 devices: a whole 2x2x4 slice. The times are simulated.
32 devices in a mesh: batch: 4 (over y, x), proto: 8 (over z, core).
Axes of the slice: x: 2, y: 2, z: 4, core: 2. Of those that a mesh axis runs over, the one named last changes fastest.
Arguments:
- features: bfloat16 [2048, 256], P('batch'), may hold values from -6 to 6
- prototypes: bfloat16 [16384, 256], P(('proto', 'batch')), may hold values from -6 to 6
Outputs:
- assignments: bfloat16 [2048, 16384], P('batch', 'proto')
All inputs are finite; a program needn't handle non-finite values.
Results may differ from a plain program's by a relative error of at most 0.0061.
Values may be sent and summed in bfloat16 or wider, within the bound.
No kernel may reach another device: no remote copies, remote signals or barrier semaphores. Data moves between devices by JAX's collectives and lax.ppermute only.
A program may use at most 64 MiB of HBM per device.

v0:
```python
import jax
import jax.numpy as jnp
from jax import lax
from jax.sharding import PartitionSpec as P

ITERS = 3


def unit_rows(matrix):
    values = matrix.astype(jnp.float32)
    scale = lax.rsqrt(1e-06 + jnp.sum(values * values, axis=1, keepdims=True))
    return (values * scale).astype(jnp.bfloat16)


def proto_sums(partial_value):
    return lax.psum(partial_value, "batch")


def image_sums(partial_value):
    return lax.psum(partial_value, "proto")


def local(features, prototypes):
    unit_feat = unit_rows(features)
    scores = jnp.einsum(
        "bd,kd->bk",
        unit_feat,
        unit_rows(lax.all_gather(prototypes, "batch", axis=0, tiled=True)),
        preferred_element_type=jnp.float32,
    )
    weights = jnp.exp(20.0 * scores)
    total_protos = float(weights.shape[1] * lax.axis_size("proto"))
    row_factor = jnp.ones((weights.shape[0],), jnp.float32)
    col_factor = jnp.ones((weights.shape[1],), jnp.float32)
    for step in range(ITERS):
        column_part = jnp.dot(row_factor, weights, precision=lax.Precision.HIGHEST)
        col_factor = 1.0 / proto_sums(column_part)
        row_part = jnp.dot(weights, col_factor, precision=lax.Precision.HIGHEST)
        row_factor = 1.0 / image_sums(row_part)
    scaled = weights * row_factor[:, None] * (total_protos * col_factor)[None, :]
    return scaled.astype(jnp.bfloat16)


def solution(mesh):
    in_specs = (P("batch", None), P(("proto", "batch"), None))
    out_specs = P("batch", "proto")
    return jax.shard_map(local, mesh=mesh, in_specs=in_specs, out_specs=out_specs, check_vma=False)
```

profile of v0, /device:TPU:0, one launch (start us, length us, event | category | flops | bytes accessed | tf_op | source)
XLA Modules:
  0.0 151.8 jit_solution(7662014906515286091)
XLA Ops:
  6.5 0.0 all-gather.2.cloned.1.call-start
  6.5 0.7 all-gather.2.cloned.1.call-update
  7.3 1.1 fusion.4
  8.4 30.2 %all-gather.2.cloned.1.call-done = bf16[2048,256]{1,0:T(8,128)(2,1)} async-done(((bf16[512,256]{1,0:T(8,128)(2,1)}), bf16[2048,256]{1,0:T(8,128)(2,1)}) %all-gather.2.cloned.1.call-update) | async-done | bytes 1048592 | tf_op jit(solution)/shard_map/all_gather | solution.py:28
  38.6 1.6 %fusion = f32[2048]{0:T(1024)S(1)} fusion(bf16[2048,256]{1,0:T(8,128)(2,1)} %all-gather.2.cloned.1.call-done), kind=kLoop, calls=%fused_computation.4 | loop fusion | flops 1570816 | bytes 1056768 | tf_op jit(solution)/shard_map/reduce_sum | solution.py:11
  40.1 2.2 %multiply_exponential_fusion = f32[512,2048]{1,0:T(8,128)S(1)} fusion(bf16[2048,256]{1,0:T(8,128)(2,1)} %all-gather.2.cloned.1.call-done, f32[2048]{0:T(1024)S(1)} %add_rsqrt_fusion, bf16[512,256]{1,0:T(8,128)(2,1)} %param.2, f32[512]{0:T(512)S(1)} %add_rsqrt_fusion.1), kind=kOutput, calls=%fused_computation.1 | convolution fusion | flops 539885568 | bytes 5515264 | tf_op jit(solution)/shard_map/bd,kd->bk/dot_general | solution.py:25
  42.4 0.0 copy-start
  42.4 1.9 %copy-done = f32[512,2048]{1,0:T(8,128)} copy-done((f32[512,2048]{1,0:T(8,128)}, f32[512,2048]{1,0:T(8,128)S(1)}, u32[]{:S(2)}) %copy-start) | copy-done | bytes 4194328
  44.3 2.1 %fusion.8 = f32[1,2048]{1,0:T(1,128)S(1)} fusion(f32[512,2048]{1,0:T(8,128)S(1)} %multiply_exponential_fusion), kind=kOutput, calls=%fused_computation.18 | convolution fusion | flops 12582912 | bytes 4202496 | tf_op jit(solution)/shard_map/dot_general | solution.py:36
  46.4 9.1 %psum.42 = f32[2048]{0:T(1024)S(1)} all-reduce(f32[2048]{0:T(1024)S(1)} %bitcast.27), channel_id=1, replica_groups=mesh['batch'=4,'proto'=8] {'batch'}, use_global_device_ids=true, to_apply=%region_2.0 | all-reduce | flops 2048 | bytes 16384 | tf_op jit(solution)/shard_map/psum | solution.py:16
  55.5 5.8 %fusion.11 = f32[1,512]{1,0:T(1,128)S(1)} fusion(f32[512,2048]{1,0:T(8,128)} %copy-done, f32[2048,1]{0,1:T(1,128)S(1)} %bitcast.23), kind=kOutput, calls=%fused_computation.24 | convolution fusion | flops 12582912 | bytes 4204544 | tf_op jit(solution)/shard_map/dot_general | solution.py:38
  61.2 14.3 %psum.43 = f32[512]{0:T(512)S(1)} all-reduce(f32[512]{0:T(512)S(1)} %bitcast.28), channel_id=1, replica_groups=mesh['batch'=4,'proto'=8] {'proto'}, use_global_device_ids=true, to_apply=%region_3.0 | all-reduce | flops 512 | bytes 4096 | tf_op jit(solution)/shard_map/psum | solution.py:20
  75.6 4.3 %fusion.12 = f32[1,2048]{1,0:T(1,128)S(1)} fusion(f32[512,1]{0,1:T(1,128)S(1)} %bitcast.29, f32[512,2048]{1,0:T(8,128)} %copy-done), kind=kOutput, calls=%fused_computation.25 | convolution fusion | flops 12582912 | bytes 4204544 | tf_op jit(solution)/shard_map/dot_general | solution.py:36
  79.8 9.1 %psum.44 = f32[2048]{0:T(1024)S(1)} all-reduce(f32[2048]{0:T(1024)S(1)} %bitcast.24), channel_id=1, replica_groups=mesh['batch'=4,'proto'=8] {'batch'}, use_global_device_ids=true, to_apply=%region_4.0 | all-reduce | flops 2048 | bytes 16384 | tf_op jit(solution)/shard_map/psum | solution.py:16
  89.0 5.8 %fusion.13 = f32[1,512]{1,0:T(1,128)S(1)} fusion(f32[512,2048]{1,0:T(8,128)} %copy-done, f32[2048,1]{0,1:T(1,128)S(1)} %bitcast.25), kind=kOutput, calls=%fused_computation.26 | convolution fusion | flops 12582912 | bytes 4204544 | tf_op jit(solution)/shard_map/dot_general | solution.py:38
  94.7 13.6 %psum.45 = f32[512]{0:T(512)S(1)} all-reduce(f32[512]{0:T(512)S(1)} %bitcast.30), channel_id=1, replica_groups=mesh['batch'=4,'proto'=8] {'proto'}, use_global_device_ids=true, to_apply=%region_5.0 | all-reduce | flops 512 | bytes 4096 | tf_op jit(solution)/shard_map/psum | solution.py:20
  108.3 4.3 %fusion.14 = f32[1,2048]{1,0:T(1,128)S(1)} fusion(f32[512,1]{0,1:T(1,128)S(1)} %bitcast.31, f32[512,2048]{1,0:T(8,128)} %copy-done), kind=kOutput, calls=%fused_computation.27 | convolution fusion | flops 12582912 | bytes 4204544 | tf_op jit(solution)/shard_map/dot_general | solution.py:36
  112.6 9.1 %psum.46 = f32[2048]{0:T(1024)S(1)} all-reduce(f32[2048]{0:T(1024)S(1)} %bitcast.26), channel_id=1, replica_groups=mesh['batch'=4,'proto'=8] {'batch'}, use_global_device_ids=true, to_apply=%region_6.0 | all-reduce | flops 2048 | bytes 16384 | tf_op jit(solution)/shard_map/psum | solution.py:16
  121.7 5.8 %fusion.15 = f32[1,512]{1,0:T(1,128)S(1)} fusion(f32[512,2048]{1,0:T(8,128)} %copy-done, f32[2048,1]{0,1:T(1,128)S(1)} %bitcast.22), kind=kOutput, calls=%fused_computation.28 | convolution fusion | flops 12582912 | bytes 4204544 | tf_op jit(solution)/shard_map/dot_general | solution.py:38
  127.4 13.6 %psum.47 = f32[512]{0:T(512)S(1)} all-reduce(f32[512]{0:T(512)S(1)} %bitcast.32), channel_id=1, replica_groups=mesh['batch'=4,'proto'=8] {'proto'}, use_global_device_ids=true, to_apply=%region_7.0 | all-reduce | flops 512 | bytes 4096 | tf_op jit(solution)/shard_map/psum | solution.py:20
  141.0 3.9 %multiply_convert_fusion = bf16[512,2048]{1,0:T(8,128)(2,1)} fusion(f32[512,2048]{1,0:T(8,128)} %copy-done, f32[2048]{0:T(1024)S(1)} %get-tuple-element.6, f32[512]{0:T(512)S(1)} %broadcast_divide_fusion.5), kind=kLoop, calls=%fused_computation | loop fusion | flops 3145728 | bytes 6301696 | tf_op jit(solution)/shard_map/convert_element_type | solution.py:41
  (8 shorter events, 0.0 us)
Async XLA Ops:
  6.5 32.0 %all-gather.2.cloned.1.call-start = ((), (), s32[]{:S(2)}) async-start(), calls=%async_computation | async-start | bytes 1310720 | tf_op jit(solution)/shard_map/all_gather | solution.py:28
  42.4 1.9 %copy-start = (f32[512,2048]{1,0:T(8,128)}, f32[512,2048]{1,0:T(8,128)S(1)}, u32[]{:S(2)}) copy-start(f32[512,2048]{1,0:T(8,128)S(1)} %multiply_exponential_fusion) | copy-start | bytes 12582916
Sparse Core Ops, SparseCore 0:
  9.2 29.3 all-gather.1
where the time goes:
time: 152 us
  blocking collectives  68.7 us (45%)
  waiting for transfers between devices  30.9 us (20%)
  matrix products  30.1 us (20%)
  between operations  13.5 us (9%)
  other arithmetic  6.63 us (4%)
  local copies, waits for them, and re-layouts  1.92 us (1%)
    psum x3, blocking collectives, image_sums(): return lax.psum(partial_value, 'proto')  41.5 us
    all_gather x1, waiting for transfers between devices, local(): lax.all_gather(prototypes, 'batch', axis=0, tiled=True)  30.2 us
    psum x3, blocking collectives, proto_sums(): return lax.psum(partial_value, 'batch')  27.2 us
    dot_general x3, matrix products, local(): row_part = jnp.dot(weights, col_factor, precision=lax.Precision.HIGHEST)  17.3 us
    dot_general x3, matrix products, local(): column_part = jnp.dot(row_factor, weights, precision=lax.Precision.HIGHEST)  10.6 us
    convert_element_type x1, other arithmetic, local(): return scaled.astype(jnp.bfloat16)  3.92 us
  transfers between devices with their start and end apart: 1, of which 1 were waited for; matrix products, arithmetic and copies ran while one was open for 1% of the time, Pallas kernels for 0%

commit v1 on v0

--- a/solution.py
+++ b/solution.py
@@ -4,6 +4,7 @@
 from jax.sharding import PartitionSpec as P
 
 ITERS = 3
+MOST_PARTNERS = 8
 
 
 def unit_rows(matrix):
@@ -12,12 +13,53 @@
     return (values * scale).astype(jnp.bfloat16)
 
 
+def partners(size, stride, count, step):
+    pairs = []
+    for index in range(size):
+        place = index // stride % count
+        other = place ^ step if count & (count - 1) == 0 else (place + step) % count
+        pairs.append((index, index + (other - place) * stride))
+    return pairs
+
+
+def from_others(value, axis, stride, count):
+    size = lax.axis_size(axis)
+    return [lax.ppermute(value, axis, partners(size, stride, count, step)) for step in range(1, count)]
+
+
+def group_sum(value, axis, stride, count):
+    total = value
+    for other in from_others(value, axis, stride, count):
+        total = total + other
+    return total
+
+
 def proto_sums(partial_value):
-    return lax.psum(partial_value, "batch")
+    size = lax.axis_size("batch")
+    if size > MOST_PARTNERS:
+        return lax.psum(partial_value, "batch")
+    return group_sum(partial_value, "batch", 1, size)
 
 
 def image_sums(partial_value):
-    return lax.psum(partial_value, "proto")
+    size = lax.axis_size("proto")
+    if size > 2 * MOST_PARTNERS or size % 2:
+        return lax.psum(partial_value, "proto")
+    pair = group_sum(partial_value, "proto", 1, 2)
+    return group_sum(pair, "proto", 2, size // 2)
+
+
+def gather_prototypes(unit_proto):
+    size = lax.axis_size("batch")
+    if size > MOST_PARTNERS:
+        return lax.all_gather(unit_proto, "batch", axis=0, tiled=True)
+    blocks = [unit_proto] + from_others(unit_proto, "batch", 1, size)
+    place = lax.axis_index("batch")
+    order = [jnp.bitwise_xor(place, step) if size & (size - 1) == 0 else (place - step) % size for step in range(size)]
+    gathered = jnp.zeros((size,) + unit_proto.shape, unit_proto.dtype)
+    for index, block in zip(order, blocks):
+        gathered = lax.dynamic_update_index_in_dim(gathered, block, index, 0)
+    return gathered.reshape(-1, unit_proto.shape[1])
 
 
 def local(features, prototypes):
@@ -25,7 +67,7 @@
     scores = jnp.einsum(
         "bd,kd->bk",
         unit_feat,
-        unit_rows(lax.all_gather(prototypes, "batch", axis=0, tiled=True)),
+        gather_prototypes(unit_rows(prototypes)),
         preferred_element_type=jnp.float32,
     )
     weights = jnp.exp(20.0 * scores)

time: 152 us -> 83.3 us (0.55)
  blocking collectives: 68.7 us -> 0 us
  starting transfers between devices: 0.01 us -> 28.2 us
  between operations: 13.5 us -> 0.12 us
  matrix products: 30.1 us -> 19 us
  local copies, waits for them, and re-layouts: 1.92 us -> 0.14 us
  other arithmetic: 6.63 us -> 5.08 us
    psum x6 -> x0, blocking collectives: 68.7 us -> none  [the longest x3 41.5 us: image_sums(): return lax.psum(partial_value, 'proto')]
    ppermute x0 -> x24, waiting for transfers between devices: none -> 30.4 us  [from_others(): lax.ppermute(value, axis, partners(size, stride, count, step))]
    all_gather x1 -> x0, waiting for transfers between devices: 30.2 us -> none  [local(): lax.all_gather(prototypes, 'batch', axis=0, tiled=True)]
    ppermute x0 -> x24, starting transfers between devices: none -> 28.2 us  [from_others(): lax.ppermute(value, axis, partners(size, stride, count, step))]
    dot_general x3, matrix products: 17.3 us -> 11.1 us  [local(): row_part = jnp.dot(weights, col_factor, precision=lax.Precision.HIGHEST)]
    dot_general x3, matrix products: 10.6 us -> 6.22 us  [local(): column_part = jnp.dot(row_factor, weights, precision=lax.Precision.HIGHEST)]
    convert_element_type x1, other arithmetic: 3.92 us -> 1.73 us  [local(): return scaled.astype(jnp.bfloat16)]
    unnamed x2 -> x0, local copies, waits for them, and re-layouts: 1.92 us -> none
  transfers between devices with their start and end apart: 1 -> 24, of which waited for: 1 -> 20; matrix products, arithmetic and copies ran while one was open for 1% -> 1% of each run, Pallas kernels for 0% -> 0%
where the time goes in v1:
time: 83.3 us; the launch traced here: 83 us
  waiting for transfers between devices  30.4 us (36%)
  starting transfers between devices  28.2 us (34%)
  matrix products  19 us (23%)
  other arithmetic  5.08 us (6%)
    ppermute x24, waiting for transfers between devices, from_others(): lax.ppermute(value, axis, partners(size, stride, count, step))  30.4 us
    ppermute x24, starting transfers between devices, from_others(): lax.ppermute(value, axis, partners(size, stride, count, step))  28.2 us
    dot_general x3, matrix products, local(): row_part = jnp.dot(weights, col_factor, precision=lax.Precision.HIGHEST)  11.1 us
    dot_general x3, matrix products, local(): column_part = jnp.dot(row_factor, weights, precision=lax.Precision.HIGHEST)  6.22 us
    reduce_sum x2, other arithmetic, unit_rows(): scale = lax.rsqrt(1e-06 + jnp.sum(values * values, axis=1, keepdims=True))  2.19 us
    convert_element_type x1, other arithmetic, local(): return scaled.astype(jnp.bfloat16)  1.73 us
    dot_general x1, matrix products, local(): jnp.einsum('bd,kd->bk', unit_feat, gather_prototypes(unit_rows(prototypes...  1.72 us
  transfers between devices with their start and end apart: 24, of which 20 were waited for; matrix products, arithmetic and copies ran while one was open for 1% of the time, Pallas kernels for 0%

profile of v1, /device:TPU:0, one launch (start us, length us, event | category | flops | bytes accessed | tf_op | source)
XLA Modules:
  0.0 83.0 jit_solution(7302471902944002122)
XLA Ops:
  0.0 1.1 %fusion.2 = f32[512]{0:T(512)S(1)} fusion(bf16[512,256]{1,0:T(8,128)(2,1)} %param.3), kind=kLoop, calls=%fused_computation.8 | loop fusion | flops 392704 | bytes 264192 | tf_op jit(solution)/shard_map/reduce_sum | solution.py:12
  1.2 1.1 %bitcast_dynamic-update-slice_fusion.3 = (bf16[4,512,256]{2,1,0:T(8,128)(2,1)S(1)}, bf16[512,256]{1,0:T(8,128)(2,1)S(1)}) fusion(bf16[4,512,256]{2,1,0:T(8,128)(2,1)S(1)} %broadcast_in_dim.20, s32[]{:T(128)S(6)} %select_n.13, f32[512]{0:T(512)S(1)} %add_rsqrt_fusion, bf16[512,256]{1,0:T(8,128)(2,1)} %param.3), kind=kLoop, calls=%fused_computation.13 | loop fusion | flops 393216 | bytes 788484 | tf_op jit(solution)/shard_map/jit(dynamic_update_index_in_dim)/dynamic_update_slice | solution.py:61
  2.3 3.0 %collective-permute-start.1 = (bf16[512,256]{1,0:T(8,128)(2,1)S(1)}, bf16[512,256]{1,0:T(8,128)(2,1)S(1)}, u32[]{:S(2)}, u32[]{:S(2)}) collective-permute-start(bf16[512,256]{1,0:T(8,128)(2,1)S(1)} %get-tuple-element.8), channel_id=1, source_target_pairs={{0,16},{8,24},{16,0},{24,8},{1,17},{9,25},{17,1},{25,9},{2,18},{10... | collective-permute-start | bytes 786440 | tf_op jit(solution)/shard_map/ppermute | solution.py:27
  5.3 1.5 %collective-permute-start = (bf16[512,256]{1,0:T(8,128)(2,1)S(1)}, bf16[512,256]{1,0:T(8,128)(2,1)S(1)}, u32[]{:S(2)}, u32[]{:S(2)}) collective-permute-start(bf16[512,256]{1,0:T(8,128)(2,1)S(1)} %get-tuple-element.8), channel_id=1, source_target_pairs={{0,8},{8,0},{16,24},{24,16},{1,9},{9,1},{17,25},{25,17},{2,10},{10... | collective-permute-start | bytes 786440 | tf_op jit(solution)/shard_map/ppermute | solution.py:27
  6.9 1.1 %fusion = f32[512]{0:T(512)S(1)} fusion(bf16[512,256]{1,0:T(8,128)(2,1)} %param.2), kind=kLoop, calls=%fused_computation.6 | loop fusion | flops 392704 | bytes 264192 | tf_op jit(solution)/shard_map/reduce_sum | solution.py:12
  8.0 6.6 %collective-permute-done = bf16[512,256]{1,0:T(8,128)(2,1)S(1)} collective-permute-done((bf16[512,256]{1,0:T(8,128)(2,1)S(1)}, bf16[512,256]{1,0:T(8,128)(2,1)S(1)}, u32[]{:S(2)}, u32[]{:S(2)}) %collective-permute-start) | collective-permute-done | bytes 262176 | tf_op jit(solution)/shard_map/ppermute | solution.py:27
  14.6 3.9 %collective-permute-done.2 = bf16[512,256]{1,0:T(8,128)(2,1)S(1)} collective-permute-done((bf16[512,256]{1,0:T(8,128)(2,1)S(1)}, bf16[512,256]{1,0:T(8,128)(2,1)S(1)}, u32[]{:S(2)}, u32[]{:S(2)}) %collective-permute-start.2) | collective-permute-done | bytes 262176 | tf_op jit(solution)/shard_map/ppermute | solution.py:27
  18.5 1.7 %multiply_exponential_fusion = f32[512,2048]{1,0:T(8,128)S(1)} fusion(bf16[2048,256]{1,0:T(8,128)(2,1)S(1)} %bitcast.32, bf16[512,256]{1,0:T(8,128)(2,1)} %param.2, f32[512]{0:T(512)S(1)} %add_rsqrt_fusion.1), kind=kOutput, calls=%fused_computation.1 | convolution fusion | flops 538312704 | bytes 5507072 | tf_op jit(solution)/shard_map/bd,kd->bk/dot_general | solution.py:67
  20.3 2.1 %fusion.6 = f32[1,2048]{1,0:T(1,128)S(1)} fusion(f32[512,2048]{1,0:T(8,128)S(1)} %multiply_exponential_fusion), kind=kOutput, calls=%fused_computation.24 | convolution fusion | flops 12582912 | bytes 4202496 | tf_op jit(solution)/shard_map/dot_general | solution.py:78
  22.3 2.6 %collective-permute-start.5 = (f32[2048]{0:T(1024)S(1)}, f32[2048]{0:T(1024)S(1)}, u32[]{:S(2)}, u32[]{:S(2)}) collective-permute-start(f32[2048]{0:T(1024)S(1)} %bitcast.37), channel_id=1, source_target_pairs={{0,24},{8,16},{16,8},{24,0},{1,25},{9,17},{17,9},{25,1},{2,26},{10... | collective-permute-start | bytes 24584 | tf_op jit(solution)/shard_map/ppermute | solution.py:27
  25.8 1.1 %collective-permute-done.5 = f32[2048]{0:T(1024)S(1)} collective-permute-done((f32[2048]{0:T(1024)S(1)}, f32[2048]{0:T(1024)S(1)}, u32[]{:S(2)}, u32[]{:S(2)}) %collective-permute-start.5) | collective-permute-done | bytes 8224 | tf_op jit(solution)/shard_map/ppermute | solution.py:27
  26.9 1.7 %collective-permute-done.4 = f32[2048]{0:T(1024)S(1)} collective-permute-done((f32[2048]{0:T(1024)S(1)}, f32[2048]{0:T(1024)S(1)}, u32[]{:S(2)}, u32[]{:S(2)}) %collective-permute-start.4) | collective-permute-done | bytes 8224 | tf_op jit(solution)/shard_map/ppermute | solution.py:27
  29.1 3.6 %fusion.10 = f32[1,512]{1,0:T(1,128)S(1)} fusion(f32[512,2048]{1,0:T(8,128)S(1)} %multiply_exponential_fusion, f32[2048,1]{0,1:T(1,128)S(1)} %bitcast.41), kind=kOutput, calls=%fused_computation.27 | convolution fusion | flops 12582912 | bytes 4204544 | tf_op jit(solution)/shard_map/dot_general | solution.py:80
  32.7 1.2 %collective-permute-done.6 = f32[512]{0:T(512)S(1)} collective-permute-done((f32[512]{0:T(512)S(1)}, f32[512]{0:T(512)S(1)}, u32[]{:S(2)}, u32[]{:S(2)}) %collective-permute-start.6) | collective-permute-done | bytes 2080 | tf_op jit(solution)/shard_map/ppermute | solution.py:27
  33.9 3.6 %collective-permute-start.9 = (f32[512]{0:T(512)S(1)}, f32[512]{0:T(512)S(1)}, u32[]{:S(2)}, u32[]{:S(2)}) collective-permute-start(f32[512]{0:T(512)S(1)} %add.101), channel_id=1, source_target_pairs={{0,6},{1,7},{2,4},{3,5},{4,2},{5,3},{6,0},{7,1},{8,14},{9,15},{10,... | collective-permute-start | bytes 6152 | tf_op jit(solution)/shard_map/ppermute | solution.py:27
  39.3 2.7 %collective-permute-done.8 = f32[512]{0:T(512)S(1)} collective-permute-done((f32[512]{0:T(512)S(1)}, f32[512]{0:T(512)S(1)}, u32[]{:S(2)}, u32[]{:S(2)}) %collective-permute-start.8) | collective-permute-done | bytes 2080 | tf_op jit(solution)/shard_map/ppermute | solution.py:27
  42.0 2.1 %fusion.11 = f32[1,2048]{1,0:T(1,128)S(1)} fusion(f32[512,1]{0,1:T(1,128)S(1)} %bitcast.54, f32[512,2048]{1,0:T(8,128)S(1)} %multiply_exponential_fusion), kind=kOutput, calls=%fused_computation.28 | convolution fusion | flops 12582912 | bytes 4204544 | tf_op jit(solution)/shard_map/dot_general | solution.py:78
  44.1 1.5 %collective-permute-start.12 = (f32[2048]{0:T(1024)S(1)}, f32[2048]{0:T(1024)S(1)}, u32[]{:S(2)}, u32[]{:S(2)}) collective-permute-start(f32[2048]{0:T(1024)S(1)} %bitcast.33), channel_id=1, source_target_pairs={{0,24},{8,16},{16,8},{24,0},{1,25},{9,17},{17,9},{25,1},{2,26},{10... | collective-permute-start | bytes 24584 | tf_op jit(solution)/shard_map/ppermute | solution.py:27
  46.1 1.5 %collective-permute-start.10 = (f32[2048]{0:T(1024)S(1)}, f32[2048]{0:T(1024)S(1)}, u32[]{:S(2)}, u32[]{:S(2)}) collective-permute-start(f32[2048]{0:T(1024)S(1)} %bitcast.35), channel_id=1, source_target_pairs={{0,8},{8,0},{16,24},{24,16},{1,9},{9,1},{17,25},{25,17},{2,10},{10... | collective-permute-start | bytes 24584 | tf_op jit(solution)/shard_map/ppermute | solution.py:27
  47.6 1.1 %collective-permute-done.12 = f32[2048]{0:T(1024)S(1)} collective-permute-done((f32[2048]{0:T(1024)S(1)}, f32[2048]{0:T(1024)S(1)}, u32[]{:S(2)}, u32[]{:S(2)}) %collective-permute-start.12) | collective-permute-done | bytes 8224 | tf_op jit(solution)/shard_map/ppermute | solution.py:27
  49.7 3.8 %fusion.12 = f32[1,512]{1,0:T(1,128)S(1)} fusion(f32[512,2048]{1,0:T(8,128)S(1)} %multiply_exponential_fusion, f32[2048,1]{0,1:T(1,128)S(1)} %bitcast.42), kind=kOutput, calls=%fused_computation.29 | convolution fusion | flops 12582912 | bytes 4204544 | tf_op jit(solution)/shard_map/dot_general | solution.py:80
  53.6 1.2 %collective-permute-done.13 = f32[512]{0:T(512)S(1)} collective-permute-done((f32[512]{0:T(512)S(1)}, f32[512]{0:T(512)S(1)}, u32[]{:S(2)}, u32[]{:S(2)}) %collective-permute-start.13) | collective-permute-done | bytes 2080 | tf_op jit(solution)/shard_map/ppermute | solution.py:27
  54.7 1.5 %collective-permute-start.16 = (f32[512]{0:T(512)S(1)}, f32[512]{0:T(512)S(1)}, u32[]{:S(2)}, u32[]{:S(2)}) collective-permute-start(f32[512]{0:T(512)S(1)} %add.108), channel_id=1, source_target_pairs={{0,6},{1,7},{2,4},{3,5},{4,2},{5,3},{6,0},{7,1},{8,14},{9,15},{10,... | collective-permute-start | bytes 6152 | tf_op jit(solution)/shard_map/ppermute | solution.py:27
  56.8 2.4 %collective-permute-start.14 = (f32[512]{0:T(512)S(1)}, f32[512]{0:T(512)S(1)}, u32[]{:S(2)}, u32[]{:S(2)}) collective-permute-start(f32[512]{0:T(512)S(1)} %add.108), channel_id=1, source_target_pairs={{0,2},{1,3},{2,0},{3,1},{4,6},{5,7},{6,4},{7,5},{8,10},{9,11},{10,... | collective-permute-start | bytes 6152 | tf_op jit(solution)/shard_map/ppermute | solution.py:27
  60.7 2.1 %fusion.13 = f32[1,2048]{1,0:T(1,128)S(1)} fusion(f32[512,1]{0,1:T(1,128)S(1)} %bitcast.55, f32[512,2048]{1,0:T(8,128)S(1)} %multiply_exponential_fusion), kind=kOutput, calls=%fused_computation.30 | convolution fusion | flops 12582912 | bytes 4204544 | tf_op jit(solution)/shard_map/dot_general | solution.py:78
  62.8 2.5 %collective-permute-start.19 = (f32[2048]{0:T(1024)S(1)}, f32[2048]{0:T(1024)S(1)}, u32[]{:S(2)}, u32[]{:S(2)}) collective-permute-start(f32[2048]{0:T(1024)S(1)} %bitcast.43), channel_id=1, source_target_pairs={{0,24},{8,16},{16,8},{24,0},{1,25},{9,17},{17,9},{25,1},{2,26},{10... | collective-permute-start | bytes 24584 | tf_op jit(solution)/shard_map/ppermute | solution.py:27
  67.3 1.5 %collective-permute-done.18 = f32[2048]{0:T(1024)S(1)} collective-permute-done((f32[2048]{0:T(1024)S(1)}, f32[2048]{0:T(1024)S(1)}, u32[]{:S(2)}, u32[]{:S(2)}) %collective-permute-start.18) | collective-permute-done | bytes 8224 | tf_op jit(solution)/shard_map/ppermute | solution.py:27
  69.4 3.6 %fusion.14 = f32[1,512]{1,0:T(1,128)S(1)} fusion(f32[512,2048]{1,0:T(8,128)S(1)} %multiply_exponential_fusion, f32[2048,1]{0,1:T(1,128)S(1)} %bitcast.47), kind=kOutput, calls=%fused_computation.31 | convolution fusion | flops 12582912 | bytes 4204544 | tf_op jit(solution)/shard_map/dot_general | solution.py:80
  73.0 1.2 %collective-permute-done.20 = f32[512]{0:T(512)S(1)} collective-permute-done((f32[512]{0:T(512)S(1)}, f32[512]{0:T(512)S(1)}, u32[]{:S(2)}, u32[]{:S(2)}) %collective-permute-start.20) | collective-permute-done | bytes 2080 | tf_op jit(solution)/shard_map/ppermute | solution.py:27
  74.2 2.6 %collective-permute-start.23 = (f32[512]{0:T(512)S(1)}, f32[512]{0:T(512)S(1)}, u32[]{:S(2)}, u32[]{:S(2)}) collective-permute-start(f32[512]{0:T(512)S(1)} %add.115), channel_id=1, source_target_pairs={{0,6},{1,7},{2,4},{3,5},{4,2},{5,3},{6,0},{7,1},{8,14},{9,15},{10,... | collective-permute-start | bytes 6152 | tf_op jit(solution)/shard_map/ppermute | solution.py:27
  79.6 1.7 %collective-permute-done.22 = f32[512]{0:T(512)S(1)} collective-permute-done((f32[512]{0:T(512)S(1)}, f32[512]{0:T(512)S(1)}, u32[]{:S(2)}, u32[]{:S(2)}) %collective-permute-start.22) | collective-permute-done | bytes 2080 | tf_op jit(solution)/shard_map/ppermute | solution.py:27
  81.3 1.7 %multiply_convert_fusion = bf16[512,2048]{1,0:T(8,128)(2,1)} fusion(f32[512,2048]{1,0:T(8,128)S(1)} %multiply_exponential_fusion, f32[2048]{0:T(1024)S(1)} %get-tuple-element.5, f32[512]{0:T(512)S(1)} %add_divide_fusion.3), kind=kLoop, calls=%fused_computation | loop fusion | flops 3145728 | bytes 6301696 | tf_op jit(solution)/shard_map/convert_element_type | solution.py:83
  (42 shorter events, 12.6 us)
Async XLA Ops:
  2.3 12.3 %collective-permute-start.1 = (bf16[512,256]{1,0:T(8,128)(2,1)S(1)}, bf16[512,256]{1,0:T(8,128)(2,1)S(1)}, u32[]{:S(2)}, u32[]{:S(2)}) collective-permute-start(bf16[512,256]{1,0:T(8,128)(2,1)S(1)} %get-tuple-element.8), channel_id=1, source_target_pairs={{0,16},{8,24},{16,0},{24,8},{1,17},{9,25},{17,1},{25,9},{2,18},{10... | collective-permute-start | bytes 786440 | tf_op jit(solution)/shard_map/ppermute | solution.py:27
  5.3 9.2 %collective-permute-start = (bf16[512,256]{1,0:T(8,128)(2,1)S(1)}, bf16[512,256]{1,0:T(8,128)(2,1)S(1)}, u32[]{:S(2)}, u32[]{:S(2)}) collective-permute-start(bf16[512,256]{1,0:T(8,128)(2,1)S(1)} %get-tuple-element.8), channel_id=1, source_target_pairs={{0,8},{8,0},{16,24},{24,16},{1,9},{9,1},{17,25},{25,17},{2,10},{10... | collective-permute-start | bytes 786440 | tf_op jit(solution)/shard_map/ppermute | solution.py:27
  6.8 11.7 %collective-permute-start.2 = (bf16[512,256]{1,0:T(8,128)(2,1)S(1)}, bf16[512,256]{1,0:T(8,128)(2,1)S(1)}, u32[]{:S(2)}, u32[]{:S(2)}) collective-permute-start(bf16[512,256]{1,0:T(8,128)(2,1)S(1)} %get-tuple-element.8), channel_id=1, source_target_pairs={{0,24},{8,16},{16,8},{24,0},{1,25},{9,17},{17,9},{25,1},{2,26},{10... | collective-permute-start | bytes 786440 | tf_op jit(solution)/shard_map/ppermute | solution.py:27
  22.3 4.6 %collective-permute-start.5 = (f32[2048]{0:T(1024)S(1)}, f32[2048]{0:T(1024)S(1)}, u32[]{:S(2)}, u32[]{:S(2)}) collective-permute-start(f32[2048]{0:T(1024)S(1)} %bitcast.37), channel_id=1, source_target_pairs={{0,24},{8,16},{16,8},{24,0},{1,25},{9,17},{17,9},{25,1},{2,26},{10... | collective-permute-start | bytes 24584 | tf_op jit(solution)/shard_map/ppermute | solution.py:27
  24.9 3.7 %collective-permute-start.4 = (f32[2048]{0:T(1024)S(1)}, f32[2048]{0:T(1024)S(1)}, u32[]{:S(2)}, u32[]{:S(2)}) collective-permute-start(f32[2048]{0:T(1024)S(1)} %bitcast.38), channel_id=1, source_target_pairs={{0,16},{8,24},{16,0},{24,8},{1,17},{9,25},{17,1},{25,9},{2,18},{10... | collective-permute-start | bytes 24584 | tf_op jit(solution)/shard_map/ppermute | solution.py:27
  25.4 3.7 %collective-permute-start.3 = (f32[2048]{0:T(1024)S(1)}, f32[2048]{0:T(1024)S(1)}, u32[]{:S(2)}, u32[]{:S(2)}) collective-permute-start(f32[2048]{0:T(1024)S(1)} %bitcast.39), channel_id=1, source_target_pairs={{0,8},{8,0},{16,24},{24,16},{1,9},{9,1},{17,25},{25,17},{2,10},{10... | collective-permute-start | bytes 24584 | tf_op jit(solution)/shard_map/ppermute | solution.py:27
  32.7 1.2 %collective-permute-start.6 = (f32[512]{0:T(512)S(1)}, f32[512]{0:T(512)S(1)}, u32[]{:S(2)}, u32[]{:S(2)}) collective-permute-start(f32[512]{0:T(512)S(1)} %bitcast.48), channel_id=1, source_target_pairs={{0,1},{1,0},{2,3},{3,2},{4,5},{5,4},{6,7},{7,6},{8,9},{9,8},{10,11... | collective-permute-start | bytes 6152 | tf_op jit(solution)/shard_map/ppermute | solution.py:27
  33.9 5.4 %collective-permute-start.9 = (f32[512]{0:T(512)S(1)}, f32[512]{0:T(512)S(1)}, u32[]{:S(2)}, u32[]{:S(2)}) collective-permute-start(f32[512]{0:T(512)S(1)} %add.101), channel_id=1, source_target_pairs={{0,6},{1,7},{2,4},{3,5},{4,2},{5,3},{6,0},{7,1},{8,14},{9,15},{10,... | collective-permute-start | bytes 6152 | tf_op jit(solution)/shard_map/ppermute | solution.py:27
  37.5 4.5 %collective-permute-start.8 = (f32[512]{0:T(512)S(1)}, f32[512]{0:T(512)S(1)}, u32[]{:S(2)}, u32[]{:S(2)}) collective-permute-start(f32[512]{0:T(512)S(1)} %add.101), channel_id=1, source_target_pairs={{0,4},{1,5},{2,6},{3,7},{4,0},{5,1},{6,2},{7,3},{8,12},{9,13},{10,... | collective-permute-start | bytes 6152 | tf_op jit(solution)/shard_map/ppermute | solution.py:27
  37.5 4.5 %collective-permute-start.7 = (f32[512]{0:T(512)S(1)}, f32[512]{0:T(512)S(1)}, u32[]{:S(2)}, u32[]{:S(2)}) collective-permute-start(f32[512]{0:T(512)S(1)} %add.101), channel_id=1, source_target_pairs={{0,2},{1,3},{2,0},{3,1},{4,6},{5,7},{6,4},{7,5},{8,10},{9,11},{10,... | collective-permute-start | bytes 6152 | tf_op jit(solution)/shard_map/ppermute | solution.py:27
  44.1 4.6 %collective-permute-start.12 = (f32[2048]{0:T(1024)S(1)}, f32[2048]{0:T(1024)S(1)}, u32[]{:S(2)}, u32[]{:S(2)}) collective-permute-start(f32[2048]{0:T(1024)S(1)} %bitcast.33), channel_id=1, source_target_pairs={{0,24},{8,16},{16,8},{24,0},{1,25},{9,17},{17,9},{25,1},{2,26},{10... | collective-permute-start | bytes 24584 | tf_op jit(solution)/shard_map/ppermute | solution.py:27
  45.6 3.7 %collective-permute-start.11 = (f32[2048]{0:T(1024)S(1)}, f32[2048]{0:T(1024)S(1)}, u32[]{:S(2)}, u32[]{:S(2)}) collective-permute-start(f32[2048]{0:T(1024)S(1)} %bitcast.34), channel_id=1, source_target_pairs={{0,16},{8,24},{16,0},{24,8},{1,17},{9,25},{17,1},{25,9},{2,18},{10... | collective-permute-start | bytes 24584 | tf_op jit(solution)/shard_map/ppermute | solution.py:27
  46.1 3.7 %collective-permute-start.10 = (f32[2048]{0:T(1024)S(1)}, f32[2048]{0:T(1024)S(1)}, u32[]{:S(2)}, u32[]{:S(2)}) collective-permute-start(f32[2048]{0:T(1024)S(1)} %bitcast.35), channel_id=1, source_target_pairs={{0,8},{8,0},{16,24},{24,16},{1,9},{9,1},{17,25},{25,17},{2,10},{10... | collective-permute-start | bytes 24584 | tf_op jit(solution)/shard_map/ppermute | solution.py:27
  53.5 1.2 %collective-permute-start.13 = (f32[512]{0:T(512)S(1)}, f32[512]{0:T(512)S(1)}, u32[]{:S(2)}, u32[]{:S(2)}) collective-permute-start(f32[512]{0:T(512)S(1)} %bitcast.50), channel_id=1, source_target_pairs={{0,1},{1,0},{2,3},{3,2},{4,5},{5,4},{6,7},{7,6},{8,9},{9,8},{10,11... | collective-permute-start | bytes 6152 | tf_op jit(solution)/shard_map/ppermute | solution.py:27
  54.7 5.4 %collective-permute-start.16 = (f32[512]{0:T(512)S(1)}, f32[512]{0:T(512)S(1)}, u32[]{:S(2)}, u32[]{:S(2)}) collective-permute-start(f32[512]{0:T(512)S(1)} %add.108), channel_id=1, source_target_pairs={{0,6},{1,7},{2,4},{3,5},{4,2},{5,3},{6,0},{7,1},{8,14},{9,15},{10,... | collective-permute-start | bytes 6152 | tf_op jit(solution)/shard_map/ppermute | solution.py:27
  56.2 4.5 %collective-permute-start.15 = (f32[512]{0:T(512)S(1)}, f32[512]{0:T(512)S(1)}, u32[]{:S(2)}, u32[]{:S(2)}) collective-permute-start(f32[512]{0:T(512)S(1)} %add.108), channel_id=1, source_target_pairs={{0,4},{1,5},{2,6},{3,7},{4,0},{5,1},{6,2},{7,3},{8,12},{9,13},{10,... | collective-permute-start | bytes 6152 | tf_op jit(solution)/shard_map/ppermute | solution.py:27
  56.8 3.9 %collective-permute-start.14 = (f32[512]{0:T(512)S(1)}, f32[512]{0:T(512)S(1)}, u32[]{:S(2)}, u32[]{:S(2)}) collective-permute-start(f32[512]{0:T(512)S(1)} %add.108), channel_id=1, source_target_pairs={{0,2},{1,3},{2,0},{3,1},{4,6},{5,7},{6,4},{7,5},{8,10},{9,11},{10,... | collective-permute-start | bytes 6152 | tf_op jit(solution)/shard_map/ppermute | solution.py:27
  62.8 4.6 %collective-permute-start.19 = (f32[2048]{0:T(1024)S(1)}, f32[2048]{0:T(1024)S(1)}, u32[]{:S(2)}, u32[]{:S(2)}) collective-permute-start(f32[2048]{0:T(1024)S(1)} %bitcast.43), channel_id=1, source_target_pairs={{0,24},{8,16},{16,8},{24,0},{1,25},{9,17},{17,9},{25,1},{2,26},{10... | collective-permute-start | bytes 24584 | tf_op jit(solution)/shard_map/ppermute | solution.py:27
  65.2 3.7 %collective-permute-start.18 = (f32[2048]{0:T(1024)S(1)}, f32[2048]{0:T(1024)S(1)}, u32[]{:S(2)}, u32[]{:S(2)}) collective-permute-start(f32[2048]{0:T(1024)S(1)} %bitcast.44), channel_id=1, source_target_pairs={{0,16},{8,24},{16,0},{24,8},{1,17},{9,25},{17,1},{25,9},{2,18},{10... | collective-permute-start | bytes 24584 | tf_op jit(solution)/shard_map/ppermute | solution.py:27
  65.7 3.7 %collective-permute-start.17 = (f32[2048]{0:T(1024)S(1)}, f32[2048]{0:T(1024)S(1)}, u32[]{:S(2)}, u32[]{:S(2)}) collective-permute-start(f32[2048]{0:T(1024)S(1)} %bitcast.45), channel_id=1, source_target_pairs={{0,8},{8,0},{16,24},{24,16},{1,9},{9,1},{17,25},{25,17},{2,10},{10... | collective-permute-start | bytes 24584 | tf_op jit(solution)/shard_map/ppermute | solution.py:27
  73.0 1.2 %collective-permute-start.20 = (f32[512]{0:T(512)S(1)}, f32[512]{0:T(512)S(1)}, u32[]{:S(2)}, u32[]{:S(2)}) collective-permute-start(f32[512]{0:T(512)S(1)} %bitcast.52), channel_id=1, source_target_pairs={{0,1},{1,0},{2,3},{3,2},{4,5},{5,4},{6,7},{7,6},{8,9},{9,8},{10,11... | collective-permute-start | bytes 6152 | tf_op jit(solution)/shard_map/ppermute | solution.py:27
  74.2 5.4 %collective-permute-start.23 = (f32[512]{0:T(512)S(1)}, f32[512]{0:T(512)S(1)}, u32[]{:S(2)}, u32[]{:S(2)}) collective-permute-start(f32[512]{0:T(512)S(1)} %add.115), channel_id=1, source_target_pairs={{0,6},{1,7},{2,4},{3,5},{4,2},{5,3},{6,0},{7,1},{8,14},{9,15},{10,... | collective-permute-start | bytes 6152 | tf_op jit(solution)/shard_map/ppermute | solution.py:27
  76.8 4.5 %collective-permute-start.22 = (f32[512]{0:T(512)S(1)}, f32[512]{0:T(512)S(1)}, u32[]{:S(2)}, u32[]{:S(2)}) collective-permute-start(f32[512]{0:T(512)S(1)} %add.115), channel_id=1, source_target_pairs={{0,4},{1,5},{2,6},{3,7},{4,0},{5,1},{6,2},{7,3},{8,12},{9,13},{10,... | collective-permute-start | bytes 6152 | tf_op jit(solution)/shard_map/ppermute | solution.py:27
  77.7 3.6 %collective-permute-start.21 = (f32[512]{0:T(512)S(1)}, f32[512]{0:T(512)S(1)}, u32[]{:S(2)}, u32[]{:S(2)}) collective-permute-start(f32[512]{0:T(512)S(1)} %add.115), channel_id=1, source_target_pairs={{0,2},{1,3},{2,0},{3,1},{4,6},{5,7},{6,4},{7,5},{8,10},{9,11},{10,... | collective-permute-start | bytes 6152 | tf_op jit(solution)/shard_map/ppermute | solution.py:27

commit v2 on v1

v2 whole, which is shorter than its diff:
```python
import functools

import jax
import jax.numpy as jnp
from jax import lax
from jax.experimental import pallas as pl
from jax.experimental.pallas import tpu as pltpu
from jax.sharding import PartitionSpec as P

ITERS = 3
MOST_PARTNERS = 8
BLOCK_BYTES = 20 * 2**20
VMEM = pltpu.VMEM
IN_VMEM = pl.BlockSpec(memory_space=pltpu.VMEM)
F32 = jnp.float32
LANES = 128


def unit_rows(matrix):
    values = matrix.astype(F32)
    scale = lax.rsqrt(1e-06 + jnp.sum(values * values, axis=1, keepdims=True))
    return (values * scale).astype(jnp.bfloat16)


def partners(size, stride, count, step):
    pairs = []
    for index in range(size):
        place = index // stride % count
        other = place ^ step if count & (count - 1) == 0 else (place + step) % count
        pairs.append((index, index + (other - place) * stride))
    return pairs


def from_others(value, axis, stride, count):
    size = lax.axis_size(axis)
    return [lax.ppermute(value, axis, partners(size, stride, count, step)) for step in range(1, count)]


def swap_cores(value):
    return lax.ppermute(value, "proto", partners(lax.axis_size("proto"), 1, 2, 1))


def group_sum(value, axis, stride, count):
    total = value
    for other in from_others(value, axis, stride, count):
        total = total + other
    return total


def proto_sums(partial_value):
    size = lax.axis_size("batch")
    if size > MOST_PARTNERS:
        return lax.psum(partial_value, "batch")
    return group_sum(partial_value, "batch", 1, size)


def image_sums(partial_value):
    size = lax.axis_size("proto")
    if size > 2 * MOST_PARTNERS or size % 2:
        return lax.psum(partial_value, "proto")
    pair = group_sum(partial_value, "proto", 1, 2)
    return group_sum(pair, "proto", 2, size // 2)


def split_plan(features, prototypes):
    unit_feat = unit_rows(features)
    gathered = lax.all_gather(unit_rows(prototypes), "batch", axis=0, tiled=True)
    scores = jnp.einsum("bd,kd->bk", unit_feat, gathered, preferred_element_type=F32)
    weights = jnp.exp(20.0 * scores)
    total_protos = float(weights.shape[1] * lax.axis_size("proto"))
    row_factor = jnp.ones((weights.shape[0],), F32)
    col_factor = jnp.ones((weights.shape[1],), F32)
    for step in range(ITERS):
        column_part = jnp.dot(row_factor, weights, precision=lax.Precision.HIGHEST)
        col_factor = 1.0 / proto_sums(column_part)
        row_part = jnp.dot(weights, col_factor, precision=lax.Precision.HIGHEST)
        row_factor = 1.0 / image_sums(row_part)
    scaled = weights * row_factor[:, None] * (total_protos * col_factor)[None, :]
    return scaled.astype(jnp.bfloat16)


def call(kernel, outs, args, limit, scratch=(), flops=0, transcendentals=0):
    pinned = [pltpu.with_memory_space_constraint(arg, VMEM) for arg in args]
    moved = sum(arg.size * arg.dtype.itemsize for arg in args)
    return pl.pallas_call(
        kernel,
        out_shape=[VMEM(shape, dtype) for shape, dtype in outs],
        in_specs=[IN_VMEM] * len(pinned),
        out_specs=[IN_VMEM] * len(outs),
        scratch_shapes=list(scratch),
        compiler_params=pltpu.CompilerParams(vmem_limit_bytes=limit * 2**20),
        cost_estimate=pl.CostEstimate(flops=flops, bytes_accessed=moved, transcendentals=transcendentals),
    )(*pinned)


def scores_of(protos, images):
    return lax.dot_general(protos, images, (((1,), (1,)), ((), ())), preferred_element_type=F32)


def tiles(width):
    return [slice(start, start + LANES) for start in range(0, width, LANES)]


def image_parts(weights_ref, rows, col_factor, store, add):
    count = rows.stop - rows.start
    factor = jnp.broadcast_to(col_factor, (count, LANES))
    for tile in tiles(weights_ref.shape[1]):
        product = weights_ref[rows, tile] * factor
        part = jnp.sum(jnp.sum(product.reshape(count // 8, 8, LANES), axis=0), axis=0, keepdims=True)
        store[:, tile] = store[:, tile] + part if add else part


def first_kernel(others, *refs):
    own, fetched, swapped = refs[0], refs[1 : 1 + others], refs[1 + others : 1 + 2 * others]
    protos, unit_feat, unit_proto, weights, part = refs[1 + 2 * others :]
    block = own.shape[0]
    half = block // 2
    core = lax.axis_index("proto") % 2
    unit_proto[...] = unit_rows(protos[...])
    unit_feat[:block, :] = unit_rows(own[...])
    for index in range(others):
        base = (index + 1) * block
        mine = pl.multiple_of(base + core * half, half)
        theirs = pl.multiple_of(base + (1 - core) * half, half)
        unit_feat[pl.ds(mine, half), :] = unit_rows(fetched[index][...])
        unit_feat[pl.ds(theirs, half), :] = unit_rows(swapped[index][...])
    rows = slice(0, protos.shape[0])
    total = jnp.zeros((rows.stop, LANES), F32)
    step = 2 * LANES
    for start in range(0, weights.shape[1], step):
        values = jnp.exp(20.0 * scores_of(unit_proto[...], unit_feat[start : start + step, :]))
        weights[:, start : start + step] = values
        for tile in tiles(step):
            total = total + values[:, tile]
    image_parts(weights, rows, 1.0 / jnp.sum(total, axis=1, keepdims=True), part, False)


def more_kernel(others, *refs):
    protos, unit_feat, unit_proto, weights = refs[:others], *refs[others:]
    block = protos[0].shape[0]
    for index in range(others):
        unit_proto[index * block : (index + 1) * block, :] = unit_rows(protos[index][...])
    step = 4 * LANES

    def body(index, carry):
        columns = pl.ds(pl.multiple_of(index * step, step), step)
        weights[:, columns] = jnp.exp(20.0 * scores_of(unit_proto[...], unit_feat[columns, :]))
        return carry

    lax.fori_loop(0, weights.shape[1] // step, body, 0)


def summed(parts, steps, block):
    total = parts[0][...]
    for part, step in zip(parts[1:], steps):
        value = part[...]
        if step:
            order = [index ^ step for index in range(value.shape[1] // block)]
            value = jnp.concatenate([value[:, i * block : (i + 1) * block] for i in order], axis=1)
        total = total + value
    return total


def pass_kernel(steps, block, *refs):
    count = len(steps) + 1
    parts, weights, (part, col_factor) = refs[:count], refs[count:-2], refs[-2:]
    row_factor = 1.0 / summed(parts, steps, block)
    base = 0
    for matrix in weights:
        height = matrix.shape[0]
        for start in range(0, height, block):
            rows = slice(start, start + block)
            total = jnp.zeros((block, LANES), F32)
            for tile in tiles(matrix.shape[1]):
                total = total + matrix[rows, tile] * row_factor[:, tile]
            factor = 1.0 / jnp.sum(total, axis=1, keepdims=True)
            col_factor[base + start : base + start + block, :] = jnp.broadcast_to(factor, (block, LANES))
            image_parts(matrix, rows, factor, part, base + start > 0)
        base += height


def ready_kernel(scale, unit_feat, own_proto, more_proto, col_factor, ready):
    block = ready.shape[0]
    images = unit_feat[:block, :]
    for start in range(0, ready.shape[1], block):
        protos = own_proto[...] if start == 0 else more_proto[start - block : start, :]
        values = jnp.exp(20.0 * scores_of(images, protos))
        for tile in tiles(block):
            at = slice(start + tile.start, start + tile.stop)
            factor = scale * jnp.transpose(col_factor[at, :])[:1, :]
            ready[:, at] = values[:, tile] * factor


def last_kernel(steps, block, *refs):
    count = len(steps) + 1
    parts, ready, out, staged, sems = refs[:count], *refs[count:]
    total = summed(parts, steps, block)
    factors = []
    for tile in tiles(block):
        factors.append(jnp.transpose(jnp.broadcast_to(1.0 / total[:, tile], (LANES, LANES))))
    factor = jnp.concatenate(factors, axis=0)
    place = lax.axis_index("batch")
    copies = []
    for index in range(ready.shape[1] // block):
        for tile in tiles(block):
            at = slice(tile.start, tile.stop)
            values = ready[:, index * block + tile.start : index * block + tile.stop]
            staged[index, :, at] = (values * factor).astype(staged.dtype)
        column = pl.multiple_of(jnp.bitwise_xor(place, index) * block, block)
        copies.append(pltpu.make_async_copy(staged.at[index], out.at[:, pl.ds(column, block)], sems.at[index]))
        copies[-1].start()
    for copy in copies:
        copy.wait()


def whole_plan(features, prototypes):
    bf16 = jnp.bfloat16
    blocks = lax.axis_size("batch")
    others = blocks - 1
    block, depth = features.shape
    height = prototypes.shape[0]
    images = blocks * block
    z_count = lax.axis_size("proto") // 2
    total_protos = float(height * blocks * lax.axis_size("proto"))

    core = lax.axis_index("proto") % 2
    mine = lax.dynamic_slice_in_dim(features, core * (block // 2), block // 2, 0)
    fetched = from_others(mine, "batch", 1, blocks)
    swapped = [swap_cores(value) for value in fetched]
    received = from_others(prototypes, "batch", 1, blocks)

    def around(value):
        pair = value + swap_cores(value)
        return [pair] + from_others(pair, "proto", 2, z_count)

    unit_feat, own_proto, own_weights, part = call(
        functools.partial(first_kernel, others),
        [((images, depth), bf16), ((height, depth), bf16), ((height, images), F32), ((1, images), F32)],
        [features, *fetched, *swapped, prototypes],
        16,
        flops=2 * height * images * depth,
        transcendentals=height * images,
    )
    chips = sum(around(part))
    chips, *received = lax.optimization_barrier((chips, *received))
    parts = [chips] + from_others(chips, "batch", 1, blocks)
    steps = list(range(1, blocks))
    more_proto, more_weights = call(
        functools.partial(more_kernel, others),
        [((others * height, depth), bf16), ((others * height, images), F32)],
        [*received, unit_feat],
        16,
        flops=2 * others * height * images * depth,
        transcendentals=others * height * images,
    )
    for step in range(1, ITERS):
        part, col_factor = call(
            functools.partial(pass_kernel, steps, block),
            [((1, images), F32), ((blocks * height, LANES), F32)],
            [*parts, own_weights, more_weights],
            8,
            flops=4 * blocks * height * images,
        )
        parts = around(part)
        steps = [0] * (z_count - 1)
    (ready,) = call(
        functools.partial(ready_kernel, total_protos),
        [((block, blocks * height), F32)],
        [unit_feat, own_proto, more_proto, col_factor],
        16,
        flops=2 * block * blocks * height * depth,
        transcendentals=block * blocks * height,
    )
    pinned = [pltpu.with_memory_space_constraint(arg, VMEM) for arg in [*parts, ready]]
    return pl.pallas_call(
        functools.partial(last_kernel, steps, block),
        out_shape=jax.ShapeDtypeStruct((block, blocks * height), bf16),
        in_specs=[IN_VMEM] * len(pinned),
        out_specs=pl.BlockSpec(memory_space=pl.ANY),
        scratch_shapes=[VMEM((blocks, block, height), bf16), pltpu.SemaphoreType.DMA((blocks,))],
        compiler_params=pltpu.CompilerParams(vmem_limit_bytes=8 * 2**20),
    )(*pinned)


def local(features, prototypes):
    blocks = lax.axis_size("batch")
    block, height = features.shape[0], prototypes.shape[0]
    fits = 4 * blocks * blocks * block * height <= BLOCK_BYTES
    even = block == height and block % (2 * LANES) == 0 and blocks & (blocks - 1) == 0
    if fits and even and lax.axis_size("proto") % 2 == 0 and lax.axis_size("proto") <= 2 * MOST_PARTNERS:
        return whole_plan(features, prototypes)
    return split_plan(features, prototypes)


def solution(mesh):
    in_specs = (P("batch", None), P(("proto", "batch"), None))
    out_specs = P("batch", "proto")
    return jax.shard_map(local, mesh=mesh, in_specs=in_specs, out_specs=out_specs, check_vma=False)
```

time: 83.3 us -> 69.2 us (0.83)
  matrix products: 19 us -> 0 us
  Pallas kernels: 0 us -> 13.2 us
  other arithmetic: 5.08 us -> 0.05 us
  waiting for transfers between devices: 30.4 us -> 27.3 us
  local copies, waits for them, and re-layouts: 0.14 us -> 2.81 us
  starting transfers between devices: 28.2 us -> 25.6 us
    dot_general x7 -> x0, matrix products: 19 us -> none  [the longest x3 11.1 us: local(): row_part = jnp.dot(weights, col_factor, precision=lax.Precision.HIGHEST)]
    pallas_call x0 -> x6, Pallas kernels: none -> 13.2 us  [the longest x5 11.5 us: call(): pl.pallas_call(kernel, out_shape=[VMEM(shape, dtype) for shape, dtype in...]
    ppermute x24 -> x18, waiting for transfers between devices: 30.4 us -> 23 us  [from_others(): lax.ppermute(value, axis, partners(size, stride, count, step))]
    ppermute x0 -> x6, waiting for transfers between devices: none -> 4.32 us  [swap_cores(): lax.ppermute(value, 'proto', partners(lax.axis_size('proto'), 1, 2, 1))]
    ppermute x24 -> x18, starting transfers between devices: 28.2 us -> 24.9 us  [from_others(): lax.ppermute(value, axis, partners(size, stride, count, step))]
    reduce_sum x2 -> x0, other arithmetic: 2.19 us -> none  [unit_rows(): scale = lax.rsqrt(1e-06 + jnp.sum(values * values, axis=1, keepdims=True))]
    unnamed x0 -> x4, local copies, waits for them, and re-layouts: none -> 1.9 us
    convert_element_type x1 -> x0, other arithmetic: 1.73 us -> none  [local(): return scaled.astype(jnp.bfloat16)]
  transfers between devices with their start and end apart: 24 -> 24, of which waited for: 20 -> 17; matrix products, arithmetic and copies ran while one was open for 1% -> 0% of each run, Pallas kernels for 0% -> 5%
where the time goes in v2:
time: 69.2 us; the launch traced here: 69 us
  waiting for transfers between devices  27.3 us (39%)
  starting transfers between devices  25.6 us (37%)
  Pallas kernels  13.2 us (19%)
  local copies, waits for them, and re-layouts  2.81 us (4%)
    ppermute x18, starting transfers between devices, from_others(): lax.ppermute(value, axis, partners(size, stride, count, step))  24.9 us
    ppermute x18, waiting for transfers between devices, from_others(): lax.ppermute(value, axis, partners(size, stride, count, step))  23 us
    pallas_call x5, Pallas kernels, call(): pl.pallas_call(kernel, out_shape=[VMEM(shape, dtype) for shape, dtype in...  11.5 us
    ppermute x6, waiting for transfers between devices, swap_cores(): lax.ppermute(value, 'proto', partners(lax.axis_size('proto'), 1, 2, 1))  4.32 us
    unnamed x4, local copies, waits for them, and re-layouts  1.9 us
    pallas_call x1, Pallas kernels, whole_plan(): pl.pallas_call(functools.partial(last_kernel, steps, block), out_shape=ja...  1.68 us
  transfers between devices with their start and end apart: 24, of which 17 were waited for; matrix products, arithmetic and copies ran while one was open for 0% of the time, Pallas kernels for 5%

profile of v2, /device:TPU:0, one launch (start us, length us, event | category | flops | bytes accessed | tf_op | source)
XLA Modules:
  0.0 69.0 jit_solution(7750257468784346311)
XLA Ops:
  0.0 0.9 %constant_dynamic-slice_fusion = bf16[256,256]{1,0:T(8,128)(2,1)S(1)} fusion(bf16[512,256]{1,0:T(8,128)(2,1)} %refs_0_.1, s32[]{:T(128)S(6)} %select_n.11), kind=kLoop, calls=%fused_computation.1 | loop fusion | bytes 262148 | tf_op jit(solution)/shard_map/dynamic_slice | solution.py:227
  0.9 4.0 %collective-permute-start.2 = (bf16[256,256]{1,0:T(8,128)(2,1)S(1)}, bf16[256,256]{1,0:T(8,128)(2,1)S(1)}, u32[]{:S(2)}, u32[]{:S(2)}) collective-permute-start(bf16[256,256]{1,0:T(8,128)(2,1)S(1)} %constant_dynamic-slice_fusion), channel_id=1, source_target_pairs={{0,24},{8,16},{16,8},{24,0},{1,25},{9,17},{17,9},{25,1},{2,26},{10... | collective-permute-start | bytes 393224 | tf_op jit(solution)/shard_map/ppermute | solution.py:36
  5.5 3.3 %collective-permute-done.2.refs_3_ = bf16[256,256]{1,0:T(8,128)(2,1)S(1)} collective-permute-done((bf16[256,256]{1,0:T(8,128)(2,1)S(1)}, bf16[256,256]{1,0:T(8,128)(2,1)S(1)}, u32[]{:S(2)}, u32[]{:S(2)}) %collective-permute-start.2) | collective-permute-done | bytes 131104 | tf_op jit(solution)/shard_map/ppermute | solution.py:36
  8.8 2.4 %collective-permute-done.1.refs_2_ = bf16[256,256]{1,0:T(8,128)(2,1)S(1)} collective-permute-done((bf16[256,256]{1,0:T(8,128)(2,1)S(1)}, bf16[256,256]{1,0:T(8,128)(2,1)S(1)}, u32[]{:S(2)}, u32[]{:S(2)}) %collective-permute-start.1) | collective-permute-done | bytes 131104 | tf_op jit(solution)/shard_map/ppermute | solution.py:36
  11.7 0.8 %collective-permute-done.4.refs_5_ = bf16[256,256]{1,0:T(8,128)(2,1)S(1)} collective-permute-done((bf16[256,256]{1,0:T(8,128)(2,1)S(1)}, bf16[256,256]{1,0:T(8,128)(2,1)S(1)}, u32[]{:S(2)}, u32[]{:S(2)}) %collective-permute-start.4) | collective-permute-done | bytes 131104 | tf_op jit(solution)/shard_map/ppermute | solution.py:40
  12.8 0.9 %copy-done = bf16[512,256]{1,0:T(8,128)(2,1)S(1)} copy-done((bf16[512,256]{1,0:T(8,128)(2,1)S(1)}, bf16[512,256]{1,0:T(8,128)(2,1)}, u32[]{:S(2)}) %copy-start) | copy-done | bytes 262168
  13.7 0.9 %copy-done.1 = bf16[512,256]{1,0:T(8,128)(2,1)S(1)} copy-done((bf16[512,256]{1,0:T(8,128)(2,1)S(1)}, bf16[512,256]{1,0:T(8,128)(2,1)}, u32[]{:S(2)}) %copy-start.1) | copy-done | bytes 262168
  14.7 1.6 %shard_map.28 = (bf16[2048,256]{1,0:T(8,128)(2,1)S(1)}, bf16[512,256]{1,0:T(8,128)(2,1)S(1)}, f32[512,2048]{1,0:T(8,128)S(1)}, f32[1,2048]{1,0:T(1,128)S(1)}) custom-call(bf16[512,256]{1,0:T(8,128)(2,1)S(1)} %copy-done, bf16[256,256]{1,0:T(8,128)(2,1)S(1)} %collective-permute-done.refs_1_, bf16[256,256]{1,0:T(8,128)(2,1)S(1)} %collective-permute-done.1.refs_2_, ...), custom_call_target="tpu_custom_call" | custom-call | flops 536870912 | bytes 1310720 | tf_op jit(solution)/shard_map/pallas_call | solution.py:85
  16.6 0.9 %collective-permute-done.6 = f32[1,2048]{1,0:T(1,128)S(1)} collective-permute-done((f32[1,2048]{1,0:T(1,128)S(1)}, f32[1,2048]{1,0:T(1,128)S(1)}, u32[]{:S(2)}, u32[]{:S(2)}) %collective-permute-start.6) | collective-permute-done | bytes 8224 | tf_op jit(solution)/shard_map/ppermute | solution.py:40
  17.5 3.8 %collective-permute-start.9 = (f32[1,2048]{1,0:T(1,128)S(1)}, f32[1,2048]{1,0:T(1,128)S(1)}, u32[]{:S(2)}, u32[]{:S(2)}) collective-permute-start(f32[1,2048]{1,0:T(1,128)S(1)} %add.27), channel_id=1, source_target_pairs={{0,6},{1,7},{2,4},{3,5},{4,2},{5,3},{6,0},{7,1},{8,14},{9,15},{10,... | collective-permute-start | bytes 24584 | tf_op jit(solution)/shard_map/ppermute | solution.py:36
  21.3 0.7 collective-permute-start.7
  22.0 1.6 %collective-permute-start.10 = (bf16[512,256]{1,0:T(8,128)(2,1)S(1)}, bf16[512,256]{1,0:T(8,128)(2,1)S(1)}, u32[]{:S(2)}, u32[]{:S(2)}) collective-permute-start(bf16[512,256]{1,0:T(8,128)(2,1)S(1)} %copy-done.1), channel_id=1, source_target_pairs={{0,8},{8,0},{16,24},{24,16},{1,9},{9,1},{17,25},{25,17},{2,10},{10... | collective-permute-start | bytes 786440 | tf_op jit(solution)/shard_map/ppermute | solution.py:36
  23.6 1.5 %collective-permute-start.12 = (bf16[512,256]{1,0:T(8,128)(2,1)S(1)}, bf16[512,256]{1,0:T(8,128)(2,1)S(1)}, u32[]{:S(2)}, u32[]{:S(2)}) collective-permute-start(bf16[512,256]{1,0:T(8,128)(2,1)S(1)} %copy-done.1), channel_id=1, source_target_pairs={{0,24},{8,16},{16,8},{24,0},{1,25},{9,17},{17,9},{25,1},{2,26},{10... | collective-permute-start | bytes 786440 | tf_op jit(solution)/shard_map/ppermute | solution.py:36
  25.9 5.3 %collective-permute-done.10.refs_0_ = bf16[512,256]{1,0:T(8,128)(2,1)S(1)} collective-permute-done((bf16[512,256]{1,0:T(8,128)(2,1)S(1)}, bf16[512,256]{1,0:T(8,128)(2,1)S(1)}, u32[]{:S(2)}, u32[]{:S(2)}) %collective-permute-start.10) | collective-permute-done | bytes 262176 | tf_op jit(solution)/shard_map/ppermute | solution.py:36
  31.2 5.4 %collective-permute-done.12.refs_2_ = bf16[512,256]{1,0:T(8,128)(2,1)S(1)} collective-permute-done((bf16[512,256]{1,0:T(8,128)(2,1)S(1)}, bf16[512,256]{1,0:T(8,128)(2,1)S(1)}, u32[]{:S(2)}, u32[]{:S(2)}) %collective-permute-start.12) | collective-permute-done | bytes 262176 | tf_op jit(solution)/shard_map/ppermute | solution.py:36
  36.6 1.4 %collective-permute-done.11.refs_1_ = bf16[512,256]{1,0:T(8,128)(2,1)S(1)} collective-permute-done((bf16[512,256]{1,0:T(8,128)(2,1)S(1)}, bf16[512,256]{1,0:T(8,128)(2,1)S(1)}, u32[]{:S(2)}, u32[]{:S(2)}) %collective-permute-start.11) | collective-permute-done | bytes 262176 | tf_op jit(solution)/shard_map/ppermute | solution.py:36
  38.0 1.4 %collective-permute-start.15 = (f32[1,2048]{1,0:T(1,128)S(1)}, f32[1,2048]{1,0:T(1,128)S(1)}, u32[]{:S(2)}, u32[]{:S(2)}) collective-permute-start(f32[1,2048]{1,0:T(1,128)S(1)} %add_add_fusion.refs_0_), channel_id=1, source_target_pairs={{0,24},{8,16},{16,8},{24,0},{1,25},{9,17},{17,9},{25,1},{2,26},{10... | collective-permute-start | bytes 24584 | tf_op jit(solution)/shard_map/ppermute | solution.py:36
  39.4 0.8 %collective-permute-start.14 = (f32[1,2048]{1,0:T(1,128)S(1)}, f32[1,2048]{1,0:T(1,128)S(1)}, u32[]{:S(2)}, u32[]{:S(2)}) collective-permute-start(f32[1,2048]{1,0:T(1,128)S(1)} %add_add_fusion.refs_0_), channel_id=1, source_target_pairs={{0,16},{8,24},{16,0},{24,8},{1,17},{9,25},{17,1},{25,9},{2,18},{10... | collective-permute-start | bytes 24584 | tf_op jit(solution)/shard_map/ppermute | solution.py:36
  40.2 1.2 %collective-permute-start.13 = (f32[1,2048]{1,0:T(1,128)S(1)}, f32[1,2048]{1,0:T(1,128)S(1)}, u32[]{:S(2)}, u32[]{:S(2)}) collective-permute-start(f32[1,2048]{1,0:T(1,128)S(1)} %add_add_fusion.refs_0_), channel_id=1, source_target_pairs={{0,8},{8,0},{16,24},{24,16},{1,9},{9,1},{17,25},{25,17},{2,10},{10... | collective-permute-start | bytes 24584 | tf_op jit(solution)/shard_map/ppermute | solution.py:36
  41.5 2.7 %shard_map.29 = (bf16[1536,256]{1,0:T(8,128)(2,1)S(1)}, f32[1536,2048]{1,0:T(8,128)S(1)}) custom-call(bf16[512,256]{1,0:T(8,128)(2,1)S(1)} %collective-permute-done.10.refs_0_, bf16[512,256]{1,0:T(8,128)(2,1)S(1)} %collective-permute-done.11.refs_1_, bf16[512,256]{1,0:T(8,128)(2,1)S(1)} %collective-permute-done.12.refs_2_, ...), custom_call_target="tpu_custom_call" | custom-call | flops 1610612736 | bytes 1835008 | tf_op jit(solution)/shard_map/pallas_call | solution.py:85
  44.2 3.7 %shard_map.30 = (f32[1,2048]{1,0:T(1,128)S(1)}, f32[2048,128]{1,0:T(8,128)}) custom-call(f32[1,2048]{1,0:T(1,128)S(1)} %add_add_fusion.refs_0_, f32[1,2048]{1,0:T(1,128)S(1)} %collective-permute-done.13.refs_1_, f32[1,2048]{1,0:T(1,128)S(1)} %collective-permute-done.14.refs_2_, f32[1,2048]{1,0:T(1,128)S(1)} %collective-permute-done.15.refs_3_, ...), custom_call_target="tpu_custom_call" | custom-call | flops 16777216 | bytes 16809984 | tf_op jit(solution)/shard_map/pallas_call | solution.py:85
  47.9 1.2 %collective-permute-done.16 = f32[1,2048]{1,0:T(1,128)S(1)} collective-permute-done((f32[1,2048]{1,0:T(1,128)S(1)}, f32[1,2048]{1,0:T(1,128)S(1)}, u32[]{:S(2)}, u32[]{:S(2)}) %collective-permute-start.16) | collective-permute-done | bytes 8224 | tf_op jit(solution)/shard_map/ppermute | solution.py:40
  49.1 3.5 %collective-permute-start.19 = (f32[1,2048]{1,0:T(1,128)S(1)}, f32[1,2048]{1,0:T(1,128)S(1)}, u32[]{:S(2)}, u32[]{:S(2)}) collective-permute-start(f32[1,2048]{1,0:T(1,128)S(1)} %add.31.refs_0_), channel_id=1, source_target_pairs={{0,6},{1,7},{2,4},{3,5},{4,2},{5,3},{6,0},{7,1},{8,14},{9,15},{10,... | collective-permute-start | bytes 24584 | tf_op jit(solution)/shard_map/ppermute | solution.py:36
  52.6 0.9 %collective-permute-start.17 = (f32[1,2048]{1,0:T(1,128)S(1)}, f32[1,2048]{1,0:T(1,128)S(1)}, u32[]{:S(2)}, u32[]{:S(2)}) collective-permute-start(f32[1,2048]{1,0:T(1,128)S(1)} %add.31.refs_0_), channel_id=1, source_target_pairs={{0,2},{1,3},{2,0},{3,1},{4,6},{5,7},{6,4},{7,5},{8,10},{9,11},{10,... | collective-permute-start | bytes 24584 | tf_op jit(solution)/shard_map/ppermute | solution.py:36
  53.5 1.1 %collective-permute-done.19.refs_3_ = f32[1,2048]{1,0:T(1,128)S(1)} collective-permute-done((f32[1,2048]{1,0:T(1,128)S(1)}, f32[1,2048]{1,0:T(1,128)S(1)}, u32[]{:S(2)}, u32[]{:S(2)}) %collective-permute-start.19) | collective-permute-done | bytes 8224 | tf_op jit(solution)/shard_map/ppermute | solution.py:36
  54.6 2.6 %collective-permute-done.18.refs_2_ = f32[1,2048]{1,0:T(1,128)S(1)} collective-permute-done((f32[1,2048]{1,0:T(1,128)S(1)}, f32[1,2048]{1,0:T(1,128)S(1)}, u32[]{:S(2)}, u32[]{:S(2)}) %collective-permute-start.18) | collective-permute-done | bytes 8224 | tf_op jit(solution)/shard_map/ppermute | solution.py:36
  57.2 2.7 %shard_map.31 = (f32[1,2048]{1,0:T(1,128)S(1)}, f32[2048,128]{1,0:T(8,128)S(1)}) custom-call(f32[1,2048]{1,0:T(1,128)S(1)} %add.31.refs_0_, f32[1,2048]{1,0:T(1,128)S(1)} %collective-permute-done.17.refs_1_, f32[1,2048]{1,0:T(1,128)S(1)} %collective-permute-done.18.refs_2_, f32[1,2048]{1,0:T(1,128)S(1)} %collective-permute-done.19.refs_3_, ...), custom_call_target="tpu_custom_call" | custom-call | flops 16777216 | bytes 16809984 | tf_op jit(solution)/shard_map/pallas_call | solution.py:85
  60.0 1.2 %collective-permute-done.20 = f32[1,2048]{1,0:T(1,128)S(1)} collective-permute-done((f32[1,2048]{1,0:T(1,128)S(1)}, f32[1,2048]{1,0:T(1,128)S(1)}, u32[]{:S(2)}, u32[]{:S(2)}) %collective-permute-start.20) | collective-permute-done | bytes 8224 | tf_op jit(solution)/shard_map/ppermute | solution.py:40
  61.2 1.5 %collective-permute-start.23 = (f32[1,2048]{1,0:T(1,128)S(1)}, f32[1,2048]{1,0:T(1,128)S(1)}, u32[]{:S(2)}, u32[]{:S(2)}) collective-permute-start(f32[1,2048]{1,0:T(1,128)S(1)} %add.32.refs_0_), channel_id=1, source_target_pairs={{0,6},{1,7},{2,4},{3,5},{4,2},{5,3},{6,0},{7,1},{8,14},{9,15},{10,... | collective-permute-start | bytes 24584 | tf_op jit(solution)/shard_map/ppermute | solution.py:36
  63.4 2.3 %collective-permute-start.21 = (f32[1,2048]{1,0:T(1,128)S(1)}, f32[1,2048]{1,0:T(1,128)S(1)}, u32[]{:S(2)}, u32[]{:S(2)}) collective-permute-start(f32[1,2048]{1,0:T(1,128)S(1)} %add.32.refs_0_), channel_id=1, source_target_pairs={{0,2},{1,3},{2,0},{3,1},{4,6},{5,7},{6,4},{7,5},{8,10},{9,11},{10,... | collective-permute-start | bytes 24584 | tf_op jit(solution)/shard_map/ppermute | solution.py:36
  65.6 0.8 %shard_map.32.refs_4_ = f32[512,2048]{1,0:T(8,128)S(1)} custom-call(bf16[2048,256]{1,0:T(8,128)(2,1)S(1)} %get-tuple-element.24.refs_3_.unit_feat, bf16[512,256]{1,0:T(8,128)(2,1)S(1)} %get-tuple-element.28.own_proto, bf16[1536,256]{1,0:T(8,128)(2,1)S(1)} %get-tuple-element.29.more_proto, f32[2048,128]{1,0:T(8,128)S(1)} %get-tuple-element.30.col_factor), custom_call_target="tpu_custom_call" | custom-call | flops 536870912 | bytes 3145728 | tf_op jit(solution)/shard_map/pallas_call | solution.py:85
  67.3 1.7 %shard_map.33 = bf16[512,2048]{1,0:T(8,128)(2,1)} custom-call(f32[1,2048]{1,0:T(1,128)S(1)} %add.32.refs_0_, f32[1,2048]{1,0:T(1,128)S(1)} %collective-permute-done.21.refs_1_, f32[1,2048]{1,0:T(1,128)S(1)} %collective-permute-done.22.refs_2_, f32[1,2048]{1,0:T(1,128)S(1)} %collective-permute-done.23.refs_3_, f32[512,2048]{1,0:T(8,128)S(1)} %shard_map.32.refs_4_), custom_call_target="tpu_custom_call" | custom-call | tf_op jit(solution)/shard_map/pallas_call | solution.py:275
  (31 shorter events, 4.2 us)
Async XLA Ops:
  0.9 7.9 %collective-permute-start.2 = (bf16[256,256]{1,0:T(8,128)(2,1)S(1)}, bf16[256,256]{1,0:T(8,128)(2,1)S(1)}, u32[]{:S(2)}, u32[]{:S(2)}) collective-permute-start(bf16[256,256]{1,0:T(8,128)(2,1)S(1)} %constant_dynamic-slice_fusion), channel_id=1, source_target_pairs={{0,24},{8,16},{16,8},{24,0},{1,25},{9,17},{17,9},{25,1},{2,26},{10... | collective-permute-start | bytes 393224 | tf_op jit(solution)/shard_map/ppermute | solution.py:36
  4.9 6.3 %collective-permute-start.1 = (bf16[256,256]{1,0:T(8,128)(2,1)S(1)}, bf16[256,256]{1,0:T(8,128)(2,1)S(1)}, u32[]{:S(2)}, u32[]{:S(2)}) collective-permute-start(bf16[256,256]{1,0:T(8,128)(2,1)S(1)} %constant_dynamic-slice_fusion), channel_id=1, source_target_pairs={{0,16},{8,24},{16,0},{24,8},{1,17},{9,25},{17,1},{25,9},{2,18},{10... | collective-permute-start | bytes 393224 | tf_op jit(solution)/shard_map/ppermute | solution.py:36
  5.4 6.0 %collective-permute-start = (bf16[256,256]{1,0:T(8,128)(2,1)S(1)}, bf16[256,256]{1,0:T(8,128)(2,1)S(1)}, u32[]{:S(2)}, u32[]{:S(2)}) collective-permute-start(bf16[256,256]{1,0:T(8,128)(2,1)S(1)} %constant_dynamic-slice_fusion), channel_id=1, source_target_pairs={{0,8},{8,0},{16,24},{24,16},{1,9},{9,1},{17,25},{25,17},{2,10},{10... | collective-permute-start | bytes 393224 | tf_op jit(solution)/shard_map/ppermute | solution.py:36
  8.8 2.9 %collective-permute-start.5 = (bf16[256,256]{1,0:T(8,128)(2,1)S(1)}, bf16[256,256]{1,0:T(8,128)(2,1)S(1)}, u32[]{:S(2)}, u32[]{:S(2)}) collective-permute-start(bf16[256,256]{1,0:T(8,128)(2,1)S(1)} %collective-permute-done.2.refs_3_), channel_id=1, source_target_pairs={{0,1},{1,0},{2,3},{3,2},{4,5},{5,4},{6,7},{7,6},{8,9},{9,8},{10,11... | collective-permute-start | bytes 393224 | tf_op jit(solution)/shard_map/ppermute | solution.py:40
  11.2 1.3 %collective-permute-start.4 = (bf16[256,256]{1,0:T(8,128)(2,1)S(1)}, bf16[256,256]{1,0:T(8,128)(2,1)S(1)}, u32[]{:S(2)}, u32[]{:S(2)}) collective-permute-start(bf16[256,256]{1,0:T(8,128)(2,1)S(1)} %collective-permute-done.1.refs_2_), channel_id=1, source_target_pairs={{0,1},{1,0},{2,3},{3,2},{4,5},{5,4},{6,7},{7,6},{8,9},{9,8},{10,11... | collective-permute-start | bytes 393224 | tf_op jit(solution)/shard_map/ppermute | solution.py:40
  11.4 1.3 %collective-permute-start.3 = (bf16[256,256]{1,0:T(8,128)(2,1)S(1)}, bf16[256,256]{1,0:T(8,128)(2,1)S(1)}, u32[]{:S(2)}, u32[]{:S(2)}) collective-permute-start(bf16[256,256]{1,0:T(8,128)(2,1)S(1)} %collective-permute-done.refs_1_), channel_id=1, source_target_pairs={{0,1},{1,0},{2,3},{3,2},{4,5},{5,4},{6,7},{7,6},{8,9},{9,8},{10,11... | collective-permute-start | bytes 393224 | tf_op jit(solution)/shard_map/ppermute | solution.py:40
  12.8 1.0 %copy-start = (bf16[512,256]{1,0:T(8,128)(2,1)S(1)}, bf16[512,256]{1,0:T(8,128)(2,1)}, u32[]{:S(2)}) copy-start(bf16[512,256]{1,0:T(8,128)(2,1)} %refs_0_.1) | copy-start | bytes 786436
  13.7 0.9 %copy-start.1 = (bf16[512,256]{1,0:T(8,128)(2,1)S(1)}, bf16[512,256]{1,0:T(8,128)(2,1)}, u32[]{:S(2)}) copy-start(bf16[512,256]{1,0:T(8,128)(2,1)} %refs_7_.1) | copy-start | bytes 786436
  16.3 1.2 %collective-permute-start.6 = (f32[1,2048]{1,0:T(1,128)S(1)}, f32[1,2048]{1,0:T(1,128)S(1)}, u32[]{:S(2)}, u32[]{:S(2)}) collective-permute-start(f32[1,2048]{1,0:T(1,128)S(1)} %get-tuple-element.18), channel_id=1, source_target_pairs={{0,1},{1,0},{2,3},{3,2},{4,5},{5,4},{6,7},{7,6},{8,9},{9,8},{10,11... | collective-permute-start | bytes 24584 | tf_op jit(solution)/shard_map/ppermute | solution.py:40
  17.5 7.6 %collective-permute-start.9 = (f32[1,2048]{1,0:T(1,128)S(1)}, f32[1,2048]{1,0:T(1,128)S(1)}, u32[]{:S(2)}, u32[]{:S(2)}) collective-permute-start(f32[1,2048]{1,0:T(1,128)S(1)} %add.27), channel_id=1, source_target_pairs={{0,6},{1,7},{2,4},{3,5},{4,2},{5,3},{6,0},{7,1},{8,14},{9,15},{10,... | collective-permute-start | bytes 24584 | tf_op jit(solution)/shard_map/ppermute | solution.py:36
  21.3 4.5 %collective-permute-start.8 = (f32[1,2048]{1,0:T(1,128)S(1)}, f32[1,2048]{1,0:T(1,128)S(1)}, u32[]{:S(2)}, u32[]{:S(2)}) collective-permute-start(f32[1,2048]{1,0:T(1,128)S(1)} %add.27), channel_id=1, source_target_pairs={{0,4},{1,5},{2,6},{3,7},{4,0},{5,1},{6,2},{7,3},{8,12},{9,13},{10,... | collective-permute-start | bytes 24584 | tf_op jit(solution)/shard_map/ppermute | solution.py:36
  21.3 4.5 %collective-permute-start.7 = (f32[1,2048]{1,0:T(1,128)S(1)}, f32[1,2048]{1,0:T(1,128)S(1)}, u32[]{:S(2)}, u32[]{:S(2)}) collective-permute-start(f32[1,2048]{1,0:T(1,128)S(1)} %add.27), channel_id=1, source_target_pairs={{0,2},{1,3},{2,0},{3,1},{4,6},{5,7},{6,4},{7,5},{8,10},{9,11},{10,... | collective-permute-start | bytes 24584 | tf_op jit(solution)/shard_map/ppermute | solution.py:36
  22.0 9.2 %collective-permute-start.10 = (bf16[512,256]{1,0:T(8,128)(2,1)S(1)}, bf16[512,256]{1,0:T(8,128)(2,1)S(1)}, u32[]{:S(2)}, u32[]{:S(2)}) collective-permute-start(bf16[512,256]{1,0:T(8,128)(2,1)S(1)} %copy-done.1), channel_id=1, source_target_pairs={{0,8},{8,0},{16,24},{24,16},{1,9},{9,1},{17,25},{25,17},{2,10},{10... | collective-permute-start | bytes 786440 | tf_op jit(solution)/shard_map/ppermute | solution.py:36
  23.6 13.0 %collective-permute-start.12 = (bf16[512,256]{1,0:T(8,128)(2,1)S(1)}, bf16[512,256]{1,0:T(8,128)(2,1)S(1)}, u32[]{:S(2)}, u32[]{:S(2)}) collective-permute-start(bf16[512,256]{1,0:T(8,128)(2,1)S(1)} %copy-done.1), channel_id=1, source_target_pairs={{0,24},{8,16},{16,8},{24,0},{1,25},{9,17},{17,9},{25,1},{2,26},{10... | collective-permute-start | bytes 786440 | tf_op jit(solution)/shard_map/ppermute | solution.py:36
  25.1 12.9 %collective-permute-start.11 = (bf16[512,256]{1,0:T(8,128)(2,1)S(1)}, bf16[512,256]{1,0:T(8,128)(2,1)S(1)}, u32[]{:S(2)}, u32[]{:S(2)}) collective-permute-start(bf16[512,256]{1,0:T(8,128)(2,1)S(1)} %copy-done.1), channel_id=1, source_target_pairs={{0,16},{8,24},{16,0},{24,8},{1,17},{9,25},{17,1},{25,9},{2,18},{10... | collective-permute-start | bytes 786440 | tf_op jit(solution)/shard_map/ppermute | solution.py:36
  38.0 6.2 %collective-permute-start.15 = (f32[1,2048]{1,0:T(1,128)S(1)}, f32[1,2048]{1,0:T(1,128)S(1)}, u32[]{:S(2)}, u32[]{:S(2)}) collective-permute-start(f32[1,2048]{1,0:T(1,128)S(1)} %add_add_fusion.refs_0_), channel_id=1, source_target_pairs={{0,24},{8,16},{16,8},{24,0},{1,25},{9,17},{17,9},{25,1},{2,26},{10... | collective-permute-start | bytes 24584 | tf_op jit(solution)/shard_map/ppermute | solution.py:36
  39.4 4.8 %collective-permute-start.14 = (f32[1,2048]{1,0:T(1,128)S(1)}, f32[1,2048]{1,0:T(1,128)S(1)}, u32[]{:S(2)}, u32[]{:S(2)}) collective-permute-start(f32[1,2048]{1,0:T(1,128)S(1)} %add_add_fusion.refs_0_), channel_id=1, source_target_pairs={{0,16},{8,24},{16,0},{24,8},{1,17},{9,25},{17,1},{25,9},{2,18},{10... | collective-permute-start | bytes 24584 | tf_op jit(solution)/shard_map/ppermute | solution.py:36
  40.2 4.0 %collective-permute-start.13 = (f32[1,2048]{1,0:T(1,128)S(1)}, f32[1,2048]{1,0:T(1,128)S(1)}, u32[]{:S(2)}, u32[]{:S(2)}) collective-permute-start(f32[1,2048]{1,0:T(1,128)S(1)} %add_add_fusion.refs_0_), channel_id=1, source_target_pairs={{0,8},{8,0},{16,24},{24,16},{1,9},{9,1},{17,25},{25,17},{2,10},{10... | collective-permute-start | bytes 24584 | tf_op jit(solution)/shard_map/ppermute | solution.py:36
  47.9 1.2 %collective-permute-start.16 = (f32[1,2048]{1,0:T(1,128)S(1)}, f32[1,2048]{1,0:T(1,128)S(1)}, u32[]{:S(2)}, u32[]{:S(2)}) collective-permute-start(f32[1,2048]{1,0:T(1,128)S(1)} %get-tuple-element.26), channel_id=1, source_target_pairs={{0,1},{1,0},{2,3},{3,2},{4,5},{5,4},{6,7},{7,6},{8,9},{9,8},{10,11... | collective-permute-start | bytes 24584 | tf_op jit(solution)/shard_map/ppermute | solution.py:40
  49.1 5.5 %collective-permute-start.19 = (f32[1,2048]{1,0:T(1,128)S(1)}, f32[1,2048]{1,0:T(1,128)S(1)}, u32[]{:S(2)}, u32[]{:S(2)}) collective-permute-start(f32[1,2048]{1,0:T(1,128)S(1)} %add.31.refs_0_), channel_id=1, source_target_pairs={{0,6},{1,7},{2,4},{3,5},{4,2},{5,3},{6,0},{7,1},{8,14},{9,15},{10,... | collective-permute-start | bytes 24584 | tf_op jit(solution)/shard_map/ppermute | solution.py:36
  52.6 4.5 %collective-permute-start.18 = (f32[1,2048]{1,0:T(1,128)S(1)}, f32[1,2048]{1,0:T(1,128)S(1)}, u32[]{:S(2)}, u32[]{:S(2)}) collective-permute-start(f32[1,2048]{1,0:T(1,128)S(1)} %add.31.refs_0_), channel_id=1, source_target_pairs={{0,4},{1,5},{2,6},{3,7},{4,0},{5,1},{6,2},{7,3},{8,12},{9,13},{10,... | collective-permute-start | bytes 24584 | tf_op jit(solution)/shard_map/ppermute | solution.py:36
  52.6 4.5 %collective-permute-start.17 = (f32[1,2048]{1,0:T(1,128)S(1)}, f32[1,2048]{1,0:T(1,128)S(1)}, u32[]{:S(2)}, u32[]{:S(2)}) collective-permute-start(f32[1,2048]{1,0:T(1,128)S(1)} %add.31.refs_0_), channel_id=1, source_target_pairs={{0,2},{1,3},{2,0},{3,1},{4,6},{5,7},{6,4},{7,5},{8,10},{9,11},{10,... | collective-permute-start | bytes 24584 | tf_op jit(solution)/shard_map/ppermute | solution.py:36
  59.9 1.2 %collective-permute-start.20 = (f32[1,2048]{1,0:T(1,128)S(1)}, f32[1,2048]{1,0:T(1,128)S(1)}, u32[]{:S(2)}, u32[]{:S(2)}) collective-permute-start(f32[1,2048]{1,0:T(1,128)S(1)} %get-tuple-element.27), channel_id=1, source_target_pairs={{0,1},{1,0},{2,3},{3,2},{4,5},{5,4},{6,7},{7,6},{8,9},{9,8},{10,11... | collective-permute-start | bytes 24584 | tf_op jit(solution)/shard_map/ppermute | solution.py:40
  61.2 5.6 %collective-permute-start.23 = (f32[1,2048]{1,0:T(1,128)S(1)}, f32[1,2048]{1,0:T(1,128)S(1)}, u32[]{:S(2)}, u32[]{:S(2)}) collective-permute-start(f32[1,2048]{1,0:T(1,128)S(1)} %add.32.refs_0_), channel_id=1, source_target_pairs={{0,6},{1,7},{2,4},{3,5},{4,2},{5,3},{6,0},{7,1},{8,14},{9,15},{10,... | collective-permute-start | bytes 24584 | tf_op jit(solution)/shard_map/ppermute | solution.py:36
  62.7 4.6 %collective-permute-start.22 = (f32[1,2048]{1,0:T(1,128)S(1)}, f32[1,2048]{1,0:T(1,128)S(1)}, u32[]{:S(2)}, u32[]{:S(2)}) collective-permute-start(f32[1,2048]{1,0:T(1,128)S(1)} %add.32.refs_0_), channel_id=1, source_target_pairs={{0,4},{1,5},{2,6},{3,7},{4,0},{5,1},{6,2},{7,3},{8,12},{9,13},{10,... | collective-permute-start | bytes 24584 | tf_op jit(solution)/shard_map/ppermute | solution.py:36
  63.4 4.0 %collective-permute-start.21 = (f32[1,2048]{1,0:T(1,128)S(1)}, f32[1,2048]{1,0:T(1,128)S(1)}, u32[]{:S(2)}, u32[]{:S(2)}) collective-permute-start(f32[1,2048]{1,0:T(1,128)S(1)} %add.32.refs_0_), channel_id=1, source_target_pairs={{0,2},{1,3},{2,0},{3,1},{4,6},{5,7},{6,4},{7,5},{8,10},{9,11},{10,... | collective-permute-start | bytes 24584 | tf_op jit(solution)/shard_map/ppermute | solution.py:36

commit v3 on v1

v3 whole, which is shorter than its diff:
```python
import functools

import jax
import jax.numpy as jnp
from jax import lax
from jax.experimental import pallas as pl
from jax.experimental.pallas import tpu as pltpu
from jax.sharding import PartitionSpec as P

ITERS = 3
MOST_PARTNERS = 8
BLOCK_BYTES = 20 * 2**20
VMEM = pltpu.VMEM
IN_VMEM = pl.BlockSpec(memory_space=pltpu.VMEM)
F32 = jnp.float32
LANES = 128


def unit_rows(matrix):
    values = matrix.astype(F32)
    scale = lax.rsqrt(1e-06 + jnp.sum(values * values, axis=1, keepdims=True))
    return (values * scale).astype(jnp.bfloat16)


def partners(size, stride, count, step):
    pairs = []
    for index in range(size):
        place = index // stride % count
        other = place ^ step if count & (count - 1) == 0 else (place + step) % count
        pairs.append((index, index + (other - place) * stride))
    return pairs


def from_others(value, axis, stride, count):
    size = lax.axis_size(axis)
    return [lax.ppermute(value, axis, partners(size, stride, count, step)) for step in range(1, count)]


def swap_cores(value):
    return lax.ppermute(value, "proto", partners(lax.axis_size("proto"), 1, 2, 1))


def group_sum(value, axis, stride, count):
    total = value
    for other in from_others(value, axis, stride, count):
        total = total + other
    return total


def proto_sums(partial_value):
    size = lax.axis_size("batch")
    if size > MOST_PARTNERS:
        return lax.psum(partial_value, "batch")
    return group_sum(partial_value, "batch", 1, size)


def image_sums(partial_value):
    size = lax.axis_size("proto")
    if size > 2 * MOST_PARTNERS or size % 2:
        return lax.psum(partial_value, "proto")
    pair = group_sum(partial_value, "proto", 1, 2)
    return group_sum(pair, "proto", 2, size // 2)


def split_plan(features, prototypes):
    unit_feat = unit_rows(features)
    gathered = lax.all_gather(unit_rows(prototypes), "batch", axis=0, tiled=True)
    scores = jnp.einsum("bd,kd->bk", unit_feat, gathered, preferred_element_type=F32)
    weights = jnp.exp(20.0 * scores)
    total_protos = float(weights.shape[1] * lax.axis_size("proto"))
    row_factor = jnp.ones((weights.shape[0],), F32)
    col_factor = jnp.ones((weights.shape[1],), F32)
    for step in range(ITERS):
        column_part = jnp.dot(row_factor, weights, precision=lax.Precision.HIGHEST)
        col_factor = 1.0 / proto_sums(column_part)
        row_part = jnp.dot(weights, col_factor, precision=lax.Precision.HIGHEST)
        row_factor = 1.0 / image_sums(row_part)
    scaled = weights * row_factor[:, None] * (total_protos * col_factor)[None, :]
    return scaled.astype(jnp.bfloat16)


def call(kernel, outs, args, limit, cost=0, aliases=None, scratch=()):
    pinned = [pltpu.with_memory_space_constraint(arg, VMEM) for arg in args]
    return pl.pallas_call(
        kernel,
        out_shape=[VMEM(shape, dtype) for shape, dtype in outs],
        in_specs=[IN_VMEM] * len(pinned),
        out_specs=[IN_VMEM] * len(outs),
        input_output_aliases=aliases or {},
        scratch_shapes=list(scratch),
        compiler_params=pltpu.CompilerParams(vmem_limit_bytes=limit * 2**20),
        cost_estimate=pl.CostEstimate(flops=cost, bytes_accessed=0, transcendentals=0),
    )(*pinned)


def scores_of(protos, images):
    return lax.dot_general(protos, images, (((1,), (1,)), ((), ())), preferred_element_type=F32)


def tiles(width):
    return [slice(start, start + LANES) for start in range(0, width, LANES)]


def fill(weights, total, rows, columns, unit_proto, unit_feat):
    step = 2 * LANES
    for column in range(columns.start, columns.stop, step):
        values = jnp.exp(20.0 * scores_of(unit_proto, unit_feat[column : column + step, :]))
        weights[rows, column : column + step] = values
        for tile in tiles(step):
            total = total + values[:, tile]
    return total


def add_images(part, weights, rows, col_factor):
    count = col_factor.shape[0]
    for tile in tiles(weights.shape[1]):
        product = weights[rows, tile] * col_factor
        part[:, tile] = part[:, tile] + jnp.sum(product.reshape(count // 8, 8, LANES), axis=0)


def spread(lane_sums):
    return jnp.broadcast_to(1.0 / jnp.sum(lane_sums, axis=1, keepdims=True), lane_sums.shape)


def unit_kernel(*refs):
    half = len(refs) // 2
    for raw, unit in zip(refs[:half], refs[half:]):
        unit[...] = unit_rows(raw[...])


def near_kernel(own_feat, near, near_swapped, own_proto, first, unit_feat, unit_proto, weights, sums):
    block = own_feat.shape[0]
    core = lax.axis_index("proto") % 2
    unit_feat[:block, :] = own_feat[...]
    unit_feat[pl.ds(pl.multiple_of((1 + core) * block, block), block), :] = unit_rows(near[...])
    unit_feat[pl.ds(pl.multiple_of((2 - core) * block, block), block), :] = unit_rows(near_swapped[...])
    unit_proto[:block, :] = own_proto[...]
    unit_proto[block : 2 * block, :] = unit_rows(first[...])

    def body(index, carry):
        rows = pl.ds(pl.multiple_of(index * block, block), block)
        total = jnp.zeros((block, LANES), F32)
        sums[rows, :] = fill(weights, total, rows, slice(0, 3 * block), unit_proto[rows, :], unit_feat)
        return carry

    lax.fori_loop(0, 2, body, 0)


def far_kernel(far, far_swapped, sums, unit_proto, feat_in, weights_in, unit_feat, weights, part):
    half = far.shape[0]
    block = 2 * half
    core = lax.axis_index("proto") % 2
    unit_feat[pl.ds(pl.multiple_of(3 * block + (1 - core) * half, half), half), :] = unit_rows(far[...])
    unit_feat[pl.ds(pl.multiple_of(3 * block + core * half, half), half), :] = unit_rows(far_swapped[...])
    part[...] = jnp.zeros(part.shape, F32)

    def body(index, carry):
        rows = pl.ds(pl.multiple_of(index * block, block), block)
        total = fill(weights, sums[rows, :], rows, slice(3 * block, 4 * block), unit_proto[rows, :], unit_feat)
        add_images(part, weights, rows, spread(total))
        return carry

    lax.fori_loop(0, 2, body, 0)


def more_kernel(index, raw, unit_feat, proto_in, weights_in, part_in, unit_proto, weights, part, *row_sums):
    block = raw.shape[0]
    rows = slice(index * block, (index + 1) * block)
    unit_proto[rows, :] = unit_rows(raw[...])
    total = jnp.zeros((block, LANES), F32)
    total = fill(weights, total, rows, slice(0, 4 * block), unit_proto[rows, :], unit_feat)
    add_images(part, weights, rows, spread(total))
    for store in row_sums:
        store[...] = flat(part)


def flat(part):
    return jnp.sum(part[...], axis=0, keepdims=True)


def summed(parts):
    total = parts[0][...]
    for part in parts[1:]:
        total = total + part[...]
    return total


def pass_kernel(count, block, *refs):
    parts, weights, row_sums, *col_factor, part = refs[:count], *refs[count:]
    row_factor = 1.0 / summed(parts)
    part[...] = jnp.zeros(part.shape, F32)

    def body(index, carry):
        rows = pl.ds(pl.multiple_of(index * block, block), block)
        total = jnp.zeros((block, LANES), F32)
        for tile in tiles(weights.shape[1]):
            total = total + weights[rows, tile] * row_factor[:, tile]
        factor = spread(total)
        for store in col_factor:
            store[rows, :] = factor
        add_images(part, weights, rows, factor)
        return carry

    lax.fori_loop(0, weights.shape[0] // block, body, 0)
    row_sums[...] = flat(part)


def ready_kernel(scale, unit_feat, unit_proto, col_factor, ready):
    block = ready.shape[0]
    images = unit_feat[:block, :]
    for start in range(0, ready.shape[1], block):
        values = jnp.exp(20.0 * scores_of(images, unit_proto[start : start + block, :]))
        for tile in tiles(block):
            at = slice(start + tile.start, start + tile.stop)
            factor = scale * jnp.transpose(col_factor[at, :])[:1, :]
            ready[:, at] = values[:, tile] * factor


def last_kernel(count, block, *refs):
    parts, ready, out, staged, sems = refs[:count], *refs[count:]
    total = summed(parts)
    factors = []
    for tile in tiles(block):
        factors.append(jnp.transpose(jnp.broadcast_to(1.0 / total[:, tile], (LANES, LANES))))
    factor = jnp.concatenate(factors, axis=0)
    place = lax.axis_index("batch")
    core = lax.axis_index("proto") % 2
    copies = []
    for index, step in enumerate((0, 1 + core, 2 - core, 3)):
        for tile in tiles(block):
            values = ready[:, index * block + tile.start : index * block + tile.stop]
            staged[index, :, tile] = (values * factor).astype(staged.dtype)
        column = pl.multiple_of(jnp.bitwise_xor(place, step) * block, block)
        copies.append(pltpu.make_async_copy(staged.at[index], out.at[:, pl.ds(column, block)], sems.at[index]))
        copies[-1].start()
    for copy in copies:
        copy.wait()


def by_core(steps):
    protos, blocks = lax.axis_size("proto"), lax.axis_size("batch")
    return [
        (place * protos + proto, (place ^ steps[proto % 2]) * protos + proto)
        for place in range(blocks)
        for proto in range(protos)
    ]


def send(value, steps):
    return lax.ppermute(value, ("batch", "proto"), by_core(steps))


def whole_plan(features, prototypes):
    bf16 = jnp.bfloat16
    blocks = lax.axis_size("batch")
    block, depth = features.shape
    images = blocks * block
    z_count = lax.axis_size("proto") // 2
    total_protos = float(images * lax.axis_size("proto"))
    feat_shape = ((images, depth), bf16)
    weights_shape = ((images, images), F32)
    part_shape = ((8, images), F32)
    lanes_shape = ((images, LANES), F32)

    half = block // 2
    core = lax.axis_index("proto") % 2
    own_feat, own_proto = call(unit_kernel, [((block, depth), bf16)] * 2, [features, prototypes], 4)
    near = send(features, (1, 2))
    first = send(prototypes, (1, 2))
    later, own_proto = lax.optimization_barrier((prototypes, own_proto))
    second = send(later, (2, 1))
    near_half = lax.dynamic_slice_in_dim(near, (1 - core) * half, half, 0)
    forward, own_feat, own_proto = lax.optimization_barrier((near_half, own_feat, own_proto))
    far = send(forward, (2, 1))
    last = send(first, (2, 1))
    unit_feat, unit_proto, weights, sums = call(
        near_kernel,
        [feat_shape, feat_shape, weights_shape, lanes_shape],
        [own_feat, near, swap_cores(near), own_proto, first],
        16,
    )
    unit_feat, weights, part = call(
        far_kernel,
        [feat_shape, weights_shape, part_shape],
        [far, swap_cores(far), sums, unit_proto, unit_feat, weights],
        16,
        aliases={4: 0, 5: 1},
    )
    outs = [feat_shape, weights_shape, part_shape, ((1, images), F32)]
    for index, raw in ((2, second), (3, last)):
        unit_proto, weights, part, *row_sums = call(
            functools.partial(more_kernel, index),
            outs if index == 3 else outs[:3],
            [raw, unit_feat, unit_proto, weights, part],
            16,
            aliases={2: 0, 3: 1, 4: 2},
        )

    def around(value):
        total = value + swap_cores(value)
        for other in reversed(from_others(total, "proto", 2, z_count)):
            total = lax.optimization_barrier(total + other)
        return [total]

    parts = around(*row_sums)
    for step in range(1, ITERS):
        outs = [((1, images), F32), lanes_shape]
        row_sums, *col_factor = call(
            functools.partial(pass_kernel, len(parts), block),
            outs if step == ITERS - 1 else outs[:1],
            [*parts, weights],
            8,
            cost=4 * images * images,
            scratch=[VMEM(*part_shape)],
        )
        parts = around(row_sums)
    (ready,) = call(
        functools.partial(ready_kernel, total_protos),
        [((block, images), F32)],
        [unit_feat, unit_proto, *col_factor],
        16,
        cost=2 * block * images * depth,
    )
    pinned = [pltpu.with_memory_space_constraint(arg, VMEM) for arg in [*parts, ready]]
    return pl.pallas_call(
        functools.partial(last_kernel, len(parts), block),
        out_shape=jax.ShapeDtypeStruct((block, images), bf16),
        in_specs=[IN_VMEM] * len(pinned),
        out_specs=pl.BlockSpec(memory_space=pl.ANY),
        scratch_shapes=[VMEM((blocks, block, block), bf16), pltpu.SemaphoreType.DMA((blocks,))],
        compiler_params=pltpu.CompilerParams(vmem_limit_bytes=8 * 2**20),
    )(*pinned)


def local(features, prototypes):
    blocks = lax.axis_size("batch")
    block, height = features.shape[0], prototypes.shape[0]
    fits = 4 * blocks * blocks * block * height <= BLOCK_BYTES
    even = block == height and block % (2 * LANES) == 0 and blocks == 4
    if fits and even and lax.axis_size("proto") % 2 == 0 and lax.axis_size("proto") <= 2 * MOST_PARTNERS:
        return whole_plan(features, prototypes)
    return split_plan(features, prototypes)


def solution(mesh):
    in_specs = (P("batch", None), P(("proto", "batch"), None))
    out_specs = P("batch", "proto")
    return jax.shard_map(local, mesh=mesh, in_specs=in_specs, out_specs=out_specs, check_vma=False)
```

time: 83.3 us -> 52 us (0.62)
  matrix products: 19 us -> 0 us
  waiting for transfers between devices: 30.4 us -> 16.3 us
  Pallas kernels: 0 us -> 12.4 us
  starting transfers between devices: 28.2 us -> 20.9 us
  other arithmetic: 5.08 us -> 0.13 us
  local copies, waits for them, and re-layouts: 0.14 us -> 1.91 us
    ppermute x24 -> x9, waiting for transfers between devices: 30.4 us -> 7.35 us  [from_others(): lax.ppermute(value, axis, partners(size, stride, count, step))]
    dot_general x7 -> x0, matrix products: 19 us -> none  [the longest x3 11.1 us: local(): row_part = jnp.dot(weights, col_factor, precision=lax.Precision.HIGHEST)]
    ppermute x24 -> x9, starting transfers between devices: 28.2 us -> 13.4 us  [from_others(): lax.ppermute(value, axis, partners(size, stride, count, step))]
    pallas_call x0 -> x9, Pallas kernels: none -> 12.4 us  [the longest x8 10.8 us: call(): pl.pallas_call(kernel, out_shape=[VMEM(shape, dtype) for shape, dtype in...]
    ppermute x0 -> x10, waiting for transfers between devices: none -> 8.95 us  [the longest x5 5.46 us: send(): return lax.ppermute(value, ('batch', 'proto'), by_core(steps))]
    ppermute x0 -> x10, starting transfers between devices: none -> 7.51 us  [the longest x5 7.22 us: send(): return lax.ppermute(value, ('batch', 'proto'), by_core(steps))]
    reduce_sum x2 -> x0, other arithmetic: 2.19 us -> none  [unit_rows(): scale = lax.rsqrt(1e-06 + jnp.sum(values * values, axis=1, keepdims=True))]
    unnamed x0 -> x4, local copies, waits for them, and re-layouts: none -> 1.9 us
  transfers between devices with their start and end apart: 24 -> 19, of which waited for: 20 -> 16; matrix products, arithmetic and copies ran while one was open for 1% -> 0% of each run, Pallas kernels for 0% -> 10%
where the time goes in v3:
time: 52 us; the launch traced here: 51.8 us
  starting transfers between devices  20.9 us (40%)
  waiting for transfers between devices  16.3 us (31%)
  Pallas kernels  12.4 us (24%)
  local copies, waits for them, and re-layouts  1.91 us (4%)
    ppermute x9, starting transfers between devices, from_others(): lax.ppermute(value, axis, partners(size, stride, count, step))  13.4 us
    pallas_call x8, Pallas kernels, call(): pl.pallas_call(kernel, out_shape=[VMEM(shape, dtype) for shape, dtype in...  10.8 us
    ppermute x9, waiting for transfers between devices, from_others(): lax.ppermute(value, axis, partners(size, stride, count, step))  7.35 us
    ppermute x5, starting transfers between devices, send(): return lax.ppermute(value, ('batch', 'proto'), by_core(steps))  7.22 us
    ppermute x5, waiting for transfers between devices, send(): return lax.ppermute(value, ('batch', 'proto'), by_core(steps))  5.46 us
    ppermute x5, waiting for transfers between devices, swap_cores(): lax.ppermute(value, 'proto', partners(lax.axis_size('proto'), 1, 2, 1))  3.48 us
    unnamed x4, local copies, waits for them, and re-layouts  1.9 us
    pallas_call x1, Pallas kernels, whole_plan(): pl.pallas_call(functools.partial(last_kernel, len(parts), block), out_sha...  1.68 us
  transfers between devices with their start and end apart: 19, of which 16 were waited for; matrix products, arithmetic and copies ran while one was open for 0% of the time, Pallas kernels for 10%

profile of v3, /device:TPU:0, one launch (start us, length us, event | category | flops | bytes accessed | tf_op | source)
XLA Modules:
  0.0 51.8 jit_solution(17089681586407270555)
XLA Ops:
  0.0 2.9 %collective-permute-start.2 = (bf16[512,256]{1,0:T(8,128)(2,1)}, bf16[512,256]{1,0:T(8,128)(2,1)S(1)}, u32[]{:S(2)}, u32[]{:S(2)}) collective-permute-start(bf16[512,256]{1,0:T(8,128)(2,1)} %refs_0_.1), channel_id=1, source_target_pairs={{0,8},{1,17},{2,10},{3,19},{4,12},{5,21},{6,14},{7,23},{8,0},{9,25... | collective-permute-start | bytes 786440 | tf_op jit(solution)/shard_map/ppermute | solution.py:250
  3.0 0.9 %copy-done = bf16[512,256]{1,0:T(8,128)(2,1)S(1)} copy-done((bf16[512,256]{1,0:T(8,128)(2,1)S(1)}, bf16[512,256]{1,0:T(8,128)(2,1)}, u32[]{:S(2)}) %copy-start) | copy-done | bytes 262168
  3.9 0.9 %copy-done.1 = bf16[512,256]{1,0:T(8,128)(2,1)S(1)} copy-done((bf16[512,256]{1,0:T(8,128)(2,1)S(1)}, bf16[512,256]{1,0:T(8,128)(2,1)}, u32[]{:S(2)}) %copy-start.1) | copy-done | bytes 262168
  5.1 2.4 %collective-permute-done.2.near = bf16[512,256]{1,0:T(8,128)(2,1)S(1)} collective-permute-done((bf16[512,256]{1,0:T(8,128)(2,1)}, bf16[512,256]{1,0:T(8,128)(2,1)S(1)}, u32[]{:S(2)}, u32[]{:S(2)}) %collective-permute-start.2) | collective-permute-done | bytes 262176 | tf_op jit(solution)/shard_map/ppermute | solution.py:250
  7.6 2.1 %collective-permute-start.3 = (bf16[256,256]{1,0:T(8,128)(2,1)S(1)}, bf16[256,256]{1,0:T(8,128)(2,1)S(1)}, u32[]{:S(2)}, u32[]{:S(2)}) collective-permute-start(bf16[256,256]{1,0:T(8,128)(2,1)S(1)} %constant_dynamic-slice_fusion), channel_id=1, source_target_pairs={{0,16},{1,9},{2,18},{3,11},{4,20},{5,13},{6,22},{7,15},{8,24},{9,1... | collective-permute-start | bytes 393224 | tf_op jit(solution)/shard_map/ppermute | solution.py:250
  9.8 0.5 %collective-permute-done.first = bf16[512,256]{1,0:T(8,128)(2,1)S(1)} collective-permute-done((bf16[512,256]{1,0:T(8,128)(2,1)}, bf16[512,256]{1,0:T(8,128)(2,1)S(1)}, u32[]{:S(2)}, u32[]{:S(2)}) %collective-permute-start) | collective-permute-done | bytes 262176 | tf_op jit(solution)/shard_map/ppermute | solution.py:250
  10.3 2.1 %collective-permute-start.1 = (bf16[512,256]{1,0:T(8,128)(2,1)S(1)}, bf16[512,256]{1,0:T(8,128)(2,1)S(1)}, u32[]{:S(2)}, u32[]{:S(2)}) collective-permute-start(bf16[512,256]{1,0:T(8,128)(2,1)S(1)} %collective-permute-done.first), channel_id=1, source_target_pairs={{0,16},{1,9},{2,18},{3,11},{4,20},{5,13},{6,22},{7,15},{8,24},{9,1... | collective-permute-start | bytes 786440 | tf_op jit(solution)/shard_map/ppermute | solution.py:250
  12.7 1.6 %shard_map.29 = (bf16[2048,256]{1,0:T(8,128)(2,1)S(1)}, bf16[2048,256]{1,0:T(8,128)(2,1)S(1)}, f32[2048,2048]{1,0:T(8,128)S(1)}, f32[2048,128]{1,0:T(8,128)S(1)}) custom-call(bf16[512,256]{1,0:T(8,128)(2,1)S(1)} %get-tuple-element.31.own_feat, bf16[512,256]{1,0:T(8,128)(2,1)S(1)} %collective-permute-done.2.near, ...), custom_call_target="tpu_custom_call" | custom-call | tf_op jit(solution)/shard_map/pallas_call | solution.py:84
  14.3 1.4 %shard_map.30 = (bf16[2048,256]{1,0:T(8,128)(2,1)S(1)}, f32[2048,2048]{1,0:T(8,128)S(1)}, f32[8,2048]{1,0:T(8,128)S(1)}) custom-call(bf16[256,256]{1,0:T(8,128)(2,1)S(1)} %collective-permute-done.3.far, bf16[256,256]{1,0:T(8,128)(2,1)S(1)} %collective-permute-done.4.far_swapped, ...), custom_call_target="tpu_custom_call", output_to_operand_aliasing={{0}: (4, {}), {1}: (5, {})} | custom-call | tf_op jit(solution)/shard_map/pallas_call | solution.py:84
  15.7 0.6 %collective-permute-done.6.raw = bf16[512,256]{1,0:T(8,128)(2,1)S(1)} collective-permute-done((bf16[512,256]{1,0:T(8,128)(2,1)}, bf16[512,256]{1,0:T(8,128)(2,1)S(1)}, u32[]{:S(2)}, u32[]{:S(2)}) %collective-permute-start.6) | collective-permute-done | bytes 262176 | tf_op jit(solution)/shard_map/ppermute | solution.py:250
  16.3 1.1 %shard_map.31 = (bf16[2048,256]{1,0:T(8,128)(2,1)S(1)}, f32[2048,2048]{1,0:T(8,128)S(1)}, f32[8,2048]{1,0:T(8,128)S(1)}) custom-call(bf16[512,256]{1,0:T(8,128)(2,1)S(1)} %collective-permute-done.6.raw, bf16[2048,256]{1,0:T(8,128)(2,1)S(1)} %get-tuple-element.37.unit_feat, ...), custom_call_target="tpu_custom_call", output_to_operand_aliasing={{0}: (2, {}), {1}: (3, {}), {2}: (4, {})} | custom-call | tf_op jit(solution)/shard_map/pallas_call | solution.py:84
  17.4 1.7 %collective-permute-done.1.raw = bf16[512,256]{1,0:T(8,128)(2,1)S(1)} collective-permute-done((bf16[512,256]{1,0:T(8,128)(2,1)S(1)}, bf16[512,256]{1,0:T(8,128)(2,1)S(1)}, u32[]{:S(2)}, u32[]{:S(2)}) %collective-permute-start.1) | collective-permute-done | bytes 262176 | tf_op jit(solution)/shard_map/ppermute | solution.py:250
  19.1 1.2 %shard_map.32 = (bf16[2048,256]{1,0:T(8,128)(2,1)S(1)}, f32[2048,2048]{1,0:T(8,128)S(1)}, f32[8,2048]{1,0:T(8,128)S(1)}, f32[1,2048]{1,0:T(1,128)S(1)}) custom-call(bf16[512,256]{1,0:T(8,128)(2,1)S(1)} %collective-permute-done.1.raw, bf16[2048,256]{1,0:T(8,128)(2,1)S(1)} %get-tuple-element.37.unit_feat, ...), custom_call_target="tpu_custom_call", output_to_operand_aliasing={{0}: (2, {}), {1}: (3, {}), {2}: (4, {})} | custom-call | tf_op jit(solution)/shard_map/pallas_call | solution.py:84
  20.3 1.2 %collective-permute-done.7 = f32[1,2048]{1,0:T(1,128)S(1)} collective-permute-done((f32[1,2048]{1,0:T(1,128)S(1)}, f32[1,2048]{1,0:T(1,128)S(1)}, u32[]{:S(2)}, u32[]{:S(2)}) %collective-permute-start.7) | collective-permute-done | bytes 8224 | tf_op jit(solution)/shard_map/ppermute | solution.py:40
  21.5 3.7 %collective-permute-start.8 = (f32[1,2048]{1,0:T(1,128)S(1)}, f32[1,2048]{1,0:T(1,128)S(1)}, u32[]{:S(2)}, u32[]{:S(2)}) collective-permute-start(f32[1,2048]{1,0:T(1,128)S(1)} %add.45), channel_id=1, source_target_pairs={{0,6},{1,7},{2,4},{3,5},{4,2},{5,3},{6,0},{7,1},{8,14},{9,15},{10,... | collective-permute-start | bytes 24584 | tf_op jit(solution)/shard_map/ppermute | solution.py:36
  25.2 0.8 %collective-permute-start.10 = (f32[1,2048]{1,0:T(1,128)S(1)}, f32[1,2048]{1,0:T(1,128)S(1)}, u32[]{:S(2)}, u32[]{:S(2)}) collective-permute-start(f32[1,2048]{1,0:T(1,128)S(1)} %add.45), channel_id=1, source_target_pairs={{0,2},{1,3},{2,0},{3,1},{4,6},{5,7},{6,4},{7,5},{8,10},{9,11},{10,... | collective-permute-start | bytes 24584 | tf_op jit(solution)/shard_map/ppermute | solution.py:36
  26.0 1.1 %collective-permute-done.8 = f32[1,2048]{1,0:T(1,128)S(1)} collective-permute-done((f32[1,2048]{1,0:T(1,128)S(1)}, f32[1,2048]{1,0:T(1,128)S(1)}, u32[]{:S(2)}, u32[]{:S(2)}) %collective-permute-start.8) | collective-permute-done | bytes 8224 | tf_op jit(solution)/shard_map/ppermute | solution.py:36
  27.1 2.7 %collective-permute-done.9 = f32[1,2048]{1,0:T(1,128)S(1)} collective-permute-done((f32[1,2048]{1,0:T(1,128)S(1)}, f32[1,2048]{1,0:T(1,128)S(1)}, u32[]{:S(2)}, u32[]{:S(2)}) %collective-permute-start.9) | collective-permute-done | bytes 8224 | tf_op jit(solution)/shard_map/ppermute | solution.py:36
  29.8 2.2 %shard_map.33 = f32[1,2048]{1,0:T(1,128)S(1)} custom-call(f32[1,2048]{1,0:T(1,128)S(1)} %add.48.refs_0_, f32[2048,2048]{1,0:T(8,128)S(1)} %get-tuple-element.45.refs_1_), custom_call_target="tpu_custom_call" | custom-call | flops 16777216 | tf_op jit(solution)/shard_map/pallas_call | solution.py:84
  32.1 1.2 %collective-permute-done.11 = f32[1,2048]{1,0:T(1,128)S(1)} collective-permute-done((f32[1,2048]{1,0:T(1,128)S(1)}, f32[1,2048]{1,0:T(1,128)S(1)}, u32[]{:S(2)}, u32[]{:S(2)}) %collective-permute-start.11) | collective-permute-done | bytes 8224 | tf_op jit(solution)/shard_map/ppermute | solution.py:40
  33.3 1.5 %collective-permute-start.12 = (f32[1,2048]{1,0:T(1,128)S(1)}, f32[1,2048]{1,0:T(1,128)S(1)}, u32[]{:S(2)}, u32[]{:S(2)}) collective-permute-start(f32[1,2048]{1,0:T(1,128)S(1)} %add.49), channel_id=1, source_target_pairs={{0,6},{1,7},{2,4},{3,5},{4,2},{5,3},{6,0},{7,1},{8,14},{9,15},{10,... | collective-permute-start | bytes 24584 | tf_op jit(solution)/shard_map/ppermute | solution.py:36
  34.8 0.6 %collective-permute-start.13 = (f32[1,2048]{1,0:T(1,128)S(1)}, f32[1,2048]{1,0:T(1,128)S(1)}, u32[]{:S(2)}, u32[]{:S(2)}) collective-permute-start(f32[1,2048]{1,0:T(1,128)S(1)} %add.49), channel_id=1, source_target_pairs={{0,4},{1,5},{2,6},{3,7},{4,0},{5,1},{6,2},{7,3},{8,12},{9,13},{10,... | collective-permute-start | bytes 24584 | tf_op jit(solution)/shard_map/ppermute | solution.py:36
  35.4 2.3 %collective-permute-start.14 = (f32[1,2048]{1,0:T(1,128)S(1)}, f32[1,2048]{1,0:T(1,128)S(1)}, u32[]{:S(2)}, u32[]{:S(2)}) collective-permute-start(f32[1,2048]{1,0:T(1,128)S(1)} %add.49), channel_id=1, source_target_pairs={{0,2},{1,3},{2,0},{3,1},{4,6},{5,7},{6,4},{7,5},{8,10},{9,11},{10,... | collective-permute-start | bytes 24584 | tf_op jit(solution)/shard_map/ppermute | solution.py:36
  37.7 1.1 %collective-permute-done.12 = f32[1,2048]{1,0:T(1,128)S(1)} collective-permute-done((f32[1,2048]{1,0:T(1,128)S(1)}, f32[1,2048]{1,0:T(1,128)S(1)}, u32[]{:S(2)}, u32[]{:S(2)}) %collective-permute-start.12) | collective-permute-done | bytes 8224 | tf_op jit(solution)/shard_map/ppermute | solution.py:36
  39.4 2.2 %shard_map.34 = (f32[1,2048]{1,0:T(1,128)S(1)}, f32[2048,128]{1,0:T(8,128)S(1)}) custom-call(f32[1,2048]{1,0:T(1,128)S(1)} %add.52.refs_0_, f32[2048,2048]{1,0:T(8,128)S(1)} %get-tuple-element.45.refs_1_), custom_call_target="tpu_custom_call" | custom-call | flops 16777216 | tf_op jit(solution)/shard_map/pallas_call | solution.py:84
  41.7 1.2 %collective-permute-done.15 = f32[1,2048]{1,0:T(1,128)S(1)} collective-permute-done((f32[1,2048]{1,0:T(1,128)S(1)}, f32[1,2048]{1,0:T(1,128)S(1)}, u32[]{:S(2)}, u32[]{:S(2)}) %collective-permute-start.15) | collective-permute-done | bytes 8224 | tf_op jit(solution)/shard_map/ppermute | solution.py:40
  42.9 2.6 %collective-permute-start.16 = (f32[1,2048]{1,0:T(1,128)S(1)}, f32[1,2048]{1,0:T(1,128)S(1)}, u32[]{:S(2)}, u32[]{:S(2)}) collective-permute-start(f32[1,2048]{1,0:T(1,128)S(1)} %add.53), channel_id=1, source_target_pairs={{0,6},{1,7},{2,4},{3,5},{4,2},{5,3},{6,0},{7,1},{8,14},{9,15},{10,... | collective-permute-start | bytes 24584 | tf_op jit(solution)/shard_map/ppermute | solution.py:36
  45.5 0.9 %collective-permute-start.17 = (f32[1,2048]{1,0:T(1,128)S(1)}, f32[1,2048]{1,0:T(1,128)S(1)}, u32[]{:S(2)}, u32[]{:S(2)}) collective-permute-start(f32[1,2048]{1,0:T(1,128)S(1)} %add.53), channel_id=1, source_target_pairs={{0,4},{1,5},{2,6},{3,7},{4,0},{5,1},{6,2},{7,3},{8,12},{9,13},{10,... | collective-permute-start | bytes 24584 | tf_op jit(solution)/shard_map/ppermute | solution.py:36
  46.4 1.0 %collective-permute-start.18 = (f32[1,2048]{1,0:T(1,128)S(1)}, f32[1,2048]{1,0:T(1,128)S(1)}, u32[]{:S(2)}, u32[]{:S(2)}) collective-permute-start(f32[1,2048]{1,0:T(1,128)S(1)} %add.53), channel_id=1, source_target_pairs={{0,2},{1,3},{2,0},{3,1},{4,6},{5,7},{6,4},{7,5},{8,10},{9,11},{10,... | collective-permute-start | bytes 24584 | tf_op jit(solution)/shard_map/ppermute | solution.py:36
  47.4 0.8 %shard_map.35.refs_1_ = f32[512,2048]{1,0:T(8,128)S(1)} custom-call(bf16[2048,256]{1,0:T(8,128)(2,1)S(1)} %get-tuple-element.37.unit_feat, bf16[2048,256]{1,0:T(8,128)(2,1)S(1)} %get-tuple-element.47.unit_proto, f32[2048,128]{1,0:T(8,128)S(1)} %get-tuple-element.48.col_factor), custom_call_target="tpu_custom_call" | custom-call | flops 536870912 | tf_op jit(solution)/shard_map/pallas_call | solution.py:84
  48.5 1.5 %collective-permute-done.17 = f32[1,2048]{1,0:T(1,128)S(1)} collective-permute-done((f32[1,2048]{1,0:T(1,128)S(1)}, f32[1,2048]{1,0:T(1,128)S(1)}, u32[]{:S(2)}, u32[]{:S(2)}) %collective-permute-start.17) | collective-permute-done | bytes 8224 | tf_op jit(solution)/shard_map/ppermute | solution.py:36
  50.1 1.7 %shard_map.36 = bf16[512,2048]{1,0:T(8,128)(2,1)} custom-call(f32[1,2048]{1,0:T(1,128)S(1)} %add.56.refs_0_, f32[512,2048]{1,0:T(8,128)S(1)} %shard_map.35.refs_1_), custom_call_target="tpu_custom_call" | custom-call | tf_op jit(solution)/shard_map/pallas_call | solution.py:325
  (32 shorter events, 2.0 us)
Async XLA Ops:
  0.0 7.5 %collective-permute-start.2 = (bf16[512,256]{1,0:T(8,128)(2,1)}, bf16[512,256]{1,0:T(8,128)(2,1)S(1)}, u32[]{:S(2)}, u32[]{:S(2)}) collective-permute-start(bf16[512,256]{1,0:T(8,128)(2,1)} %refs_0_.1), channel_id=1, source_target_pairs={{0,8},{1,17},{2,10},{3,19},{4,12},{5,21},{6,14},{7,23},{8,0},{9,25... | collective-permute-start | bytes 786440 | tf_op jit(solution)/shard_map/ppermute | solution.py:250
  2.9 7.4 %collective-permute-start = (bf16[512,256]{1,0:T(8,128)(2,1)}, bf16[512,256]{1,0:T(8,128)(2,1)S(1)}, u32[]{:S(2)}, u32[]{:S(2)}) collective-permute-start(bf16[512,256]{1,0:T(8,128)(2,1)} %refs_1_.1), channel_id=1, source_target_pairs={{0,8},{1,17},{2,10},{3,19},{4,12},{5,21},{6,14},{7,23},{8,0},{9,25... | collective-permute-start | bytes 786440 | tf_op jit(solution)/shard_map/ppermute | solution.py:250
  3.0 0.9 %copy-start = (bf16[512,256]{1,0:T(8,128)(2,1)S(1)}, bf16[512,256]{1,0:T(8,128)(2,1)}, u32[]{:S(2)}) copy-start(bf16[512,256]{1,0:T(8,128)(2,1)} %refs_0_.1) | copy-start | bytes 786436
  3.9 0.9 %copy-start.1 = (bf16[512,256]{1,0:T(8,128)(2,1)S(1)}, bf16[512,256]{1,0:T(8,128)(2,1)}, u32[]{:S(2)}) copy-start(bf16[512,256]{1,0:T(8,128)(2,1)} %refs_1_.1) | copy-start | bytes 786436
  7.5 5.2 %collective-permute-start.5 = (bf16[512,256]{1,0:T(8,128)(2,1)S(1)}, bf16[512,256]{1,0:T(8,128)(2,1)S(1)}, u32[]{:S(2)}, u32[]{:S(2)}) collective-permute-start(bf16[512,256]{1,0:T(8,128)(2,1)S(1)} %collective-permute-done.2.near), channel_id=1, source_target_pairs={{0,1},{1,0},{2,3},{3,2},{4,5},{5,4},{6,7},{7,6},{8,9},{9,8},{10,11... | collective-permute-start | bytes 786440 | tf_op jit(solution)/shard_map/ppermute | solution.py:40
  7.6 5.1 %collective-permute-start.3 = (bf16[256,256]{1,0:T(8,128)(2,1)S(1)}, bf16[256,256]{1,0:T(8,128)(2,1)S(1)}, u32[]{:S(2)}, u32[]{:S(2)}) collective-permute-start(bf16[256,256]{1,0:T(8,128)(2,1)S(1)} %constant_dynamic-slice_fusion), channel_id=1, source_target_pairs={{0,16},{1,9},{2,18},{3,11},{4,20},{5,13},{6,22},{7,15},{8,24},{9,1... | collective-permute-start | bytes 393224 | tf_op jit(solution)/shard_map/ppermute | solution.py:250
  9.7 6.6 %collective-permute-start.6 = (bf16[512,256]{1,0:T(8,128)(2,1)}, bf16[512,256]{1,0:T(8,128)(2,1)S(1)}, u32[]{:S(2)}, u32[]{:S(2)}) collective-permute-start(bf16[512,256]{1,0:T(8,128)(2,1)} %refs_1_.1), channel_id=1, source_target_pairs={{0,16},{1,9},{2,18},{3,11},{4,20},{5,13},{6,22},{7,15},{8,24},{9,1... | collective-permute-start | bytes 786440 | tf_op jit(solution)/shard_map/ppermute | solution.py:250
  10.3 8.8 %collective-permute-start.1 = (bf16[512,256]{1,0:T(8,128)(2,1)S(1)}, bf16[512,256]{1,0:T(8,128)(2,1)S(1)}, u32[]{:S(2)}, u32[]{:S(2)}) collective-permute-start(bf16[512,256]{1,0:T(8,128)(2,1)S(1)} %collective-permute-done.first), channel_id=1, source_target_pairs={{0,16},{1,9},{2,18},{3,11},{4,20},{5,13},{6,22},{7,15},{8,24},{9,1... | collective-permute-start | bytes 786440 | tf_op jit(solution)/shard_map/ppermute | solution.py:250
  12.7 1.6 %collective-permute-start.4 = (bf16[256,256]{1,0:T(8,128)(2,1)S(1)}, bf16[256,256]{1,0:T(8,128)(2,1)S(1)}, u32[]{:S(2)}, u32[]{:S(2)}) collective-permute-start(bf16[256,256]{1,0:T(8,128)(2,1)S(1)} %collective-permute-done.3.far), channel_id=1, source_target_pairs={{0,1},{1,0},{2,3},{3,2},{4,5},{5,4},{6,7},{7,6},{8,9},{9,8},{10,11... | collective-permute-start | bytes 393224 | tf_op jit(solution)/shard_map/ppermute | solution.py:40
  20.3 1.2 %collective-permute-start.7 = (f32[1,2048]{1,0:T(1,128)S(1)}, f32[1,2048]{1,0:T(1,128)S(1)}, u32[]{:S(2)}, u32[]{:S(2)}) collective-permute-start(f32[1,2048]{1,0:T(1,128)S(1)} %get-tuple-element.44), channel_id=1, source_target_pairs={{0,1},{1,0},{2,3},{3,2},{4,5},{5,4},{6,7},{7,6},{8,9},{9,8},{10,11... | collective-permute-start | bytes 24584 | tf_op jit(solution)/shard_map/ppermute | solution.py:40
  21.5 5.5 %collective-permute-start.8 = (f32[1,2048]{1,0:T(1,128)S(1)}, f32[1,2048]{1,0:T(1,128)S(1)}, u32[]{:S(2)}, u32[]{:S(2)}) collective-permute-start(f32[1,2048]{1,0:T(1,128)S(1)} %add.45), channel_id=1, source_target_pairs={{0,6},{1,7},{2,4},{3,5},{4,2},{5,3},{6,0},{7,1},{8,14},{9,15},{10,... | collective-permute-start | bytes 24584 | tf_op jit(solution)/shard_map/ppermute | solution.py:36
  25.2 4.5 %collective-permute-start.9 = (f32[1,2048]{1,0:T(1,128)S(1)}, f32[1,2048]{1,0:T(1,128)S(1)}, u32[]{:S(2)}, u32[]{:S(2)}) collective-permute-start(f32[1,2048]{1,0:T(1,128)S(1)} %add.45), channel_id=1, source_target_pairs={{0,4},{1,5},{2,6},{3,7},{4,0},{5,1},{6,2},{7,3},{8,12},{9,13},{10,... | collective-permute-start | bytes 24584 | tf_op jit(solution)/shard_map/ppermute | solution.py:36
  25.2 4.6 %collective-permute-start.10 = (f32[1,2048]{1,0:T(1,128)S(1)}, f32[1,2048]{1,0:T(1,128)S(1)}, u32[]{:S(2)}, u32[]{:S(2)}) collective-permute-start(f32[1,2048]{1,0:T(1,128)S(1)} %add.45), channel_id=1, source_target_pairs={{0,2},{1,3},{2,0},{3,1},{4,6},{5,7},{6,4},{7,5},{8,10},{9,11},{10,... | collective-permute-start | bytes 24584 | tf_op jit(solution)/shard_map/ppermute | solution.py:36
  32.0 1.2 %collective-permute-start.11 = (f32[1,2048]{1,0:T(1,128)S(1)}, f32[1,2048]{1,0:T(1,128)S(1)}, u32[]{:S(2)}, u32[]{:S(2)}) collective-permute-start(f32[1,2048]{1,0:T(1,128)S(1)} %shard_map.33), channel_id=1, source_target_pairs={{0,1},{1,0},{2,3},{3,2},{4,5},{5,4},{6,7},{7,6},{8,9},{9,8},{10,11... | collective-permute-start | bytes 24584 | tf_op jit(solution)/shard_map/ppermute | solution.py:40
  33.3 5.6 %collective-permute-start.12 = (f32[1,2048]{1,0:T(1,128)S(1)}, f32[1,2048]{1,0:T(1,128)S(1)}, u32[]{:S(2)}, u32[]{:S(2)}) collective-permute-start(f32[1,2048]{1,0:T(1,128)S(1)} %add.49), channel_id=1, source_target_pairs={{0,6},{1,7},{2,4},{3,5},{4,2},{5,3},{6,0},{7,1},{8,14},{9,15},{10,... | collective-permute-start | bytes 24584 | tf_op jit(solution)/shard_map/ppermute | solution.py:36
  34.8 4.5 %collective-permute-start.13 = (f32[1,2048]{1,0:T(1,128)S(1)}, f32[1,2048]{1,0:T(1,128)S(1)}, u32[]{:S(2)}, u32[]{:S(2)}) collective-permute-start(f32[1,2048]{1,0:T(1,128)S(1)} %add.49), channel_id=1, source_target_pairs={{0,4},{1,5},{2,6},{3,7},{4,0},{5,1},{6,2},{7,3},{8,12},{9,13},{10,... | collective-permute-start | bytes 24584 | tf_op jit(solution)/shard_map/ppermute | solution.py:36
  35.4 4.0 %collective-permute-start.14 = (f32[1,2048]{1,0:T(1,128)S(1)}, f32[1,2048]{1,0:T(1,128)S(1)}, u32[]{:S(2)}, u32[]{:S(2)}) collective-permute-start(f32[1,2048]{1,0:T(1,128)S(1)} %add.49), channel_id=1, source_target_pairs={{0,2},{1,3},{2,0},{3,1},{4,6},{5,7},{6,4},{7,5},{8,10},{9,11},{10,... | collective-permute-start | bytes 24584 | tf_op jit(solution)/shard_map/ppermute | solution.py:36
  41.7 1.2 %collective-permute-start.15 = (f32[1,2048]{1,0:T(1,128)S(1)}, f32[1,2048]{1,0:T(1,128)S(1)}, u32[]{:S(2)}, u32[]{:S(2)}) collective-permute-start(f32[1,2048]{1,0:T(1,128)S(1)} %get-tuple-element.46), channel_id=1, source_target_pairs={{0,1},{1,0},{2,3},{3,2},{4,5},{5,4},{6,7},{7,6},{8,9},{9,8},{10,11... | collective-permute-start | bytes 24584 | tf_op jit(solution)/shard_map/ppermute | solution.py:40
  42.9 5.6 %collective-permute-start.16 = (f32[1,2048]{1,0:T(1,128)S(1)}, f32[1,2048]{1,0:T(1,128)S(1)}, u32[]{:S(2)}, u32[]{:S(2)}) collective-permute-start(f32[1,2048]{1,0:T(1,128)S(1)} %add.53), channel_id=1, source_target_pairs={{0,6},{1,7},{2,4},{3,5},{4,2},{5,3},{6,0},{7,1},{8,14},{9,15},{10,... | collective-permute-start | bytes 24584 | tf_op jit(solution)/shard_map/ppermute | solution.py:36
  45.5 4.5 %collective-permute-start.17 = (f32[1,2048]{1,0:T(1,128)S(1)}, f32[1,2048]{1,0:T(1,128)S(1)}, u32[]{:S(2)}, u32[]{:S(2)}) collective-permute-start(f32[1,2048]{1,0:T(1,128)S(1)} %add.53), channel_id=1, source_target_pairs={{0,4},{1,5},{2,6},{3,7},{4,0},{5,1},{6,2},{7,3},{8,12},{9,13},{10,... | collective-permute-start | bytes 24584 | tf_op jit(solution)/shard_map/ppermute | solution.py:36
  46.4 3.7 %collective-permute-start.18 = (f32[1,2048]{1,0:T(1,128)S(1)}, f32[1,2048]{1,0:T(1,128)S(1)}, u32[]{:S(2)}, u32[]{:S(2)}) collective-permute-start(f32[1,2048]{1,0:T(1,128)S(1)} %add.53), channel_id=1, source_target_pairs={{0,2},{1,3},{2,0},{3,1},{4,6},{5,7},{6,4},{7,5},{8,10},{9,11},{10,... | collective-permute-start | bytes 24584 | tf_op jit(solution)/shard_map/ppermute | solution.py:36

commit v4 on v3

--- a/solution.py
+++ b/solution.py
@@ -89,7 +89,7 @@
         input_output_aliases=aliases or {},
         scratch_shapes=list(scratch),
         compiler_params=pltpu.CompilerParams(vmem_limit_bytes=limit * 2**20),
-        cost_estimate=pl.CostEstimate(flops=cost, bytes_accessed=0, transcendentals=0),
+        cost_estimate=pl.CostEstimate(flops=max(cost,1), bytes_accessed=1, transcendentals=1),
     )(*pinned)
 
 
@@ -113,7 +113,7 @@
 
 def add_images(part, weights, rows, col_factor):
     count = col_factor.shape[0]
-    for tile in tiles(weights.shape[1]):
+    for tile in tiles(part.shape[1]):
         product = weights[rows, tile] * col_factor
         part[:, tile] = part[:, tile] + jnp.sum(product.reshape(count // 8, 8, LANES), axis=0)
 
@@ -304,14 +304,15 @@
 
     parts = around(*row_sums)
     for step in range(1, ITERS):
-        outs = [((1, images), F32), lanes_shape]
+        final = step == ITERS - 1
+        wanted = block if final else images
         row_sums, *col_factor = call(
             functools.partial(pass_kernel, len(parts), block),
-            outs if step == ITERS - 1 else outs[:1],
+            [((1, wanted), F32), lanes_shape] if final else [((1, wanted), F32)],
             [*parts, weights],
             8,
             cost=4 * images * images,
-            scratch=[VMEM(*part_shape)],
+            scratch=[VMEM((8, wanted), F32)],
         )
         parts = around(row_sums)
     (ready,) = call(

time: 52 us -> 51 us (0.981)
  Pallas kernels: 12.4 us -> 11.7 us
    pallas_call x8, Pallas kernels: 10.8 us -> 9.99 us  [call(): pl.pallas_call(kernel, out_shape=[VMEM(shape, dtype) for shape, dtype in...]
  transfers between devices with their start and end apart: 19 -> 19, of which waited for: 16 -> 15; matrix products, arithmetic and copies ran while one was open for 0% -> 0% of each run, Pallas kernels for 10% -> 10%
where the time goes in v4:
time: 51 us; the launch traced here: 50.8 us
  starting transfers between devices  20.8 us (41%)
  waiting for transfers between devices  16.2 us (32%)
  Pallas kernels  11.7 us (23%)
  local copies, waits for them, and re-layouts  1.91 us (4%)
    ppermute x9, starting transfers between devices, from_others(): lax.ppermute(value, axis, partners(size, stride, count, step))  13.3 us
    pallas_call x8, Pallas kernels, call(): pl.pallas_call(kernel, out_shape=[VMEM(shape, dtype) for shape, dtype in...  9.99 us
    ppermute x9, waiting for transfers between devices, from_others(): lax.ppermute(value, axis, partners(size, stride, count, step))  7.24 us
    ppermute x5, starting transfers between devices, send(): return lax.ppermute(value, ('batch', 'proto'), by_core(steps))  7.22 us
    ppermute x5, waiting for transfers between devices, send(): return lax.ppermute(value, ('batch', 'proto'), by_core(steps))  5.46 us
    ppermute x5, waiting for transfers between devices, swap_cores(): lax.ppermute(value, 'proto', partners(lax.axis_size('proto'), 1, 2, 1))  3.47 us
    unnamed x4, local copies, waits for them, and re-layouts  1.9 us
    pallas_call x1, Pallas kernels, whole_plan(): pl.pallas_call(functools.partial(last_kernel, len(parts), block), out_sha...  1.68 us
  transfers between devices with their start and end apart: 19, of which 15 were waited for; matrix products, arithmetic and copies ran while one was open for 0% of the time, Pallas kernels for 10%

profile of v4, /device:TPU:0, one launch (start us, length us, event | category | flops | bytes accessed | tf_op | source)
XLA Modules:
  0.0 50.8 jit_solution(4622630245972477999)
XLA Ops:
  0.0 2.9 %collective-permute-start.2 = (bf16[512,256]{1,0:T(8,128)(2,1)}, bf16[512,256]{1,0:T(8,128)(2,1)S(1)}, u32[]{:S(2)}, u32[]{:S(2)}) collective-permute-start(bf16[512,256]{1,0:T(8,128)(2,1)} %refs_0_.1), channel_id=1, source_target_pairs={{0,8},{1,17},{2,10},{3,19},{4,12},{5,21},{6,14},{7,23},{8,0},{9,25... | collective-permute-start | bytes 786440 | tf_op jit(solution)/shard_map/ppermute | solution.py:250
  3.0 0.9 %copy-done = bf16[512,256]{1,0:T(8,128)(2,1)S(1)} copy-done((bf16[512,256]{1,0:T(8,128)(2,1)S(1)}, bf16[512,256]{1,0:T(8,128)(2,1)}, u32[]{:S(2)}) %copy-start) | copy-done | bytes 262168
  3.9 0.9 %copy-done.1 = bf16[512,256]{1,0:T(8,128)(2,1)S(1)} copy-done((bf16[512,256]{1,0:T(8,128)(2,1)S(1)}, bf16[512,256]{1,0:T(8,128)(2,1)}, u32[]{:S(2)}) %copy-start.1) | copy-done | bytes 262168
  5.1 2.4 %collective-permute-done.2.near = bf16[512,256]{1,0:T(8,128)(2,1)S(1)} collective-permute-done((bf16[512,256]{1,0:T(8,128)(2,1)}, bf16[512,256]{1,0:T(8,128)(2,1)S(1)}, u32[]{:S(2)}, u32[]{:S(2)}) %collective-permute-start.2) | collective-permute-done | bytes 262176 | tf_op jit(solution)/shard_map/ppermute | solution.py:250
  7.6 2.1 %collective-permute-start.3 = (bf16[256,256]{1,0:T(8,128)(2,1)S(1)}, bf16[256,256]{1,0:T(8,128)(2,1)S(1)}, u32[]{:S(2)}, u32[]{:S(2)}) collective-permute-start(bf16[256,256]{1,0:T(8,128)(2,1)S(1)} %constant_dynamic-slice_fusion), channel_id=1, source_target_pairs={{0,16},{1,9},{2,18},{3,11},{4,20},{5,13},{6,22},{7,15},{8,24},{9,1... | collective-permute-start | bytes 393224 | tf_op jit(solution)/shard_map/ppermute | solution.py:250
  9.8 0.5 %collective-permute-done.first = bf16[512,256]{1,0:T(8,128)(2,1)S(1)} collective-permute-done((bf16[512,256]{1,0:T(8,128)(2,1)}, bf16[512,256]{1,0:T(8,128)(2,1)S(1)}, u32[]{:S(2)}, u32[]{:S(2)}) %collective-permute-start) | collective-permute-done | bytes 262176 | tf_op jit(solution)/shard_map/ppermute | solution.py:250
  10.3 2.1 %collective-permute-start.1 = (bf16[512,256]{1,0:T(8,128)(2,1)S(1)}, bf16[512,256]{1,0:T(8,128)(2,1)S(1)}, u32[]{:S(2)}, u32[]{:S(2)}) collective-permute-start(bf16[512,256]{1,0:T(8,128)(2,1)S(1)} %collective-permute-done.first), channel_id=1, source_target_pairs={{0,16},{1,9},{2,18},{3,11},{4,20},{5,13},{6,22},{7,15},{8,24},{9,1... | collective-permute-start | bytes 786440 | tf_op jit(solution)/shard_map/ppermute | solution.py:250
  12.7 1.6 %shard_map.29 = (bf16[2048,256]{1,0:T(8,128)(2,1)S(1)}, bf16[2048,256]{1,0:T(8,128)(2,1)S(1)}, f32[2048,2048]{1,0:T(8,128)S(1)}, f32[2048,128]{1,0:T(8,128)S(1)}) custom-call(bf16[512,256]{1,0:T(8,128)(2,1)S(1)} %get-tuple-element.31.own_feat, bf16[512,256]{1,0:T(8,128)(2,1)S(1)} %collective-permute-done.2.near, ...), custom_call_target="tpu_custom_call" | custom-call | flops 1 | bytes 1 | tf_op jit(solution)/shard_map/pallas_call | solution.py:84
  14.3 1.4 %shard_map.30 = (bf16[2048,256]{1,0:T(8,128)(2,1)S(1)}, f32[2048,2048]{1,0:T(8,128)S(1)}, f32[8,2048]{1,0:T(8,128)S(1)}) custom-call(bf16[256,256]{1,0:T(8,128)(2,1)S(1)} %collective-permute-done.3.far, bf16[256,256]{1,0:T(8,128)(2,1)S(1)} %collective-permute-done.4.far_swapped, ...), custom_call_target="tpu_custom_call", output_to_operand_aliasing={{0}: (4, {}), {1}: (5, {})} | custom-call | flops 1 | bytes 1 | tf_op jit(solution)/shard_map/pallas_call | solution.py:84
  15.7 0.6 %collective-permute-done.6.raw = bf16[512,256]{1,0:T(8,128)(2,1)S(1)} collective-permute-done((bf16[512,256]{1,0:T(8,128)(2,1)}, bf16[512,256]{1,0:T(8,128)(2,1)S(1)}, u32[]{:S(2)}, u32[]{:S(2)}) %collective-permute-start.6) | collective-permute-done | bytes 262176 | tf_op jit(solution)/shard_map/ppermute | solution.py:250
  16.3 1.1 %shard_map.31 = (bf16[2048,256]{1,0:T(8,128)(2,1)S(1)}, f32[2048,2048]{1,0:T(8,128)S(1)}, f32[8,2048]{1,0:T(8,128)S(1)}) custom-call(bf16[512,256]{1,0:T(8,128)(2,1)S(1)} %collective-permute-done.6.raw, bf16[2048,256]{1,0:T(8,128)(2,1)S(1)} %get-tuple-element.37.unit_feat, ...), custom_call_target="tpu_custom_call", output_to_operand_aliasing={{0}: (2, {}), {1}: (3, {}), {2}: (4, {})} | custom-call | flops 1 | bytes 1 | tf_op jit(solution)/shard_map/pallas_call | solution.py:84
  17.4 1.7 %collective-permute-done.1.raw = bf16[512,256]{1,0:T(8,128)(2,1)S(1)} collective-permute-done((bf16[512,256]{1,0:T(8,128)(2,1)S(1)}, bf16[512,256]{1,0:T(8,128)(2,1)S(1)}, u32[]{:S(2)}, u32[]{:S(2)}) %collective-permute-start.1) | collective-permute-done | bytes 262176 | tf_op jit(solution)/shard_map/ppermute | solution.py:250
  19.1 1.2 %shard_map.32 = (bf16[2048,256]{1,0:T(8,128)(2,1)S(1)}, f32[2048,2048]{1,0:T(8,128)S(1)}, f32[8,2048]{1,0:T(8,128)S(1)}, f32[1,2048]{1,0:T(1,128)S(1)}) custom-call(bf16[512,256]{1,0:T(8,128)(2,1)S(1)} %collective-permute-done.1.raw, bf16[2048,256]{1,0:T(8,128)(2,1)S(1)} %get-tuple-element.37.unit_feat, ...), custom_call_target="tpu_custom_call", output_to_operand_aliasing={{0}: (2, {}), {1}: (3, {}), {2}: (4, {})} | custom-call | flops 1 | bytes 1 | tf_op jit(solution)/shard_map/pallas_call | solution.py:84
  20.3 1.2 %collective-permute-done.7 = f32[1,2048]{1,0:T(1,128)S(1)} collective-permute-done((f32[1,2048]{1,0:T(1,128)S(1)}, f32[1,2048]{1,0:T(1,128)S(1)}, u32[]{:S(2)}, u32[]{:S(2)}) %collective-permute-start.7) | collective-permute-done | bytes 8224 | tf_op jit(solution)/shard_map/ppermute | solution.py:40
  21.5 3.7 %collective-permute-start.8 = (f32[1,2048]{1,0:T(1,128)S(1)}, f32[1,2048]{1,0:T(1,128)S(1)}, u32[]{:S(2)}, u32[]{:S(2)}) collective-permute-start(f32[1,2048]{1,0:T(1,128)S(1)} %add.45), channel_id=1, source_target_pairs={{0,6},{1,7},{2,4},{3,5},{4,2},{5,3},{6,0},{7,1},{8,14},{9,15},{10,... | collective-permute-start | bytes 24584 | tf_op jit(solution)/shard_map/ppermute | solution.py:36
  25.2 0.8 %collective-permute-start.10 = (f32[1,2048]{1,0:T(1,128)S(1)}, f32[1,2048]{1,0:T(1,128)S(1)}, u32[]{:S(2)}, u32[]{:S(2)}) collective-permute-start(f32[1,2048]{1,0:T(1,128)S(1)} %add.45), channel_id=1, source_target_pairs={{0,2},{1,3},{2,0},{3,1},{4,6},{5,7},{6,4},{7,5},{8,10},{9,11},{10,... | collective-permute-start | bytes 24584 | tf_op jit(solution)/shard_map/ppermute | solution.py:36
  26.0 1.1 %collective-permute-done.8 = f32[1,2048]{1,0:T(1,128)S(1)} collective-permute-done((f32[1,2048]{1,0:T(1,128)S(1)}, f32[1,2048]{1,0:T(1,128)S(1)}, u32[]{:S(2)}, u32[]{:S(2)}) %collective-permute-start.8) | collective-permute-done | bytes 8224 | tf_op jit(solution)/shard_map/ppermute | solution.py:36
  27.1 2.7 %collective-permute-done.9 = f32[1,2048]{1,0:T(1,128)S(1)} collective-permute-done((f32[1,2048]{1,0:T(1,128)S(1)}, f32[1,2048]{1,0:T(1,128)S(1)}, u32[]{:S(2)}, u32[]{:S(2)}) %collective-permute-start.9) | collective-permute-done | bytes 8224 | tf_op jit(solution)/shard_map/ppermute | solution.py:36
  29.8 2.2 %shard_map.33 = f32[1,2048]{1,0:T(1,128)S(1)} custom-call(f32[1,2048]{1,0:T(1,128)S(1)} %add.48.refs_0_, f32[2048,2048]{1,0:T(8,128)S(1)} %get-tuple-element.45.refs_1_), custom_call_target="tpu_custom_call" | custom-call | flops 16777216 | bytes 1 | tf_op jit(solution)/shard_map/pallas_call | solution.py:84
  32.1 1.2 %collective-permute-done.11 = f32[1,2048]{1,0:T(1,128)S(1)} collective-permute-done((f32[1,2048]{1,0:T(1,128)S(1)}, f32[1,2048]{1,0:T(1,128)S(1)}, u32[]{:S(2)}, u32[]{:S(2)}) %collective-permute-start.11) | collective-permute-done | bytes 8224 | tf_op jit(solution)/shard_map/ppermute | solution.py:40
  33.3 1.5 %collective-permute-start.12 = (f32[1,2048]{1,0:T(1,128)S(1)}, f32[1,2048]{1,0:T(1,128)S(1)}, u32[]{:S(2)}, u32[]{:S(2)}) collective-permute-start(f32[1,2048]{1,0:T(1,128)S(1)} %add.49), channel_id=1, source_target_pairs={{0,6},{1,7},{2,4},{3,5},{4,2},{5,3},{6,0},{7,1},{8,14},{9,15},{10,... | collective-permute-start | bytes 24584 | tf_op jit(solution)/shard_map/ppermute | solution.py:36
  34.8 0.6 %collective-permute-start.13 = (f32[1,2048]{1,0:T(1,128)S(1)}, f32[1,2048]{1,0:T(1,128)S(1)}, u32[]{:S(2)}, u32[]{:S(2)}) collective-permute-start(f32[1,2048]{1,0:T(1,128)S(1)} %add.49), channel_id=1, source_target_pairs={{0,4},{1,5},{2,6},{3,7},{4,0},{5,1},{6,2},{7,3},{8,12},{9,13},{10,... | collective-permute-start | bytes 24584 | tf_op jit(solution)/shard_map/ppermute | solution.py:36
  35.4 2.3 %collective-permute-start.14 = (f32[1,2048]{1,0:T(1,128)S(1)}, f32[1,2048]{1,0:T(1,128)S(1)}, u32[]{:S(2)}, u32[]{:S(2)}) collective-permute-start(f32[1,2048]{1,0:T(1,128)S(1)} %add.49), channel_id=1, source_target_pairs={{0,2},{1,3},{2,0},{3,1},{4,6},{5,7},{6,4},{7,5},{8,10},{9,11},{10,... | collective-permute-start | bytes 24584 | tf_op jit(solution)/shard_map/ppermute | solution.py:36
  37.7 1.1 %collective-permute-done.12 = f32[1,2048]{1,0:T(1,128)S(1)} collective-permute-done((f32[1,2048]{1,0:T(1,128)S(1)}, f32[1,2048]{1,0:T(1,128)S(1)}, u32[]{:S(2)}, u32[]{:S(2)}) %collective-permute-start.12) | collective-permute-done | bytes 8224 | tf_op jit(solution)/shard_map/ppermute | solution.py:36
  39.4 1.4 %shard_map.34 = (f32[1,512]{1,0:T(1,128)S(1)}, f32[2048,128]{1,0:T(8,128)S(1)}) custom-call(f32[1,2048]{1,0:T(1,128)S(1)} %add.52.refs_0_, f32[2048,2048]{1,0:T(8,128)S(1)} %get-tuple-element.45.refs_1_), custom_call_target="tpu_custom_call" | custom-call | flops 16777216 | bytes 1 | tf_op jit(solution)/shard_map/pallas_call | solution.py:84
  41.0 1.1 %collective-permute-done.15 = f32[1,512]{1,0:T(1,128)S(1)} collective-permute-done((f32[1,512]{1,0:T(1,128)S(1)}, f32[1,512]{1,0:T(1,128)S(1)}, u32[]{:S(2)}, u32[]{:S(2)}) %collective-permute-start.15) | collective-permute-done | bytes 2080 | tf_op jit(solution)/shard_map/ppermute | solution.py:40
  42.1 2.5 %collective-permute-start.16 = (f32[1,512]{1,0:T(1,128)S(1)}, f32[1,512]{1,0:T(1,128)S(1)}, u32[]{:S(2)}, u32[]{:S(2)}) collective-permute-start(f32[1,512]{1,0:T(1,128)S(1)} %add.53), channel_id=1, source_target_pairs={{0,6},{1,7},{2,4},{3,5},{4,2},{5,3},{6,0},{7,1},{8,14},{9,15},{10,... | collective-permute-start | bytes 6152 | tf_op jit(solution)/shard_map/ppermute | solution.py:36
  44.6 0.9 %collective-permute-start.17 = (f32[1,512]{1,0:T(1,128)S(1)}, f32[1,512]{1,0:T(1,128)S(1)}, u32[]{:S(2)}, u32[]{:S(2)}) collective-permute-start(f32[1,512]{1,0:T(1,128)S(1)} %add.53), channel_id=1, source_target_pairs={{0,4},{1,5},{2,6},{3,7},{4,0},{5,1},{6,2},{7,3},{8,12},{9,13},{10,... | collective-permute-start | bytes 6152 | tf_op jit(solution)/shard_map/ppermute | solution.py:36
  45.5 1.0 %collective-permute-start.18 = (f32[1,512]{1,0:T(1,128)S(1)}, f32[1,512]{1,0:T(1,128)S(1)}, u32[]{:S(2)}, u32[]{:S(2)}) collective-permute-start(f32[1,512]{1,0:T(1,128)S(1)} %add.53), channel_id=1, source_target_pairs={{0,2},{1,3},{2,0},{3,1},{4,6},{5,7},{6,4},{7,5},{8,10},{9,11},{10,... | collective-permute-start | bytes 6152 | tf_op jit(solution)/shard_map/ppermute | solution.py:36
  46.5 0.8 %shard_map.35.refs_1_ = f32[512,2048]{1,0:T(8,128)S(1)} custom-call(bf16[2048,256]{1,0:T(8,128)(2,1)S(1)} %get-tuple-element.37.unit_feat, bf16[2048,256]{1,0:T(8,128)(2,1)S(1)} %get-tuple-element.47.unit_proto, f32[2048,128]{1,0:T(8,128)S(1)} %get-tuple-element.48.col_factor), custom_call_target="tpu_custom_call" | custom-call | flops 536870912 | bytes 1 | tf_op jit(solution)/shard_map/pallas_call | solution.py:84
  47.5 1.6 %collective-permute-done.17 = f32[1,512]{1,0:T(1,128)S(1)} collective-permute-done((f32[1,512]{1,0:T(1,128)S(1)}, f32[1,512]{1,0:T(1,128)S(1)}, u32[]{:S(2)}, u32[]{:S(2)}) %collective-permute-start.17) | collective-permute-done | bytes 2080 | tf_op jit(solution)/shard_map/ppermute | solution.py:36
  49.1 1.7 %shard_map.36 = bf16[512,2048]{1,0:T(8,128)(2,1)} custom-call(f32[1,512]{1,0:T(1,128)S(1)} %add.56.refs_0_, f32[512,2048]{1,0:T(8,128)S(1)} %shard_map.35.refs_1_), custom_call_target="tpu_custom_call" | custom-call | tf_op jit(solution)/shard_map/pallas_call | solution.py:326
  (32 shorter events, 1.8 us)
Async XLA Ops:
  0.0 7.5 %collective-permute-start.2 = (bf16[512,256]{1,0:T(8,128)(2,1)}, bf16[512,256]{1,0:T(8,128)(2,1)S(1)}, u32[]{:S(2)}, u32[]{:S(2)}) collective-permute-start(bf16[512,256]{1,0:T(8,128)(2,1)} %refs_0_.1), channel_id=1, source_target_pairs={{0,8},{1,17},{2,10},{3,19},{4,12},{5,21},{6,14},{7,23},{8,0},{9,25... | collective-permute-start | bytes 786440 | tf_op jit(solution)/shard_map/ppermute | solution.py:250
  2.9 7.4 %collective-permute-start = (bf16[512,256]{1,0:T(8,128)(2,1)}, bf16[512,256]{1,0:T(8,128)(2,1)S(1)}, u32[]{:S(2)}, u32[]{:S(2)}) collective-permute-start(bf16[512,256]{1,0:T(8,128)(2,1)} %refs_1_.1), channel_id=1, source_target_pairs={{0,8},{1,17},{2,10},{3,19},{4,12},{5,21},{6,14},{7,23},{8,0},{9,25... | collective-permute-start | bytes 786440 | tf_op jit(solution)/shard_map/ppermute | solution.py:250
  3.0 0.9 %copy-start = (bf16[512,256]{1,0:T(8,128)(2,1)S(1)}, bf16[512,256]{1,0:T(8,128)(2,1)}, u32[]{:S(2)}) copy-start(bf16[512,256]{1,0:T(8,128)(2,1)} %refs_0_.1) | copy-start | bytes 786436
  3.9 0.9 %copy-start.1 = (bf16[512,256]{1,0:T(8,128)(2,1)S(1)}, bf16[512,256]{1,0:T(8,128)(2,1)}, u32[]{:S(2)}) copy-start(bf16[512,256]{1,0:T(8,128)(2,1)} %refs_1_.1) | copy-start | bytes 786436
  7.5 5.2 %collective-permute-start.5 = (bf16[512,256]{1,0:T(8,128)(2,1)S(1)}, bf16[512,256]{1,0:T(8,128)(2,1)S(1)}, u32[]{:S(2)}, u32[]{:S(2)}) collective-permute-start(bf16[512,256]{1,0:T(8,128)(2,1)S(1)} %collective-permute-done.2.near), channel_id=1, source_target_pairs={{0,1},{1,0},{2,3},{3,2},{4,5},{5,4},{6,7},{7,6},{8,9},{9,8},{10,11... | collective-permute-start | bytes 786440 | tf_op jit(solution)/shard_map/ppermute | solution.py:40
  7.6 5.1 %collective-permute-start.3 = (bf16[256,256]{1,0:T(8,128)(2,1)S(1)}, bf16[256,256]{1,0:T(8,128)(2,1)S(1)}, u32[]{:S(2)}, u32[]{:S(2)}) collective-permute-start(bf16[256,256]{1,0:T(8,128)(2,1)S(1)} %constant_dynamic-slice_fusion), channel_id=1, source_target_pairs={{0,16},{1,9},{2,18},{3,11},{4,20},{5,13},{6,22},{7,15},{8,24},{9,1... | collective-permute-start | bytes 393224 | tf_op jit(solution)/shard_map/ppermute | solution.py:250
  9.7 6.6 %collective-permute-start.6 = (bf16[512,256]{1,0:T(8,128)(2,1)}, bf16[512,256]{1,0:T(8,128)(2,1)S(1)}, u32[]{:S(2)}, u32[]{:S(2)}) collective-permute-start(bf16[512,256]{1,0:T(8,128)(2,1)} %refs_1_.1), channel_id=1, source_target_pairs={{0,16},{1,9},{2,18},{3,11},{4,20},{5,13},{6,22},{7,15},{8,24},{9,1... | collective-permute-start | bytes 786440 | tf_op jit(solution)/shard_map/ppermute | solution.py:250
  10.3 8.8 %collective-permute-start.1 = (bf16[512,256]{1,0:T(8,128)(2,1)S(1)}, bf16[512,256]{1,0:T(8,128)(2,1)S(1)}, u32[]{:S(2)}, u32[]{:S(2)}) collective-permute-start(bf16[512,256]{1,0:T(8,128)(2,1)S(1)} %collective-permute-done.first), channel_id=1, source_target_pairs={{0,16},{1,9},{2,18},{3,11},{4,20},{5,13},{6,22},{7,15},{8,24},{9,1... | collective-permute-start | bytes 786440 | tf_op jit(solution)/shard_map/ppermute | solution.py:250
  12.7 1.6 %collective-permute-start.4 = (bf16[256,256]{1,0:T(8,128)(2,1)S(1)}, bf16[256,256]{1,0:T(8,128)(2,1)S(1)}, u32[]{:S(2)}, u32[]{:S(2)}) collective-permute-start(bf16[256,256]{1,0:T(8,128)(2,1)S(1)} %collective-permute-done.3.far), channel_id=1, source_target_pairs={{0,1},{1,0},{2,3},{3,2},{4,5},{5,4},{6,7},{7,6},{8,9},{9,8},{10,11... | collective-permute-start | bytes 393224 | tf_op jit(solution)/shard_map/ppermute | solution.py:40
  20.3 1.2 %collective-permute-start.7 = (f32[1,2048]{1,0:T(1,128)S(1)}, f32[1,2048]{1,0:T(1,128)S(1)}, u32[]{:S(2)}, u32[]{:S(2)}) collective-permute-start(f32[1,2048]{1,0:T(1,128)S(1)} %get-tuple-element.44), channel_id=1, source_target_pairs={{0,1},{1,0},{2,3},{3,2},{4,5},{5,4},{6,7},{7,6},{8,9},{9,8},{10,11... | collective-permute-start | bytes 24584 | tf_op jit(solution)/shard_map/ppermute | solution.py:40
  21.5 5.5 %collective-permute-start.8 = (f32[1,2048]{1,0:T(1,128)S(1)}, f32[1,2048]{1,0:T(1,128)S(1)}, u32[]{:S(2)}, u32[]{:S(2)}) collective-permute-start(f32[1,2048]{1,0:T(1,128)S(1)} %add.45), channel_id=1, source_target_pairs={{0,6},{1,7},{2,4},{3,5},{4,2},{5,3},{6,0},{7,1},{8,14},{9,15},{10,... | collective-permute-start | bytes 24584 | tf_op jit(solution)/shard_map/ppermute | solution.py:36
  25.2 4.5 %collective-permute-start.9 = (f32[1,2048]{1,0:T(1,128)S(1)}, f32[1,2048]{1,0:T(1,128)S(1)}, u32[]{:S(2)}, u32[]{:S(2)}) collective-permute-start(f32[1,2048]{1,0:T(1,128)S(1)} %add.45), channel_id=1, source_target_pairs={{0,4},{1,5},{2,6},{3,7},{4,0},{5,1},{6,2},{7,3},{8,12},{9,13},{10,... | collective-permute-start | bytes 24584 | tf_op jit(solution)/shard_map/ppermute | solution.py:36
  25.2 4.6 %collective-permute-start.10 = (f32[1,2048]{1,0:T(1,128)S(1)}, f32[1,2048]{1,0:T(1,128)S(1)}, u32[]{:S(2)}, u32[]{:S(2)}) collective-permute-start(f32[1,2048]{1,0:T(1,128)S(1)} %add.45), channel_id=1, source_target_pairs={{0,2},{1,3},{2,0},{3,1},{4,6},{5,7},{6,4},{7,5},{8,10},{9,11},{10,... | collective-permute-start | bytes 24584 | tf_op jit(solution)/shard_map/ppermute | solution.py:36
  32.0 1.2 %collective-permute-start.11 = (f32[1,2048]{1,0:T(1,128)S(1)}, f32[1,2048]{1,0:T(1,128)S(1)}, u32[]{:S(2)}, u32[]{:S(2)}) collective-permute-start(f32[1,2048]{1,0:T(1,128)S(1)} %shard_map.33), channel_id=1, source_target_pairs={{0,1},{1,0},{2,3},{3,2},{4,5},{5,4},{6,7},{7,6},{8,9},{9,8},{10,11... | collective-permute-start | bytes 24584 | tf_op jit(solution)/shard_map/ppermute | solution.py:40
  33.3 5.6 %collective-permute-start.12 = (f32[1,2048]{1,0:T(1,128)S(1)}, f32[1,2048]{1,0:T(1,128)S(1)}, u32[]{:S(2)}, u32[]{:S(2)}) collective-permute-start(f32[1,2048]{1,0:T(1,128)S(1)} %add.49), channel_id=1, source_target_pairs={{0,6},{1,7},{2,4},{3,5},{4,2},{5,3},{6,0},{7,1},{8,14},{9,15},{10,... | collective-permute-start | bytes 24584 | tf_op jit(solution)/shard_map/ppermute | solution.py:36
  34.8 4.5 %collective-permute-start.13 = (f32[1,2048]{1,0:T(1,128)S(1)}, f32[1,2048]{1,0:T(1,128)S(1)}, u32[]{:S(2)}, u32[]{:S(2)}) collective-permute-start(f32[1,2048]{1,0:T(1,128)S(1)} %add.49), channel_id=1, source_target_pairs={{0,4},{1,5},{2,6},{3,7},{4,0},{5,1},{6,2},{7,3},{8,12},{9,13},{10,... | collective-permute-start | bytes 24584 | tf_op jit(solution)/shard_map/ppermute | solution.py:36
  35.4 4.0 %collective-permute-start.14 = (f32[1,2048]{1,0:T(1,128)S(1)}, f32[1,2048]{1,0:T(1,128)S(1)}, u32[]{:S(2)}, u32[]{:S(2)}) collective-permute-start(f32[1,2048]{1,0:T(1,128)S(1)} %add.49), channel_id=1, source_target_pairs={{0,2},{1,3},{2,0},{3,1},{4,6},{5,7},{6,4},{7,5},{8,10},{9,11},{10,... | collective-permute-start | bytes 24584 | tf_op jit(solution)/shard_map/ppermute | solution.py:36
  40.9 1.2 %collective-permute-start.15 = (f32[1,512]{1,0:T(1,128)S(1)}, f32[1,512]{1,0:T(1,128)S(1)}, u32[]{:S(2)}, u32[]{:S(2)}) collective-permute-start(f32[1,512]{1,0:T(1,128)S(1)} %get-tuple-element.46), channel_id=1, source_target_pairs={{0,1},{1,0},{2,3},{3,2},{4,5},{5,4},{6,7},{7,6},{8,9},{9,8},{10,11... | collective-permute-start | bytes 6152 | tf_op jit(solution)/shard_map/ppermute | solution.py:40
  42.1 5.4 %collective-permute-start.16 = (f32[1,512]{1,0:T(1,128)S(1)}, f32[1,512]{1,0:T(1,128)S(1)}, u32[]{:S(2)}, u32[]{:S(2)}) collective-permute-start(f32[1,512]{1,0:T(1,128)S(1)} %add.53), channel_id=1, source_target_pairs={{0,6},{1,7},{2,4},{3,5},{4,2},{5,3},{6,0},{7,1},{8,14},{9,15},{10,... | collective-permute-start | bytes 6152 | tf_op jit(solution)/shard_map/ppermute | solution.py:36
  44.6 4.5 %collective-permute-start.17 = (f32[1,512]{1,0:T(1,128)S(1)}, f32[1,512]{1,0:T(1,128)S(1)}, u32[]{:S(2)}, u32[]{:S(2)}) collective-permute-start(f32[1,512]{1,0:T(1,128)S(1)} %add.53), channel_id=1, source_target_pairs={{0,4},{1,5},{2,6},{3,7},{4,0},{5,1},{6,2},{7,3},{8,12},{9,13},{10,... | collective-permute-start | bytes 6152 | tf_op jit(solution)/shard_map/ppermute | solution.py:36
  45.5 3.6 %collective-permute-start.18 = (f32[1,512]{1,0:T(1,128)S(1)}, f32[1,512]{1,0:T(1,128)S(1)}, u32[]{:S(2)}, u32[]{:S(2)}) collective-permute-start(f32[1,512]{1,0:T(1,128)S(1)} %add.53), channel_id=1, source_target_pairs={{0,2},{1,3},{2,0},{3,1},{4,6},{5,7},{6,4},{7,5},{8,10},{9,11},{10,... | collective-permute-start | bytes 6152 | tf_op jit(solution)/shard_map/ppermute | solution.py:36

commit v5 on v4

--- a/solution.py
+++ b/solution.py
@@ -122,10 +122,13 @@
     return jnp.broadcast_to(1.0 / jnp.sum(lane_sums, axis=1, keepdims=True), lane_sums.shape)
 
 
-def unit_kernel(*refs):
-    half = len(refs) // 2
-    for raw, unit in zip(refs[:half], refs[half:]):
-        unit[...] = unit_rows(raw[...])
+def unit_kernel(feats, protos, unit_feat, unit_proto, raw, sems):
+    copies = [pltpu.make_async_copy(src, raw.at[i], sems.at[i]) for i, src in enumerate((feats, protos))]
+    for copy in copies:
+        copy.start()
+    for index, unit in enumerate((unit_feat, unit_proto)):
+        copies[index].wait()
+        unit[...] = unit_rows(raw[index])
 
 
 def near_kernel(own_feat, near, near_swapped, own_proto, first, unit_feat, unit_proto, weights, sums):
@@ -135,7 +138,7 @@
     unit_feat[pl.ds(pl.multiple_of((1 + core) * block, block), block), :] = unit_rows(near[...])
     unit_feat[pl.ds(pl.multiple_of((2 - core) * block, block), block), :] = unit_rows(near_swapped[...])
     unit_proto[:block, :] = own_proto[...]
-    unit_proto[block : 2 * block, :] = unit_rows(first[...])
+    unit_proto[block : 2 * block, :] = first[...]
 
     def body(index, carry):
         rows = pl.ds(pl.multiple_of(index * block, block), block)
@@ -163,12 +166,11 @@
     lax.fori_loop(0, 2, body, 0)
 
 
-def more_kernel(index, raw, unit_feat, proto_in, weights_in, part_in, unit_proto, weights, part, *row_sums):
-    block = raw.shape[0]
-    rows = slice(index * block, (index + 1) * block)
-    unit_proto[rows, :] = unit_rows(raw[...])
-    total = jnp.zeros((block, LANES), F32)
-    total = fill(weights, total, rows, slice(0, 4 * block), unit_proto[rows, :], unit_feat)
+def more_kernel(start, ready,  unit_feat, proto_in, weights_in, part_in, unit_proto, weights, part, *row_sums):
+    rows = slice(start, start + ready.shape[0])
+    unit_proto[rows, :] = ready[...]
+    total = jnp.zeros((ready.shape[0], LANES), F32)
+    total = fill(weights, total, rows, slice(0, weights.shape[1]), unit_proto[rows, :], unit_feat)
     add_images(part, weights, rows, spread(total))
     for store in row_sums:
         store[...] = flat(part)
@@ -264,21 +266,30 @@
 
     half = block // 2
     core = lax.axis_index("proto") % 2
-    own_feat, own_proto = call(unit_kernel, [((block, depth), bf16)] * 2, [features, prototypes], 4)
+    own_feat, own_proto = pl.pallas_call(
+        unit_kernel,
+        out_shape=[VMEM((block, depth), bf16)] * 2,
+        in_specs=[pl.BlockSpec(memory_space=pltpu.HBM)] * 2,
+        out_specs=[IN_VMEM] * 2,
+        scratch_shapes=[VMEM((2, block, depth), bf16), pltpu.SemaphoreType.DMA((2,))],
+        compiler_params=pltpu.CompilerParams(vmem_limit_bytes=4 * 2**20),
+        cost_estimate=pl.CostEstimate(flops=1, bytes_accessed=1, transcendentals=1),
+    )(*[pltpu.with_memory_space_constraint(arg, pltpu.HBM) for arg in (features, prototypes)])
     near = send(features, (1, 2))
-    first = send(prototypes, (1, 2))
-    later, own_proto = lax.optimization_barrier((prototypes, own_proto))
-    second = send(later, (2, 1))
+    first = send(own_proto, (1, 2))
+    second = send(own_proto, (2, 1))
     near_half = lax.dynamic_slice_in_dim(near, (1 - core) * half, half, 0)
     forward, own_feat, own_proto = lax.optimization_barrier((near_half, own_feat, own_proto))
     far = send(forward, (2, 1))
-    last = send(first, (2, 1))
+    cut = 3 * block // 4
+    last = [send(first[:cut], (2, 1)), send(first[cut:], (2, 1))]
     unit_feat, unit_proto, weights, sums = call(
         near_kernel,
         [feat_shape, feat_shape, weights_shape, lanes_shape],
         [own_feat, near, swap_cores(near), own_proto, first],
         16,
     )
+    far, sums = lax.optimization_barrier((far, sums))
     unit_feat, weights, part = call(
         far_kernel,
         [feat_shape, weights_shape, part_shape],
@@ -287,19 +298,24 @@
         aliases={4: 0, 5: 1},
     )
     outs = [feat_shape, weights_shape, part_shape, ((1, images), F32)]
-    for index, raw in ((2, second), (3, last)):
+    start = 2 * block
+    for piece in (second, *last):
+        end = start + piece.shape[0]
         unit_proto, weights, part, *row_sums = call(
-            functools.partial(more_kernel, index),
-            outs if index == 3 else outs[:3],
-            [raw, unit_feat, unit_proto, weights, part],
+            functools.partial(more_kernel, start),
+            outs if end == images else outs[:3],
+            [piece, unit_feat, unit_proto, weights, part],
             16,
             aliases={2: 0, 3: 1, 4: 2},
         )
+        start = end
 
     def around(value):
         total = value + swap_cores(value)
-        for other in reversed(from_others(total, "proto", 2, z_count)):
-            total = lax.optimization_barrier(total + other)
+        others = from_others(total, "proto", 2, z_count)
+        order = (2, 1, 3) if value.shape[1] < images else (3, 2, 1)
+        for k in order:
+            total = lax.optimization_barrier(total + others[k - 1])
         return [total]
 
     parts = around(*row_sums)

time: 51 us -> 50.4 us (0.988)
  local copies, waits for them, and re-layouts: 1.91 us -> 0.03 us
  Pallas kernels: 11.7 us -> 13.1 us
  waiting for transfers between devices: 16.2 us -> 15.4 us
  starting transfers between devices: 20.8 us -> 21.4 us
    unnamed x4 -> x0, local copies, waits for them, and re-layouts: 1.9 us -> none
    pallas_call x0 -> x1, Pallas kernels: none -> 1.31 us  [whole_plan(): pl.pallas_call(unit_kernel, out_shape=[VMEM((block, depth), bf16)] * 2, i...]
    ppermute x5 -> x6, waiting for transfers between devices: 5.46 us -> 4.29 us  [send(): return lax.ppermute(value, ('batch', 'proto'), by_core(steps))]
    ppermute x5 -> x6, starting transfers between devices: 7.22 us -> 7.54 us  [send(): return lax.ppermute(value, ('batch', 'proto'), by_core(steps))]
  transfers between devices with their start and end apart: 19 -> 20, of which waited for: 15 -> 13; matrix products, arithmetic and copies ran while one was open for 0% -> 0% of each run, Pallas kernels for 10% -> 14%
where the time goes in v5:
time: 50.4 us; the launch traced here: 50.2 us
  starting transfers between devices  21.4 us (42%)
  waiting for transfers between devices  15.4 us (31%)
  Pallas kernels  13.1 us (26%)
    ppermute x9, starting transfers between devices, from_others(): lax.ppermute(value, axis, partners(size, stride, count, step))  13.3 us
    pallas_call x8, Pallas kernels, call(): pl.pallas_call(kernel, out_shape=[VMEM(shape, dtype) for shape, dtype in...  10.1 us
    ppermute x6, starting transfers between devices, send(): return lax.ppermute(value, ('batch', 'proto'), by_core(steps))  7.54 us
    ppermute x9, waiting for transfers between devices, from_others(): lax.ppermute(value, axis, partners(size, stride, count, step))  7.22 us
    ppermute x6, waiting for transfers between devices, send(): return lax.ppermute(value, ('batch', 'proto'), by_core(steps))  4.29 us
    ppermute x5, waiting for transfers between devices, swap_cores(): lax.ppermute(value, 'proto', partners(lax.axis_size('proto'), 1, 2, 1))  3.92 us
    pallas_call x1, Pallas kernels, whole_plan(): pl.pallas_call(functools.partial(last_kernel, len(parts), block), out_sha...  1.68 us
    pallas_call x1, Pallas kernels, whole_plan(): pl.pallas_call(unit_kernel, out_shape=[VMEM((block, depth), bf16)] * 2, i...  1.31 us
  transfers between devices with their start and end apart: 20, of which 13 were waited for; matrix products, arithmetic and copies ran while one was open for 0% of the time, Pallas kernels for 14%

profile of v5, /device:TPU:0, one launch (start us, length us, event | category | flops | bytes accessed | tf_op | source)
XLA Modules:
  0.0 50.2 jit_solution(6740934633096773693)
XLA Ops:
  0.0 2.9 %collective-permute-start.2 = (bf16[512,256]{1,0:T(8,128)(2,1)}, bf16[512,256]{1,0:T(8,128)(2,1)S(1)}, u32[]{:S(2)}, u32[]{:S(2)}) collective-permute-start(bf16[512,256]{1,0:T(8,128)(2,1)} %feats.1), channel_id=1, source_target_pairs={{0,8},{1,17},{2,10},{3,19},{4,12},{5,21},{6,14},{7,23},{8,0},{9,25... | collective-permute-start | bytes 786440 | tf_op jit(solution)/shard_map/ppermute | solution.py:252
  2.9 1.3 %shard_map.28 = (bf16[512,256]{1,0:T(8,128)(2,1)S(1)}, bf16[512,256]{1,0:T(8,128)(2,1)S(1)}) custom-call(bf16[512,256]{1,0:T(8,128)(2,1)} %feats.1, bf16[512,256]{1,0:T(8,128)(2,1)} %protos.1), custom_call_target="tpu_custom_call" | custom-call | flops 1 | bytes 1 | tf_op jit(solution)/shard_map/pallas_call | solution.py:269
  4.3 3.2 %collective-permute-done.2.near = bf16[512,256]{1,0:T(8,128)(2,1)S(1)} collective-permute-done((bf16[512,256]{1,0:T(8,128)(2,1)}, bf16[512,256]{1,0:T(8,128)(2,1)S(1)}, u32[]{:S(2)}, u32[]{:S(2)}) %collective-permute-start.2) | collective-permute-done | bytes 262176 | tf_op jit(solution)/shard_map/ppermute | solution.py:252
  7.5 2.1 %collective-permute-start.3 = (bf16[256,256]{1,0:T(8,128)(2,1)S(1)}, bf16[256,256]{1,0:T(8,128)(2,1)S(1)}, u32[]{:S(2)}, u32[]{:S(2)}) collective-permute-start(bf16[256,256]{1,0:T(8,128)(2,1)S(1)} %constant_dynamic-slice_fusion), channel_id=1, source_target_pairs={{0,16},{1,9},{2,18},{3,11},{4,20},{5,13},{6,22},{7,15},{8,24},{9,1... | collective-permute-start | bytes 393224 | tf_op jit(solution)/shard_map/ppermute | solution.py:252
  9.7 1.0 %collective-permute-done.first = bf16[512,256]{1,0:T(8,128)(2,1)S(1)} collective-permute-done((bf16[512,256]{1,0:T(8,128)(2,1)S(1)}, bf16[512,256]{1,0:T(8,128)(2,1)S(1)}, u32[]{:S(2)}, u32[]{:S(2)}) %collective-permute-start) | collective-permute-done | bytes 262176 | tf_op jit(solution)/shard_map/ppermute | solution.py:252
  10.7 1.7 %collective-permute-start.6 = (bf16[384,256]{1,0:T(8,128)(2,1)S(1)}, bf16[384,256]{1,0:T(8,128)(2,1)S(1)}, u32[]{:S(2)}, u32[]{:S(2)}) collective-permute-start(bf16[384,256]{1,0:T(8,128)(2,1)S(1)} %slice.9), channel_id=1, source_target_pairs={{0,16},{1,9},{2,18},{3,11},{4,20},{5,13},{6,22},{7,15},{8,24},{9,1... | collective-permute-start | bytes 589832 | tf_op jit(solution)/shard_map/ppermute | solution.py:252
  12.4 1.5 %shard_map.29 = (bf16[2048,256]{1,0:T(8,128)(2,1)S(1)}, bf16[2048,256]{1,0:T(8,128)(2,1)S(1)}, f32[2048,2048]{1,0:T(8,128)S(1)}, f32[2048,128]{1,0:T(8,128)S(1)}) custom-call(bf16[512,256]{1,0:T(8,128)(2,1)S(1)} %get-tuple-element.33.own_feat, bf16[512,256]{1,0:T(8,128)(2,1)S(1)} %collective-permute-done.2.near, ...), custom_call_target="tpu_custom_call" | custom-call | flops 1 | bytes 1 | tf_op jit(solution)/shard_map/pallas_call | solution.py:84
  14.1 0.6 %collective-permute-start.1 = (bf16[128,256]{1,0:T(8,128)(2,1)S(1)}, bf16[128,256]{1,0:T(8,128)(2,1)S(1)}, u32[]{:S(2)}, u32[]{:S(2)}) collective-permute-start(bf16[128,256]{1,0:T(8,128)(2,1)S(1)} %slice.8), channel_id=1, source_target_pairs={{0,16},{1,9},{2,18},{3,11},{4,20},{5,13},{6,22},{7,15},{8,24},{9,1... | collective-permute-start | bytes 196616 | tf_op jit(solution)/shard_map/ppermute | solution.py:252
  14.7 0.7 %collective-permute-done.5.far_swapped = bf16[256,256]{1,0:T(8,128)(2,1)S(1)} collective-permute-done((bf16[256,256]{1,0:T(8,128)(2,1)S(1)}, bf16[256,256]{1,0:T(8,128)(2,1)S(1)}, u32[]{:S(2)}, u32[]{:S(2)}) %collective-permute-start.5) | collective-permute-done | bytes 131104 | tf_op jit(solution)/shard_map/ppermute | solution.py:40
  15.4 1.4 %shard_map.30 = (bf16[2048,256]{1,0:T(8,128)(2,1)S(1)}, f32[2048,2048]{1,0:T(8,128)S(1)}, f32[8,2048]{1,0:T(8,128)S(1)}) custom-call(bf16[256,256]{1,0:T(8,128)(2,1)S(1)} %collective-permute-done.3.far, bf16[256,256]{1,0:T(8,128)(2,1)S(1)} %collective-permute-done.5.far_swapped, ...), custom_call_target="tpu_custom_call", output_to_operand_aliasing={{0}: (4, {}), {1}: (5, {})} | custom-call | flops 1 | bytes 1 | tf_op jit(solution)/shard_map/pallas_call | solution.py:84
  16.8 1.1 %shard_map.31 = (bf16[2048,256]{1,0:T(8,128)(2,1)S(1)}, f32[2048,2048]{1,0:T(8,128)S(1)}, f32[8,2048]{1,0:T(8,128)S(1)}) custom-call(bf16[512,256]{1,0:T(8,128)(2,1)S(1)} %collective-permute-done.7.ready, bf16[2048,256]{1,0:T(8,128)(2,1)S(1)} %get-tuple-element.41.unit_feat, ...), custom_call_target="tpu_custom_call", output_to_operand_aliasing={{0}: (2, {}), {1}: (3, {}), {2}: (4, {})} | custom-call | flops 1 | bytes 1 | tf_op jit(solution)/shard_map/pallas_call | solution.py:84
  18.1 0.9 %shard_map.32 = (bf16[2048,256]{1,0:T(8,128)(2,1)S(1)}, f32[2048,2048]{1,0:T(8,128)S(1)}, f32[8,2048]{1,0:T(8,128)S(1)}) custom-call(bf16[384,256]{1,0:T(8,128)(2,1)S(1)} %collective-permute-done.6.ready, bf16[2048,256]{1,0:T(8,128)(2,1)S(1)} %get-tuple-element.41.unit_feat, ...), custom_call_target="tpu_custom_call", output_to_operand_aliasing={{0}: (2, {}), {1}: (3, {}), {2}: (4, {})} | custom-call | flops 1 | bytes 1 | tf_op jit(solution)/shard_map/pallas_call | solution.py:84
  19.0 0.6 %shard_map.33 = (bf16[2048,256]{1,0:T(8,128)(2,1)S(1)}, f32[2048,2048]{1,0:T(8,128)S(1)}, f32[8,2048]{1,0:T(8,128)S(1)}, f32[1,2048]{1,0:T(1,128)S(1)}) custom-call(bf16[128,256]{1,0:T(8,128)(2,1)S(1)} %collective-permute-done.1.ready, bf16[2048,256]{1,0:T(8,128)(2,1)S(1)} %get-tuple-element.41.unit_feat, ...), custom_call_target="tpu_custom_call", output_to_operand_aliasing={{0}: (2, {}), {1}: (3, {}), {2}: (4, {})} | custom-call | flops 1 | bytes 1 | tf_op jit(solution)/shard_map/pallas_call | solution.py:84
  20.0 0.9 %collective-permute-done.8 = f32[1,2048]{1,0:T(1,128)S(1)} collective-permute-done((f32[1,2048]{1,0:T(1,128)S(1)}, f32[1,2048]{1,0:T(1,128)S(1)}, u32[]{:S(2)}, u32[]{:S(2)}) %collective-permute-start.8) | collective-permute-done | bytes 8224 | tf_op jit(solution)/shard_map/ppermute | solution.py:40
  20.9 3.7 %collective-permute-start.9 = (f32[1,2048]{1,0:T(1,128)S(1)}, f32[1,2048]{1,0:T(1,128)S(1)}, u32[]{:S(2)}, u32[]{:S(2)}) collective-permute-start(f32[1,2048]{1,0:T(1,128)S(1)} %add.45), channel_id=1, source_target_pairs={{0,6},{1,7},{2,4},{3,5},{4,2},{5,3},{6,0},{7,1},{8,14},{9,15},{10,... | collective-permute-start | bytes 24584 | tf_op jit(solution)/shard_map/ppermute | solution.py:36
  24.6 0.8 %collective-permute-start.11 = (f32[1,2048]{1,0:T(1,128)S(1)}, f32[1,2048]{1,0:T(1,128)S(1)}, u32[]{:S(2)}, u32[]{:S(2)}) collective-permute-start(f32[1,2048]{1,0:T(1,128)S(1)} %add.45), channel_id=1, source_target_pairs={{0,2},{1,3},{2,0},{3,1},{4,6},{5,7},{6,4},{7,5},{8,10},{9,11},{10,... | collective-permute-start | bytes 24584 | tf_op jit(solution)/shard_map/ppermute | solution.py:36
  25.4 1.1 %collective-permute-done.9 = f32[1,2048]{1,0:T(1,128)S(1)} collective-permute-done((f32[1,2048]{1,0:T(1,128)S(1)}, f32[1,2048]{1,0:T(1,128)S(1)}, u32[]{:S(2)}, u32[]{:S(2)}) %collective-permute-start.9) | collective-permute-done | bytes 8224 | tf_op jit(solution)/shard_map/ppermute | solution.py:36
  26.4 2.7 %collective-permute-done.10 = f32[1,2048]{1,0:T(1,128)S(1)} collective-permute-done((f32[1,2048]{1,0:T(1,128)S(1)}, f32[1,2048]{1,0:T(1,128)S(1)}, u32[]{:S(2)}, u32[]{:S(2)}) %collective-permute-start.10) | collective-permute-done | bytes 8224 | tf_op jit(solution)/shard_map/ppermute | solution.py:36
  29.2 2.2 %shard_map.34 = f32[1,2048]{1,0:T(1,128)S(1)} custom-call(f32[1,2048]{1,0:T(1,128)S(1)} %add.48.refs_0_, f32[2048,2048]{1,0:T(8,128)S(1)} %get-tuple-element.51.refs_1_), custom_call_target="tpu_custom_call" | custom-call | flops 16777216 | bytes 1 | tf_op jit(solution)/shard_map/pallas_call | solution.py:84
  31.5 1.2 %collective-permute-done.12 = f32[1,2048]{1,0:T(1,128)S(1)} collective-permute-done((f32[1,2048]{1,0:T(1,128)S(1)}, f32[1,2048]{1,0:T(1,128)S(1)}, u32[]{:S(2)}, u32[]{:S(2)}) %collective-permute-start.12) | collective-permute-done | bytes 8224 | tf_op jit(solution)/shard_map/ppermute | solution.py:40
  32.7 1.5 %collective-permute-start.13 = (f32[1,2048]{1,0:T(1,128)S(1)}, f32[1,2048]{1,0:T(1,128)S(1)}, u32[]{:S(2)}, u32[]{:S(2)}) collective-permute-start(f32[1,2048]{1,0:T(1,128)S(1)} %add.49), channel_id=1, source_target_pairs={{0,6},{1,7},{2,4},{3,5},{4,2},{5,3},{6,0},{7,1},{8,14},{9,15},{10,... | collective-permute-start | bytes 24584 | tf_op jit(solution)/shard_map/ppermute | solution.py:36
  34.2 0.6 %collective-permute-start.14 = (f32[1,2048]{1,0:T(1,128)S(1)}, f32[1,2048]{1,0:T(1,128)S(1)}, u32[]{:S(2)}, u32[]{:S(2)}) collective-permute-start(f32[1,2048]{1,0:T(1,128)S(1)} %add.49), channel_id=1, source_target_pairs={{0,4},{1,5},{2,6},{3,7},{4,0},{5,1},{6,2},{7,3},{8,12},{9,13},{10,... | collective-permute-start | bytes 24584 | tf_op jit(solution)/shard_map/ppermute | solution.py:36
  34.8 2.3 %collective-permute-start.15 = (f32[1,2048]{1,0:T(1,128)S(1)}, f32[1,2048]{1,0:T(1,128)S(1)}, u32[]{:S(2)}, u32[]{:S(2)}) collective-permute-start(f32[1,2048]{1,0:T(1,128)S(1)} %add.49), channel_id=1, source_target_pairs={{0,2},{1,3},{2,0},{3,1},{4,6},{5,7},{6,4},{7,5},{8,10},{9,11},{10,... | collective-permute-start | bytes 24584 | tf_op jit(solution)/shard_map/ppermute | solution.py:36
  37.1 1.1 %collective-permute-done.13 = f32[1,2048]{1,0:T(1,128)S(1)} collective-permute-done((f32[1,2048]{1,0:T(1,128)S(1)}, f32[1,2048]{1,0:T(1,128)S(1)}, u32[]{:S(2)}, u32[]{:S(2)}) %collective-permute-start.13) | collective-permute-done | bytes 8224 | tf_op jit(solution)/shard_map/ppermute | solution.py:36
  38.3 0.5 collective-permute-done.14
  38.8 1.4 %shard_map.35 = (f32[1,512]{1,0:T(1,128)S(1)}, f32[2048,128]{1,0:T(8,128)S(1)}) custom-call(f32[1,2048]{1,0:T(1,128)S(1)} %add.52.refs_0_, f32[2048,2048]{1,0:T(8,128)S(1)} %get-tuple-element.51.refs_1_), custom_call_target="tpu_custom_call" | custom-call | flops 16777216 | bytes 1 | tf_op jit(solution)/shard_map/pallas_call | solution.py:84
  40.4 1.1 %collective-permute-done.16 = f32[1,512]{1,0:T(1,128)S(1)} collective-permute-done((f32[1,512]{1,0:T(1,128)S(1)}, f32[1,512]{1,0:T(1,128)S(1)}, u32[]{:S(2)}, u32[]{:S(2)}) %collective-permute-start.16) | collective-permute-done | bytes 2080 | tf_op jit(solution)/shard_map/ppermute | solution.py:40
  41.5 2.5 %collective-permute-start.19 = (f32[1,512]{1,0:T(1,128)S(1)}, f32[1,512]{1,0:T(1,128)S(1)}, u32[]{:S(2)}, u32[]{:S(2)}) collective-permute-start(f32[1,512]{1,0:T(1,128)S(1)} %add.53), channel_id=1, source_target_pairs={{0,6},{1,7},{2,4},{3,5},{4,2},{5,3},{6,0},{7,1},{8,14},{9,15},{10,... | collective-permute-start | bytes 6152 | tf_op jit(solution)/shard_map/ppermute | solution.py:36
  44.0 1.9 %collective-permute-start.17 = (f32[1,512]{1,0:T(1,128)S(1)}, f32[1,512]{1,0:T(1,128)S(1)}, u32[]{:S(2)}, u32[]{:S(2)}) collective-permute-start(f32[1,512]{1,0:T(1,128)S(1)} %add.53), channel_id=1, source_target_pairs={{0,4},{1,5},{2,6},{3,7},{4,0},{5,1},{6,2},{7,3},{8,12},{9,13},{10,... | collective-permute-start | bytes 6152 | tf_op jit(solution)/shard_map/ppermute | solution.py:36
  45.9 0.8 %shard_map.36.refs_1_ = f32[512,2048]{1,0:T(8,128)S(1)} custom-call(bf16[2048,256]{1,0:T(8,128)(2,1)S(1)} %get-tuple-element.41.unit_feat, bf16[2048,256]{1,0:T(8,128)(2,1)S(1)} %get-tuple-element.53.unit_proto, f32[2048,128]{1,0:T(8,128)S(1)} %get-tuple-element.54.col_factor), custom_call_target="tpu_custom_call" | custom-call | flops 536870912 | bytes 1 | tf_op jit(solution)/shard_map/pallas_call | solution.py:84
  46.7 1.8 %collective-permute-done.17 = f32[1,512]{1,0:T(1,128)S(1)} collective-permute-done((f32[1,512]{1,0:T(1,128)S(1)}, f32[1,512]{1,0:T(1,128)S(1)}, u32[]{:S(2)}, u32[]{:S(2)}) %collective-permute-start.17) | collective-permute-done | bytes 2080 | tf_op jit(solution)/shard_map/ppermute | solution.py:36
  48.5 1.7 %shard_map.37 = bf16[512,2048]{1,0:T(8,128)(2,1)} custom-call(f32[1,512]{1,0:T(1,128)S(1)} %add.56.refs_0_, f32[512,2048]{1,0:T(8,128)S(1)} %shard_map.36.refs_1_), custom_call_target="tpu_custom_call" | custom-call | tf_op jit(solution)/shard_map/pallas_call | solution.py:342
  (33 shorter events, 1.1 us)
Async XLA Ops:
  0.0 7.5 %collective-permute-start.2 = (bf16[512,256]{1,0:T(8,128)(2,1)}, bf16[512,256]{1,0:T(8,128)(2,1)S(1)}, u32[]{:S(2)}, u32[]{:S(2)}) collective-permute-start(bf16[512,256]{1,0:T(8,128)(2,1)} %feats.1), channel_id=1, source_target_pairs={{0,8},{1,17},{2,10},{3,19},{4,12},{5,21},{6,14},{7,23},{8,0},{9,25... | collective-permute-start | bytes 786440 | tf_op jit(solution)/shard_map/ppermute | solution.py:252
  4.3 6.4 %collective-permute-start = (bf16[512,256]{1,0:T(8,128)(2,1)S(1)}, bf16[512,256]{1,0:T(8,128)(2,1)S(1)}, u32[]{:S(2)}, u32[]{:S(2)}) collective-permute-start(bf16[512,256]{1,0:T(8,128)(2,1)S(1)} %get-tuple-element.34.own_proto), channel_id=1, source_target_pairs={{0,8},{1,17},{2,10},{3,19},{4,12},{5,21},{6,14},{7,23},{8,0},{9,25... | collective-permute-start | bytes 786440 | tf_op jit(solution)/shard_map/ppermute | solution.py:252
  7.5 4.9 %collective-permute-start.4 = (bf16[512,256]{1,0:T(8,128)(2,1)S(1)}, bf16[512,256]{1,0:T(8,128)(2,1)S(1)}, u32[]{:S(2)}, u32[]{:S(2)}) collective-permute-start(bf16[512,256]{1,0:T(8,128)(2,1)S(1)} %collective-permute-done.2.near), channel_id=1, source_target_pairs={{0,1},{1,0},{2,3},{3,2},{4,5},{5,4},{6,7},{7,6},{8,9},{9,8},{10,11... | collective-permute-start | bytes 786440 | tf_op jit(solution)/shard_map/ppermute | solution.py:40
  7.5 6.5 %collective-permute-start.3 = (bf16[256,256]{1,0:T(8,128)(2,1)S(1)}, bf16[256,256]{1,0:T(8,128)(2,1)S(1)}, u32[]{:S(2)}, u32[]{:S(2)}) collective-permute-start(bf16[256,256]{1,0:T(8,128)(2,1)S(1)} %constant_dynamic-slice_fusion), channel_id=1, source_target_pairs={{0,16},{1,9},{2,18},{3,11},{4,20},{5,13},{6,22},{7,15},{8,24},{9,1... | collective-permute-start | bytes 393224 | tf_op jit(solution)/shard_map/ppermute | solution.py:252
  9.6 7.2 %collective-permute-start.7 = (bf16[512,256]{1,0:T(8,128)(2,1)S(1)}, bf16[512,256]{1,0:T(8,128)(2,1)S(1)}, u32[]{:S(2)}, u32[]{:S(2)}) collective-permute-start(bf16[512,256]{1,0:T(8,128)(2,1)S(1)} %get-tuple-element.34.own_proto), channel_id=1, source_target_pairs={{0,16},{1,9},{2,18},{3,11},{4,20},{5,13},{6,22},{7,15},{8,24},{9,1... | collective-permute-start | bytes 786440 | tf_op jit(solution)/shard_map/ppermute | solution.py:252
  10.7 7.4 %collective-permute-start.6 = (bf16[384,256]{1,0:T(8,128)(2,1)S(1)}, bf16[384,256]{1,0:T(8,128)(2,1)S(1)}, u32[]{:S(2)}, u32[]{:S(2)}) collective-permute-start(bf16[384,256]{1,0:T(8,128)(2,1)S(1)} %slice.9), channel_id=1, source_target_pairs={{0,16},{1,9},{2,18},{3,11},{4,20},{5,13},{6,22},{7,15},{8,24},{9,1... | collective-permute-start | bytes 589832 | tf_op jit(solution)/shard_map/ppermute | solution.py:252
  14.0 1.4 %collective-permute-start.5 = (bf16[256,256]{1,0:T(8,128)(2,1)S(1)}, bf16[256,256]{1,0:T(8,128)(2,1)S(1)}, u32[]{:S(2)}, u32[]{:S(2)}) collective-permute-start(bf16[256,256]{1,0:T(8,128)(2,1)S(1)} %collective-permute-done.3.far), channel_id=1, source_target_pairs={{0,1},{1,0},{2,3},{3,2},{4,5},{5,4},{6,7},{7,6},{8,9},{9,8},{10,11... | collective-permute-start | bytes 393224 | tf_op jit(solution)/shard_map/ppermute | solution.py:40
  14.1 4.9 %collective-permute-start.1 = (bf16[128,256]{1,0:T(8,128)(2,1)S(1)}, bf16[128,256]{1,0:T(8,128)(2,1)S(1)}, u32[]{:S(2)}, u32[]{:S(2)}) collective-permute-start(bf16[128,256]{1,0:T(8,128)(2,1)S(1)} %slice.8), channel_id=1, source_target_pairs={{0,16},{1,9},{2,18},{3,11},{4,20},{5,13},{6,22},{7,15},{8,24},{9,1... | collective-permute-start | bytes 196616 | tf_op jit(solution)/shard_map/ppermute | solution.py:252
  19.7 1.2 %collective-permute-start.8 = (f32[1,2048]{1,0:T(1,128)S(1)}, f32[1,2048]{1,0:T(1,128)S(1)}, u32[]{:S(2)}, u32[]{:S(2)}) collective-permute-start(f32[1,2048]{1,0:T(1,128)S(1)} %get-tuple-element.50), channel_id=1, source_target_pairs={{0,1},{1,0},{2,3},{3,2},{4,5},{5,4},{6,7},{7,6},{8,9},{9,8},{10,11... | collective-permute-start | bytes 24584 | tf_op jit(solution)/shard_map/ppermute | solution.py:40
  20.9 5.5 %collective-permute-start.9 = (f32[1,2048]{1,0:T(1,128)S(1)}, f32[1,2048]{1,0:T(1,128)S(1)}, u32[]{:S(2)}, u32[]{:S(2)}) collective-permute-start(f32[1,2048]{1,0:T(1,128)S(1)} %add.45), channel_id=1, source_target_pairs={{0,6},{1,7},{2,4},{3,5},{4,2},{5,3},{6,0},{7,1},{8,14},{9,15},{10,... | collective-permute-start | bytes 24584 | tf_op jit(solution)/shard_map/ppermute | solution.py:36
  24.6 4.5 %collective-permute-start.10 = (f32[1,2048]{1,0:T(1,128)S(1)}, f32[1,2048]{1,0:T(1,128)S(1)}, u32[]{:S(2)}, u32[]{:S(2)}) collective-permute-start(f32[1,2048]{1,0:T(1,128)S(1)} %add.45), channel_id=1, source_target_pairs={{0,4},{1,5},{2,6},{3,7},{4,0},{5,1},{6,2},{7,3},{8,12},{9,13},{10,... | collective-permute-start | bytes 24584 | tf_op jit(solution)/shard_map/ppermute | solution.py:36
  24.6 4.6 %collective-permute-start.11 = (f32[1,2048]{1,0:T(1,128)S(1)}, f32[1,2048]{1,0:T(1,128)S(1)}, u32[]{:S(2)}, u32[]{:S(2)}) collective-permute-start(f32[1,2048]{1,0:T(1,128)S(1)} %add.45), channel_id=1, source_target_pairs={{0,2},{1,3},{2,0},{3,1},{4,6},{5,7},{6,4},{7,5},{8,10},{9,11},{10,... | collective-permute-start | bytes 24584 | tf_op jit(solution)/shard_map/ppermute | solution.py:36
  31.4 1.2 %collective-permute-start.12 = (f32[1,2048]{1,0:T(1,128)S(1)}, f32[1,2048]{1,0:T(1,128)S(1)}, u32[]{:S(2)}, u32[]{:S(2)}) collective-permute-start(f32[1,2048]{1,0:T(1,128)S(1)} %shard_map.34), channel_id=1, source_target_pairs={{0,1},{1,0},{2,3},{3,2},{4,5},{5,4},{6,7},{7,6},{8,9},{9,8},{10,11... | collective-permute-start | bytes 24584 | tf_op jit(solution)/shard_map/ppermute | solution.py:40
  32.7 5.6 %collective-permute-start.13 = (f32[1,2048]{1,0:T(1,128)S(1)}, f32[1,2048]{1,0:T(1,128)S(1)}, u32[]{:S(2)}, u32[]{:S(2)}) collective-permute-start(f32[1,2048]{1,0:T(1,128)S(1)} %add.49), channel_id=1, source_target_pairs={{0,6},{1,7},{2,4},{3,5},{4,2},{5,3},{6,0},{7,1},{8,14},{9,15},{10,... | collective-permute-start | bytes 24584 | tf_op jit(solution)/shard_map/ppermute | solution.py:36
  34.2 4.5 %collective-permute-start.14 = (f32[1,2048]{1,0:T(1,128)S(1)}, f32[1,2048]{1,0:T(1,128)S(1)}, u32[]{:S(2)}, u32[]{:S(2)}) collective-permute-start(f32[1,2048]{1,0:T(1,128)S(1)} %add.49), channel_id=1, source_target_pairs={{0,4},{1,5},{2,6},{3,7},{4,0},{5,1},{6,2},{7,3},{8,12},{9,13},{10,... | collective-permute-start | bytes 24584 | tf_op jit(solution)/shard_map/ppermute | solution.py:36
  34.8 4.0 %collective-permute-start.15 = (f32[1,2048]{1,0:T(1,128)S(1)}, f32[1,2048]{1,0:T(1,128)S(1)}, u32[]{:S(2)}, u32[]{:S(2)}) collective-permute-start(f32[1,2048]{1,0:T(1,128)S(1)} %add.49), channel_id=1, source_target_pairs={{0,2},{1,3},{2,0},{3,1},{4,6},{5,7},{6,4},{7,5},{8,10},{9,11},{10,... | collective-permute-start | bytes 24584 | tf_op jit(solution)/shard_map/ppermute | solution.py:36
  40.3 1.2 %collective-permute-start.16 = (f32[1,512]{1,0:T(1,128)S(1)}, f32[1,512]{1,0:T(1,128)S(1)}, u32[]{:S(2)}, u32[]{:S(2)}) collective-permute-start(f32[1,512]{1,0:T(1,128)S(1)} %get-tuple-element.52), channel_id=1, source_target_pairs={{0,1},{1,0},{2,3},{3,2},{4,5},{5,4},{6,7},{7,6},{8,9},{9,8},{10,11... | collective-permute-start | bytes 6152 | tf_op jit(solution)/shard_map/ppermute | solution.py:40
  41.5 7.0 %collective-permute-start.19 = (f32[1,512]{1,0:T(1,128)S(1)}, f32[1,512]{1,0:T(1,128)S(1)}, u32[]{:S(2)}, u32[]{:S(2)}) collective-permute-start(f32[1,512]{1,0:T(1,128)S(1)} %add.53), channel_id=1, source_target_pairs={{0,6},{1,7},{2,4},{3,5},{4,2},{5,3},{6,0},{7,1},{8,14},{9,15},{10,... | collective-permute-start | bytes 6152 | tf_op jit(solution)/shard_map/ppermute | solution.py:36
  44.0 4.5 %collective-permute-start.18 = (f32[1,512]{1,0:T(1,128)S(1)}, f32[1,512]{1,0:T(1,128)S(1)}, u32[]{:S(2)}, u32[]{:S(2)}) collective-permute-start(f32[1,512]{1,0:T(1,128)S(1)} %add.53), channel_id=1, source_target_pairs={{0,2},{1,3},{2,0},{3,1},{4,6},{5,7},{6,4},{7,5},{8,10},{9,11},{10,... | collective-permute-start | bytes 6152 | tf_op jit(solution)/shard_map/ppermute | solution.py:36
  44.0 4.5 %collective-permute-start.17 = (f32[1,512]{1,0:T(1,128)S(1)}, f32[1,512]{1,0:T(1,128)S(1)}, u32[]{:S(2)}, u32[]{:S(2)}) collective-permute-start(f32[1,512]{1,0:T(1,128)S(1)} %add.53), channel_id=1, source_target_pairs={{0,4},{1,5},{2,6},{3,7},{4,0},{5,1},{6,2},{7,3},{8,12},{9,13},{10,... | collective-permute-start | bytes 6152 | tf_op jit(solution)/shard_map/ppermute | solution.py:36

commit v6 on v5

--- a/solution.py
+++ b/solution.py
@@ -131,22 +131,23 @@
         unit[...] = unit_rows(raw[index])
 
 
-def near_kernel(own_feat, near, near_swapped, own_proto, first, unit_feat, unit_proto, weights, sums):
+def near_kernel(own_feat, near, near_swapped, own_proto, unit_feat, unit_proto, weights, sums):
     block = own_feat.shape[0]
     core = lax.axis_index("proto") % 2
     unit_feat[:block, :] = own_feat[...]
     unit_feat[pl.ds(pl.multiple_of((1 + core) * block, block), block), :] = unit_rows(near[...])
     unit_feat[pl.ds(pl.multiple_of((2 - core) * block, block), block), :] = unit_rows(near_swapped[...])
     unit_proto[:block, :] = own_proto[...]
-    unit_proto[block : 2 * block, :] = first[...]
-
-    def body(index, carry):
-        rows = pl.ds(pl.multiple_of(index * block, block), block)
-        total = jnp.zeros((block, LANES), F32)
-        sums[rows, :] = fill(weights, total, rows, slice(0, 3 * block), unit_proto[rows, :], unit_feat)
-        return carry
-
-    lax.fori_loop(0, 2, body, 0)
+    total = jnp.zeros((block, LANES), F32)
+    sums[:block, :] = fill(weights, total, slice(0, block), slice(0, 3 * block), own_proto[...], unit_feat)
+
+
+def first_kernel(first, sums_in, unit_feat, proto_in, weights_in, sums, unit_proto, weights):
+    block = first.shape[0]
+    rows = slice(block, 2 * block)
+    unit_proto[rows, :] = first[...]
+    total = jnp.zeros((block, LANES), F32)
+    sums[rows, :] = fill(weights, total, rows, slice(0, 3 * block), first[...], unit_feat)
 
 
 def far_kernel(far, far_swapped, sums, unit_proto, feat_in, weights_in, unit_feat, weights, part):
@@ -220,20 +221,23 @@
 
 def last_kernel(count, block, *refs):
     parts, ready, out, staged, sems = refs[:count], *refs[count:]
-    total = summed(parts)
-    factors = []
-    for tile in tiles(block):
-        factors.append(jnp.transpose(jnp.broadcast_to(1.0 / total[:, tile], (LANES, LANES))))
-    factor = jnp.concatenate(factors, axis=0)
+    inverse = 1.0 / summed(parts)
     place = lax.axis_index("batch")
     core = lax.axis_index("proto") % 2
+    bases = [jnp.bitwise_xor(place, step) * block for step in (0, 1 + core, 2 - core, 3)]
+    height = block // sems.shape[0]
     copies = []
-    for index, step in enumerate((0, 1 + core, 2 - core, 3)):
-        for tile in tiles(block):
-            values = ready[:, index * block + tile.start : index * block + tile.stop]
-            staged[index, :, tile] = (values * factor).astype(staged.dtype)
-        column = pl.multiple_of(jnp.bitwise_xor(place, step) * block, block)
-        copies.append(pltpu.make_async_copy(staged.at[index], out.at[:, pl.ds(column, block)], sems.at[index]))
+    for index in range(sems.shape[0]):
+        rows = slice(index * height, (index + 1) * height)
+        group = rows.start // LANES * LANES
+        spread_rows = jnp.transpose(jnp.broadcast_to(inverse[:, group : group + LANES], (LANES, LANES)))
+        factor = spread_rows[rows.start - group : rows.stop - group]
+        for number, base in enumerate(bases):
+            for tile in tiles(block):
+                values = ready[rows, number * block + tile.start : number * block + tile.stop]
+                column = pl.multiple_of(base + tile.start, LANES)
+                staged[rows, pl.ds(column, LANES)] = (values * factor).astype(staged.dtype)
+        copies.append(pltpu.make_async_copy(staged.at[rows], out.at[rows], sems.at[index]))
         copies[-1].start()
     for copy in copies:
         copy.wait()
@@ -281,15 +285,22 @@
     near_half = lax.dynamic_slice_in_dim(near, (1 - core) * half, half, 0)
     forward, own_feat, own_proto = lax.optimization_barrier((near_half, own_feat, own_proto))
     far = send(forward, (2, 1))
-    cut = 3 * block // 4
-    last = [send(first[:cut], (2, 1)), send(first[cut:], (2, 1))]
     unit_feat, unit_proto, weights, sums = call(
         near_kernel,
         [feat_shape, feat_shape, weights_shape, lanes_shape],
-        [own_feat, near, swap_cores(near), own_proto, first],
+        [own_feat, near, swap_cores(near), own_proto],
         16,
     )
     far, sums = lax.optimization_barrier((far, sums))
+    cut = 5 * block // 8
+    last = [send(first[:cut], (2, 1)), send(first[cut:], (2, 1))]
+    sums, unit_proto, weights = call(
+        first_kernel,
+        [lanes_shape, feat_shape, weights_shape],
+        [first, sums, unit_feat, unit_proto, weights],
+        16,
+        aliases={1: 0, 3: 1, 4: 2},
+    )
     unit_feat, weights, part = call(
         far_kernel,
         [feat_shape, weights_shape, part_shape],
@@ -312,10 +323,8 @@
 
     def around(value):
         total = value + swap_cores(value)
-        others = from_others(total, "proto", 2, z_count)
-        order = (2, 1, 3) if value.shape[1] < images else (3, 2, 1)
-        for k in order:
-            total = lax.optimization_barrier(total + others[k - 1])
+        for other in reversed(from_others(total, "proto", 2, z_count)):
+            total = lax.optimization_barrier(total + other)
         return [total]
 
     parts = around(*row_sums)
@@ -344,7 +353,7 @@
         out_shape=jax.ShapeDtypeStruct((block, images), bf16),
         in_specs=[IN_VMEM] * len(pinned),
         out_specs=pl.BlockSpec(memory_space=pl.ANY),
-        scratch_shapes=[VMEM((blocks, block, block), bf16), pltpu.SemaphoreType.DMA((blocks,))],
+        scratch_shapes=[VMEM((block, images), bf16), pltpu.SemaphoreType.DMA((2 * block // LANES,))],
         compiler_params=pltpu.CompilerParams(vmem_limit_bytes=8 * 2**20),
     )(*pinned)
 

time: 50.4 us -> 50 us (level)
  starting transfers between devices: 21.4 us -> 22.1 us
  waiting for transfers between devices: 15.4 us -> 14.7 us
    ppermute x5, waiting for transfers between devices: 3.92 us -> 3.15 us  [swap_cores(): lax.ppermute(value, 'proto', partners(lax.axis_size('proto'), 1, 2, 1))]
    ppermute x6, starting transfers between devices: 7.54 us -> 8.23 us  [send(): return lax.ppermute(value, ('batch', 'proto'), by_core(steps))]
    pallas_call x8 -> x9, Pallas kernels: 10.1 us -> 9.89 us  [call(): pl.pallas_call(kernel, out_shape=[VMEM(shape, dtype) for shape, dtype in...]
where the time goes in v6:
time: 50 us; the launch traced here: 49.9 us
  starting transfers between devices  22.1 us (44%)
  waiting for transfers between devices  14.7 us (29%)
  Pallas kernels  12.7 us (25%)
    ppermute x9, starting transfers between devices, from_others(): lax.ppermute(value, axis, partners(size, stride, count, step))  13.3 us
    pallas_call x9, Pallas kernels, call(): pl.pallas_call(kernel, out_shape=[VMEM(shape, dtype) for shape, dtype in...  9.89 us
    ppermute x6, starting transfers between devices, send(): return lax.ppermute(value, ('batch', 'proto'), by_core(steps))  8.23 us
    ppermute x9, waiting for transfers between devices, from_others(): lax.ppermute(value, axis, partners(size, stride, count, step))  7.23 us
    ppermute x6, waiting for transfers between devices, send(): return lax.ppermute(value, ('batch', 'proto'), by_core(steps))  4.31 us
    ppermute x5, waiting for transfers between devices, swap_cores(): lax.ppermute(value, 'proto', partners(lax.axis_size('proto'), 1, 2, 1))  3.15 us
    pallas_call x1, Pallas kernels, whole_plan(): pl.pallas_call(functools.partial(last_kernel, len(parts), block), out_sha...  1.51 us
    pallas_call x1, Pallas kernels, whole_plan(): pl.pallas_call(unit_kernel, out_shape=[VMEM((block, depth), bf16)] * 2, i...  1.31 us
  transfers between devices with their start and end apart: 20, of which 13 were waited for; matrix products, arithmetic and copies ran while one was open for 0% of the time, Pallas kernels for 14%

profile of v6, /device:TPU:0, one launch (start us, length us, event | category | flops | bytes accessed | tf_op | source)
XLA Modules:
  0.0 49.9 jit_solution(1356903541841370298)
XLA Ops:
  0.0 2.9 %collective-permute-start.2 = (bf16[512,256]{1,0:T(8,128)(2,1)}, bf16[512,256]{1,0:T(8,128)(2,1)S(1)}, u32[]{:S(2)}, u32[]{:S(2)}) collective-permute-start(bf16[512,256]{1,0:T(8,128)(2,1)} %feats.1), channel_id=1, source_target_pairs={{0,8},{1,17},{2,10},{3,19},{4,12},{5,21},{6,14},{7,23},{8,0},{9,25... | collective-permute-start | bytes 786440 | tf_op jit(solution)/shard_map/ppermute | solution.py:256
  2.9 1.3 %shard_map.28 = (bf16[512,256]{1,0:T(8,128)(2,1)S(1)}, bf16[512,256]{1,0:T(8,128)(2,1)S(1)}) custom-call(bf16[512,256]{1,0:T(8,128)(2,1)} %feats.1, bf16[512,256]{1,0:T(8,128)(2,1)} %protos.1), custom_call_target="tpu_custom_call" | custom-call | flops 1 | bytes 1 | tf_op jit(solution)/shard_map/pallas_call | solution.py:273
  4.3 3.2 %collective-permute-done.2.near = bf16[512,256]{1,0:T(8,128)(2,1)S(1)} collective-permute-done((bf16[512,256]{1,0:T(8,128)(2,1)}, bf16[512,256]{1,0:T(8,128)(2,1)S(1)}, u32[]{:S(2)}, u32[]{:S(2)}) %collective-permute-start.2) | collective-permute-done | bytes 262176 | tf_op jit(solution)/shard_map/ppermute | solution.py:256
  7.5 2.1 %collective-permute-start.3 = (bf16[256,256]{1,0:T(8,128)(2,1)S(1)}, bf16[256,256]{1,0:T(8,128)(2,1)S(1)}, u32[]{:S(2)}, u32[]{:S(2)}) collective-permute-start(bf16[256,256]{1,0:T(8,128)(2,1)S(1)} %constant_dynamic-slice_fusion), channel_id=1, source_target_pairs={{0,16},{1,9},{2,18},{3,11},{4,20},{5,13},{6,22},{7,15},{8,24},{9,1... | collective-permute-start | bytes 393224 | tf_op jit(solution)/shard_map/ppermute | solution.py:256
  9.7 1.0 %collective-permute-done.first = bf16[512,256]{1,0:T(8,128)(2,1)S(1)} collective-permute-done((bf16[512,256]{1,0:T(8,128)(2,1)S(1)}, bf16[512,256]{1,0:T(8,128)(2,1)S(1)}, u32[]{:S(2)}, u32[]{:S(2)}) %collective-permute-start) | collective-permute-done | bytes 262176 | tf_op jit(solution)/shard_map/ppermute | solution.py:256
  10.7 1.7 %collective-permute-start.6 = (bf16[320,256]{1,0:T(8,128)(2,1)S(1)}, bf16[320,256]{1,0:T(8,128)(2,1)S(1)}, u32[]{:S(2)}, u32[]{:S(2)}) collective-permute-start(bf16[320,256]{1,0:T(8,128)(2,1)S(1)} %slice.9), channel_id=1, source_target_pairs={{0,16},{1,9},{2,18},{3,11},{4,20},{5,13},{6,22},{7,15},{8,24},{9,1... | collective-permute-start | bytes 491528 | tf_op jit(solution)/shard_map/ppermute | solution.py:256
  12.4 0.8 %shard_map.29 = (bf16[2048,256]{1,0:T(8,128)(2,1)S(1)}, bf16[2048,256]{1,0:T(8,128)(2,1)S(1)}, f32[2048,2048]{1,0:T(8,128)S(1)}, f32[2048,128]{1,0:T(8,128)S(1)}) custom-call(bf16[512,256]{1,0:T(8,128)(2,1)S(1)} %get-tuple-element.36.own_feat, bf16[512,256]{1,0:T(8,128)(2,1)S(1)} %collective-permute-done.2.near, ...), custom_call_target="tpu_custom_call" | custom-call | flops 1 | bytes 1 | tf_op jit(solution)/shard_map/pallas_call | solution.py:84
  13.4 1.3 %collective-permute-start.1 = (bf16[192,256]{1,0:T(8,128)(2,1)S(1)}, bf16[192,256]{1,0:T(8,128)(2,1)S(1)}, u32[]{:S(2)}, u32[]{:S(2)}) collective-permute-start(bf16[192,256]{1,0:T(8,128)(2,1)S(1)} %slice.8), channel_id=1, source_target_pairs={{0,16},{1,9},{2,18},{3,11},{4,20},{5,13},{6,22},{7,15},{8,24},{9,1... | collective-permute-start | bytes 294920 | tf_op jit(solution)/shard_map/ppermute | solution.py:256
  14.7 0.6 %shard_map.30 = (f32[2048,128]{1,0:T(8,128)S(1)}, bf16[2048,256]{1,0:T(8,128)(2,1)S(1)}, f32[2048,2048]{1,0:T(8,128)S(1)}) custom-call(bf16[512,256]{1,0:T(8,128)(2,1)S(1)} %collective-permute-done.first, f32[2048,128]{1,0:T(8,128)S(1)} %get-tuple-element.40.sums_in, ...), custom_call_target="tpu_custom_call", output_to_operand_aliasing={{0}: (1, {}), {1}: (3, {}), {2}: (4, {})} | custom-call | flops 1 | bytes 1 | tf_op jit(solution)/shard_map/pallas_call | solution.py:84
  15.3 1.4 %shard_map.31 = (bf16[2048,256]{1,0:T(8,128)(2,1)S(1)}, f32[2048,2048]{1,0:T(8,128)S(1)}, f32[8,2048]{1,0:T(8,128)S(1)}) custom-call(bf16[256,256]{1,0:T(8,128)(2,1)S(1)} %collective-permute-done.3.far, bf16[256,256]{1,0:T(8,128)(2,1)S(1)} %collective-permute-done.5.far_swapped, ...), custom_call_target="tpu_custom_call", output_to_operand_aliasing={{0}: (4, {}), {1}: (5, {})} | custom-call | flops 1 | bytes 1 | tf_op jit(solution)/shard_map/pallas_call | solution.py:84
  16.8 1.1 %shard_map.32 = (bf16[2048,256]{1,0:T(8,128)(2,1)S(1)}, f32[2048,2048]{1,0:T(8,128)S(1)}, f32[8,2048]{1,0:T(8,128)S(1)}) custom-call(bf16[512,256]{1,0:T(8,128)(2,1)S(1)} %collective-permute-done.7.ready, bf16[2048,256]{1,0:T(8,128)(2,1)S(1)} %get-tuple-element.47.unit_feat, ...), custom_call_target="tpu_custom_call", output_to_operand_aliasing={{0}: (2, {}), {1}: (3, {}), {2}: (4, {})} | custom-call | flops 1 | bytes 1 | tf_op jit(solution)/shard_map/pallas_call | solution.py:84
  17.9 0.7 %shard_map.33 = (bf16[2048,256]{1,0:T(8,128)(2,1)S(1)}, f32[2048,2048]{1,0:T(8,128)S(1)}, f32[8,2048]{1,0:T(8,128)S(1)}) custom-call(bf16[320,256]{1,0:T(8,128)(2,1)S(1)} %collective-permute-done.6.ready, bf16[2048,256]{1,0:T(8,128)(2,1)S(1)} %get-tuple-element.47.unit_feat, ...), custom_call_target="tpu_custom_call", output_to_operand_aliasing={{0}: (2, {}), {1}: (3, {}), {2}: (4, {})} | custom-call | flops 1 | bytes 1 | tf_op jit(solution)/shard_map/pallas_call | solution.py:84
  18.8 0.7 %shard_map.34 = (bf16[2048,256]{1,0:T(8,128)(2,1)S(1)}, f32[2048,2048]{1,0:T(8,128)S(1)}, f32[8,2048]{1,0:T(8,128)S(1)}, f32[1,2048]{1,0:T(1,128)S(1)}) custom-call(bf16[192,256]{1,0:T(8,128)(2,1)S(1)} %collective-permute-done.1.ready, bf16[2048,256]{1,0:T(8,128)(2,1)S(1)} %get-tuple-element.47.unit_feat, ...), custom_call_target="tpu_custom_call", output_to_operand_aliasing={{0}: (2, {}), {1}: (3, {}), {2}: (4, {})} | custom-call | flops 1 | bytes 1 | tf_op jit(solution)/shard_map/pallas_call | solution.py:84
  19.9 0.8 %collective-permute-done.8 = f32[1,2048]{1,0:T(1,128)S(1)} collective-permute-done((f32[1,2048]{1,0:T(1,128)S(1)}, f32[1,2048]{1,0:T(1,128)S(1)}, u32[]{:S(2)}, u32[]{:S(2)}) %collective-permute-start.8) | collective-permute-done | bytes 8224 | tf_op jit(solution)/shard_map/ppermute | solution.py:40
  20.7 3.7 %collective-permute-start.9 = (f32[1,2048]{1,0:T(1,128)S(1)}, f32[1,2048]{1,0:T(1,128)S(1)}, u32[]{:S(2)}, u32[]{:S(2)}) collective-permute-start(f32[1,2048]{1,0:T(1,128)S(1)} %add.45), channel_id=1, source_target_pairs={{0,6},{1,7},{2,4},{3,5},{4,2},{5,3},{6,0},{7,1},{8,14},{9,15},{10,... | collective-permute-start | bytes 24584 | tf_op jit(solution)/shard_map/ppermute | solution.py:36
  24.4 0.8 %collective-permute-start.11 = (f32[1,2048]{1,0:T(1,128)S(1)}, f32[1,2048]{1,0:T(1,128)S(1)}, u32[]{:S(2)}, u32[]{:S(2)}) collective-permute-start(f32[1,2048]{1,0:T(1,128)S(1)} %add.45), channel_id=1, source_target_pairs={{0,2},{1,3},{2,0},{3,1},{4,6},{5,7},{6,4},{7,5},{8,10},{9,11},{10,... | collective-permute-start | bytes 24584 | tf_op jit(solution)/shard_map/ppermute | solution.py:36
  25.2 1.1 %collective-permute-done.9 = f32[1,2048]{1,0:T(1,128)S(1)} collective-permute-done((f32[1,2048]{1,0:T(1,128)S(1)}, f32[1,2048]{1,0:T(1,128)S(1)}, u32[]{:S(2)}, u32[]{:S(2)}) %collective-permute-start.9) | collective-permute-done | bytes 8224 | tf_op jit(solution)/shard_map/ppermute | solution.py:36
  26.3 2.7 %collective-permute-done.10 = f32[1,2048]{1,0:T(1,128)S(1)} collective-permute-done((f32[1,2048]{1,0:T(1,128)S(1)}, f32[1,2048]{1,0:T(1,128)S(1)}, u32[]{:S(2)}, u32[]{:S(2)}) %collective-permute-start.10) | collective-permute-done | bytes 8224 | tf_op jit(solution)/shard_map/ppermute | solution.py:36
  29.0 2.2 %shard_map.35 = f32[1,2048]{1,0:T(1,128)S(1)} custom-call(f32[1,2048]{1,0:T(1,128)S(1)} %add.48.refs_0_, f32[2048,2048]{1,0:T(8,128)S(1)} %get-tuple-element.57.refs_1_), custom_call_target="tpu_custom_call" | custom-call | flops 16777216 | bytes 1 | tf_op jit(solution)/shard_map/pallas_call | solution.py:84
  31.3 1.2 %collective-permute-done.12 = f32[1,2048]{1,0:T(1,128)S(1)} collective-permute-done((f32[1,2048]{1,0:T(1,128)S(1)}, f32[1,2048]{1,0:T(1,128)S(1)}, u32[]{:S(2)}, u32[]{:S(2)}) %collective-permute-start.12) | collective-permute-done | bytes 8224 | tf_op jit(solution)/shard_map/ppermute | solution.py:40
  32.5 1.5 %collective-permute-start.13 = (f32[1,2048]{1,0:T(1,128)S(1)}, f32[1,2048]{1,0:T(1,128)S(1)}, u32[]{:S(2)}, u32[]{:S(2)}) collective-permute-start(f32[1,2048]{1,0:T(1,128)S(1)} %add.49), channel_id=1, source_target_pairs={{0,6},{1,7},{2,4},{3,5},{4,2},{5,3},{6,0},{7,1},{8,14},{9,15},{10,... | collective-permute-start | bytes 24584 | tf_op jit(solution)/shard_map/ppermute | solution.py:36
  34.0 0.6 %collective-permute-start.14 = (f32[1,2048]{1,0:T(1,128)S(1)}, f32[1,2048]{1,0:T(1,128)S(1)}, u32[]{:S(2)}, u32[]{:S(2)}) collective-permute-start(f32[1,2048]{1,0:T(1,128)S(1)} %add.49), channel_id=1, source_target_pairs={{0,4},{1,5},{2,6},{3,7},{4,0},{5,1},{6,2},{7,3},{8,12},{9,13},{10,... | collective-permute-start | bytes 24584 | tf_op jit(solution)/shard_map/ppermute | solution.py:36
  34.6 2.3 %collective-permute-start.15 = (f32[1,2048]{1,0:T(1,128)S(1)}, f32[1,2048]{1,0:T(1,128)S(1)}, u32[]{:S(2)}, u32[]{:S(2)}) collective-permute-start(f32[1,2048]{1,0:T(1,128)S(1)} %add.49), channel_id=1, source_target_pairs={{0,2},{1,3},{2,0},{3,1},{4,6},{5,7},{6,4},{7,5},{8,10},{9,11},{10,... | collective-permute-start | bytes 24584 | tf_op jit(solution)/shard_map/ppermute | solution.py:36
  37.0 1.1 %collective-permute-done.13 = f32[1,2048]{1,0:T(1,128)S(1)} collective-permute-done((f32[1,2048]{1,0:T(1,128)S(1)}, f32[1,2048]{1,0:T(1,128)S(1)}, u32[]{:S(2)}, u32[]{:S(2)}) %collective-permute-start.13) | collective-permute-done | bytes 8224 | tf_op jit(solution)/shard_map/ppermute | solution.py:36
  38.7 1.4 %shard_map.36 = (f32[1,512]{1,0:T(1,128)S(1)}, f32[2048,128]{1,0:T(8,128)S(1)}) custom-call(f32[1,2048]{1,0:T(1,128)S(1)} %add.52.refs_0_, f32[2048,2048]{1,0:T(8,128)S(1)} %get-tuple-element.57.refs_1_), custom_call_target="tpu_custom_call" | custom-call | flops 16777216 | bytes 1 | tf_op jit(solution)/shard_map/pallas_call | solution.py:84
  40.2 1.1 %collective-permute-done.16 = f32[1,512]{1,0:T(1,128)S(1)} collective-permute-done((f32[1,512]{1,0:T(1,128)S(1)}, f32[1,512]{1,0:T(1,128)S(1)}, u32[]{:S(2)}, u32[]{:S(2)}) %collective-permute-start.16) | collective-permute-done | bytes 2080 | tf_op jit(solution)/shard_map/ppermute | solution.py:40
  41.3 2.5 %collective-permute-start.17 = (f32[1,512]{1,0:T(1,128)S(1)}, f32[1,512]{1,0:T(1,128)S(1)}, u32[]{:S(2)}, u32[]{:S(2)}) collective-permute-start(f32[1,512]{1,0:T(1,128)S(1)} %add.53), channel_id=1, source_target_pairs={{0,6},{1,7},{2,4},{3,5},{4,2},{5,3},{6,0},{7,1},{8,14},{9,15},{10,... | collective-permute-start | bytes 6152 | tf_op jit(solution)/shard_map/ppermute | solution.py:36
  43.8 0.9 %collective-permute-start.18 = (f32[1,512]{1,0:T(1,128)S(1)}, f32[1,512]{1,0:T(1,128)S(1)}, u32[]{:S(2)}, u32[]{:S(2)}) collective-permute-start(f32[1,512]{1,0:T(1,128)S(1)} %add.53), channel_id=1, source_target_pairs={{0,4},{1,5},{2,6},{3,7},{4,0},{5,1},{6,2},{7,3},{8,12},{9,13},{10,... | collective-permute-start | bytes 6152 | tf_op jit(solution)/shard_map/ppermute | solution.py:36
  44.8 1.0 %collective-permute-start.19 = (f32[1,512]{1,0:T(1,128)S(1)}, f32[1,512]{1,0:T(1,128)S(1)}, u32[]{:S(2)}, u32[]{:S(2)}) collective-permute-start(f32[1,512]{1,0:T(1,128)S(1)} %add.53), channel_id=1, source_target_pairs={{0,2},{1,3},{2,0},{3,1},{4,6},{5,7},{6,4},{7,5},{8,10},{9,11},{10,... | collective-permute-start | bytes 6152 | tf_op jit(solution)/shard_map/ppermute | solution.py:36
  45.7 0.8 %shard_map.37.refs_1_ = f32[512,2048]{1,0:T(8,128)S(1)} custom-call(bf16[2048,256]{1,0:T(8,128)(2,1)S(1)} %get-tuple-element.47.unit_feat, bf16[2048,256]{1,0:T(8,128)(2,1)S(1)} %get-tuple-element.59.unit_proto, f32[2048,128]{1,0:T(8,128)S(1)} %get-tuple-element.60.col_factor), custom_call_target="tpu_custom_call" | custom-call | flops 536870912 | bytes 1 | tf_op jit(solution)/shard_map/pallas_call | solution.py:84
  46.7 1.6 %collective-permute-done.18 = f32[1,512]{1,0:T(1,128)S(1)} collective-permute-done((f32[1,512]{1,0:T(1,128)S(1)}, f32[1,512]{1,0:T(1,128)S(1)}, u32[]{:S(2)}, u32[]{:S(2)}) %collective-permute-start.18) | collective-permute-done | bytes 2080 | tf_op jit(solution)/shard_map/ppermute | solution.py:36
  48.4 1.5 %shard_map.38 = bf16[512,2048]{1,0:T(8,128)(2,1)} custom-call(f32[1,512]{1,0:T(1,128)S(1)} %add.56.refs_0_, f32[512,2048]{1,0:T(8,128)S(1)} %shard_map.37.refs_1_), custom_call_target="tpu_custom_call" | custom-call | tf_op jit(solution)/shard_map/pallas_call | solution.py:351
  (34 shorter events, 1.8 us)
Async XLA Ops:
  0.0 7.5 %collective-permute-start.2 = (bf16[512,256]{1,0:T(8,128)(2,1)}, bf16[512,256]{1,0:T(8,128)(2,1)S(1)}, u32[]{:S(2)}, u32[]{:S(2)}) collective-permute-start(bf16[512,256]{1,0:T(8,128)(2,1)} %feats.1), channel_id=1, source_target_pairs={{0,8},{1,17},{2,10},{3,19},{4,12},{5,21},{6,14},{7,23},{8,0},{9,25... | collective-permute-start | bytes 786440 | tf_op jit(solution)/shard_map/ppermute | solution.py:256
  4.3 6.4 %collective-permute-start = (bf16[512,256]{1,0:T(8,128)(2,1)S(1)}, bf16[512,256]{1,0:T(8,128)(2,1)S(1)}, u32[]{:S(2)}, u32[]{:S(2)}) collective-permute-start(bf16[512,256]{1,0:T(8,128)(2,1)S(1)} %get-tuple-element.37.own_proto), channel_id=1, source_target_pairs={{0,8},{1,17},{2,10},{3,19},{4,12},{5,21},{6,14},{7,23},{8,0},{9,25... | collective-permute-start | bytes 786440 | tf_op jit(solution)/shard_map/ppermute | solution.py:256
  7.5 4.9 %collective-permute-start.4 = (bf16[512,256]{1,0:T(8,128)(2,1)S(1)}, bf16[512,256]{1,0:T(8,128)(2,1)S(1)}, u32[]{:S(2)}, u32[]{:S(2)}) collective-permute-start(bf16[512,256]{1,0:T(8,128)(2,1)S(1)} %collective-permute-done.2.near), channel_id=1, source_target_pairs={{0,1},{1,0},{2,3},{3,2},{4,5},{5,4},{6,7},{7,6},{8,9},{9,8},{10,11... | collective-permute-start | bytes 786440 | tf_op jit(solution)/shard_map/ppermute | solution.py:40
  7.5 5.8 %collective-permute-start.3 = (bf16[256,256]{1,0:T(8,128)(2,1)S(1)}, bf16[256,256]{1,0:T(8,128)(2,1)S(1)}, u32[]{:S(2)}, u32[]{:S(2)}) collective-permute-start(bf16[256,256]{1,0:T(8,128)(2,1)S(1)} %constant_dynamic-slice_fusion), channel_id=1, source_target_pairs={{0,16},{1,9},{2,18},{3,11},{4,20},{5,13},{6,22},{7,15},{8,24},{9,1... | collective-permute-start | bytes 393224 | tf_op jit(solution)/shard_map/ppermute | solution.py:256
  9.6 7.1 %collective-permute-start.7 = (bf16[512,256]{1,0:T(8,128)(2,1)S(1)}, bf16[512,256]{1,0:T(8,128)(2,1)S(1)}, u32[]{:S(2)}, u32[]{:S(2)}) collective-permute-start(bf16[512,256]{1,0:T(8,128)(2,1)S(1)} %get-tuple-element.37.own_proto), channel_id=1, source_target_pairs={{0,16},{1,9},{2,18},{3,11},{4,20},{5,13},{6,22},{7,15},{8,24},{9,1... | collective-permute-start | bytes 786440 | tf_op jit(solution)/shard_map/ppermute | solution.py:256
  10.7 7.2 %collective-permute-start.6 = (bf16[320,256]{1,0:T(8,128)(2,1)S(1)}, bf16[320,256]{1,0:T(8,128)(2,1)S(1)}, u32[]{:S(2)}, u32[]{:S(2)}) collective-permute-start(bf16[320,256]{1,0:T(8,128)(2,1)S(1)} %slice.9), channel_id=1, source_target_pairs={{0,16},{1,9},{2,18},{3,11},{4,20},{5,13},{6,22},{7,15},{8,24},{9,1... | collective-permute-start | bytes 491528 | tf_op jit(solution)/shard_map/ppermute | solution.py:256
  13.3 2.0 %collective-permute-start.5 = (bf16[256,256]{1,0:T(8,128)(2,1)S(1)}, bf16[256,256]{1,0:T(8,128)(2,1)S(1)}, u32[]{:S(2)}, u32[]{:S(2)}) collective-permute-start(bf16[256,256]{1,0:T(8,128)(2,1)S(1)} %collective-permute-done.3.far), channel_id=1, source_target_pairs={{0,1},{1,0},{2,3},{3,2},{4,5},{5,4},{6,7},{7,6},{8,9},{9,8},{10,11... | collective-permute-start | bytes 393224 | tf_op jit(solution)/shard_map/ppermute | solution.py:40
  13.4 5.4 %collective-permute-start.1 = (bf16[192,256]{1,0:T(8,128)(2,1)S(1)}, bf16[192,256]{1,0:T(8,128)(2,1)S(1)}, u32[]{:S(2)}, u32[]{:S(2)}) collective-permute-start(bf16[192,256]{1,0:T(8,128)(2,1)S(1)} %slice.8), channel_id=1, source_target_pairs={{0,16},{1,9},{2,18},{3,11},{4,20},{5,13},{6,22},{7,15},{8,24},{9,1... | collective-permute-start | bytes 294920 | tf_op jit(solution)/shard_map/ppermute | solution.py:256
  19.5 1.2 %collective-permute-start.8 = (f32[1,2048]{1,0:T(1,128)S(1)}, f32[1,2048]{1,0:T(1,128)S(1)}, u32[]{:S(2)}, u32[]{:S(2)}) collective-permute-start(f32[1,2048]{1,0:T(1,128)S(1)} %get-tuple-element.56), channel_id=1, source_target_pairs={{0,1},{1,0},{2,3},{3,2},{4,5},{5,4},{6,7},{7,6},{8,9},{9,8},{10,11... | collective-permute-start | bytes 24584 | tf_op jit(solution)/shard_map/ppermute | solution.py:40
  20.7 5.5 %collective-permute-start.9 = (f32[1,2048]{1,0:T(1,128)S(1)}, f32[1,2048]{1,0:T(1,128)S(1)}, u32[]{:S(2)}, u32[]{:S(2)}) collective-permute-start(f32[1,2048]{1,0:T(1,128)S(1)} %add.45), channel_id=1, source_target_pairs={{0,6},{1,7},{2,4},{3,5},{4,2},{5,3},{6,0},{7,1},{8,14},{9,15},{10,... | collective-permute-start | bytes 24584 | tf_op jit(solution)/shard_map/ppermute | solution.py:36
  24.4 4.5 %collective-permute-start.10 = (f32[1,2048]{1,0:T(1,128)S(1)}, f32[1,2048]{1,0:T(1,128)S(1)}, u32[]{:S(2)}, u32[]{:S(2)}) collective-permute-start(f32[1,2048]{1,0:T(1,128)S(1)} %add.45), channel_id=1, source_target_pairs={{0,4},{1,5},{2,6},{3,7},{4,0},{5,1},{6,2},{7,3},{8,12},{9,13},{10,... | collective-permute-start | bytes 24584 | tf_op jit(solution)/shard_map/ppermute | solution.py:36
  24.4 4.6 %collective-permute-start.11 = (f32[1,2048]{1,0:T(1,128)S(1)}, f32[1,2048]{1,0:T(1,128)S(1)}, u32[]{:S(2)}, u32[]{:S(2)}) collective-permute-start(f32[1,2048]{1,0:T(1,128)S(1)} %add.45), channel_id=1, source_target_pairs={{0,2},{1,3},{2,0},{3,1},{4,6},{5,7},{6,4},{7,5},{8,10},{9,11},{10,... | collective-permute-start | bytes 24584 | tf_op jit(solution)/shard_map/ppermute | solution.py:36
  31.3 1.2 %collective-permute-start.12 = (f32[1,2048]{1,0:T(1,128)S(1)}, f32[1,2048]{1,0:T(1,128)S(1)}, u32[]{:S(2)}, u32[]{:S(2)}) collective-permute-start(f32[1,2048]{1,0:T(1,128)S(1)} %shard_map.35), channel_id=1, source_target_pairs={{0,1},{1,0},{2,3},{3,2},{4,5},{5,4},{6,7},{7,6},{8,9},{9,8},{10,11... | collective-permute-start | bytes 24584 | tf_op jit(solution)/shard_map/ppermute | solution.py:40
  32.5 5.6 %collective-permute-start.13 = (f32[1,2048]{1,0:T(1,128)S(1)}, f32[1,2048]{1,0:T(1,128)S(1)}, u32[]{:S(2)}, u32[]{:S(2)}) collective-permute-start(f32[1,2048]{1,0:T(1,128)S(1)} %add.49), channel_id=1, source_target_pairs={{0,6},{1,7},{2,4},{3,5},{4,2},{5,3},{6,0},{7,1},{8,14},{9,15},{10,... | collective-permute-start | bytes 24584 | tf_op jit(solution)/shard_map/ppermute | solution.py:36
  34.0 4.5 %collective-permute-start.14 = (f32[1,2048]{1,0:T(1,128)S(1)}, f32[1,2048]{1,0:T(1,128)S(1)}, u32[]{:S(2)}, u32[]{:S(2)}) collective-permute-start(f32[1,2048]{1,0:T(1,128)S(1)} %add.49), channel_id=1, source_target_pairs={{0,4},{1,5},{2,6},{3,7},{4,0},{5,1},{6,2},{7,3},{8,12},{9,13},{10,... | collective-permute-start | bytes 24584 | tf_op jit(solution)/shard_map/ppermute | solution.py:36
  34.6 4.0 %collective-permute-start.15 = (f32[1,2048]{1,0:T(1,128)S(1)}, f32[1,2048]{1,0:T(1,128)S(1)}, u32[]{:S(2)}, u32[]{:S(2)}) collective-permute-start(f32[1,2048]{1,0:T(1,128)S(1)} %add.49), channel_id=1, source_target_pairs={{0,2},{1,3},{2,0},{3,1},{4,6},{5,7},{6,4},{7,5},{8,10},{9,11},{10,... | collective-permute-start | bytes 24584 | tf_op jit(solution)/shard_map/ppermute | solution.py:36
  40.1 1.2 %collective-permute-start.16 = (f32[1,512]{1,0:T(1,128)S(1)}, f32[1,512]{1,0:T(1,128)S(1)}, u32[]{:S(2)}, u32[]{:S(2)}) collective-permute-start(f32[1,512]{1,0:T(1,128)S(1)} %get-tuple-element.58), channel_id=1, source_target_pairs={{0,1},{1,0},{2,3},{3,2},{4,5},{5,4},{6,7},{7,6},{8,9},{9,8},{10,11... | collective-permute-start | bytes 6152 | tf_op jit(solution)/shard_map/ppermute | solution.py:40
  41.3 5.4 %collective-permute-start.17 = (f32[1,512]{1,0:T(1,128)S(1)}, f32[1,512]{1,0:T(1,128)S(1)}, u32[]{:S(2)}, u32[]{:S(2)}) collective-permute-start(f32[1,512]{1,0:T(1,128)S(1)} %add.53), channel_id=1, source_target_pairs={{0,6},{1,7},{2,4},{3,5},{4,2},{5,3},{6,0},{7,1},{8,14},{9,15},{10,... | collective-permute-start | bytes 6152 | tf_op jit(solution)/shard_map/ppermute | solution.py:36
  43.8 4.5 %collective-permute-start.18 = (f32[1,512]{1,0:T(1,128)S(1)}, f32[1,512]{1,0:T(1,128)S(1)}, u32[]{:S(2)}, u32[]{:S(2)}) collective-permute-start(f32[1,512]{1,0:T(1,128)S(1)} %add.53), channel_id=1, source_target_pairs={{0,4},{1,5},{2,6},{3,7},{4,0},{5,1},{6,2},{7,3},{8,12},{9,13},{10,... | collective-permute-start | bytes 6152 | tf_op jit(solution)/shard_map/ppermute | solution.py:36
  44.8 3.6 %collective-permute-start.19 = (f32[1,512]{1,0:T(1,128)S(1)}, f32[1,512]{1,0:T(1,128)S(1)}, u32[]{:S(2)}, u32[]{:S(2)}) collective-permute-start(f32[1,512]{1,0:T(1,128)S(1)} %add.53), channel_id=1, source_target_pairs={{0,2},{1,3},{2,0},{3,1},{4,6},{5,7},{6,4},{7,5},{8,10},{9,11},{10,... | collective-permute-start | bytes 6152 | tf_op jit(solution)/shard_map/ppermute | solution.py:36

commit v7 on v6

--- a/solution.py
+++ b/solution.py
@@ -150,12 +150,16 @@
     sums[rows, :] = fill(weights, total, rows, slice(0, 3 * block), first[...], unit_feat)
 
 
-def far_kernel(far, far_swapped, sums, unit_proto, feat_in, weights_in, unit_feat, weights, part):
+def far_kernel(far, *refs):
+    *far_swapped, sums, unit_proto, feat_in, weights_in, unit_feat, weights, part = refs
     half = far.shape[0]
     block = 2 * half
     core = lax.axis_index("proto") % 2
     unit_feat[pl.ds(pl.multiple_of(3 * block + (1 - core) * half, half), half), :] = unit_rows(far[...])
-    unit_feat[pl.ds(pl.multiple_of(3 * block + core * half, half), half), :] = unit_rows(far_swapped[...])
+    height = half // len(far_swapped)
+    for index, piece in enumerate(far_swapped):
+        start = pl.multiple_of(3 * block + core * half + index * height, height)
+        unit_feat[pl.ds(start, height), :] = unit_rows(piece[...])
     part[...] = jnp.zeros(part.shape, F32)
 
     def body(index, carry):
@@ -292,7 +296,7 @@
         16,
     )
     far, sums = lax.optimization_barrier((far, sums))
-    cut = 5 * block // 8
+    cut = 11 * block // 16
     last = [send(first[:cut], (2, 1)), send(first[cut:], (2, 1))]
     sums, unit_proto, weights = call(
         first_kernel,
@@ -301,12 +305,13 @@
         16,
         aliases={1: 0, 3: 1, 4: 2},
     )
+    swapped = [swap_cores(far[: half // 2]), swap_cores(far[half // 2 :])]
     unit_feat, weights, part = call(
         far_kernel,
         [feat_shape, weights_shape, part_shape],
-        [far, swap_cores(far), sums, unit_proto, unit_feat, weights],
+        [far, *swapped, sums, unit_proto, unit_feat, weights],
         16,
-        aliases={4: 0, 5: 1},
+        aliases={3 + len(swapped): 0, 4 + len(swapped): 1},
     )
     outs = [feat_shape, weights_shape, part_shape, ((1, images), F32)]
     start = 2 * block

time: 50 us -> 50 us (level)
  starting transfers between devices: 22.1 us -> 21.5 us
  waiting for transfers between devices: 14.7 us -> 15.3 us
    ppermute x6, starting transfers between devices: 8.23 us -> 7.3 us  [send(): return lax.ppermute(value, ('batch', 'proto'), by_core(steps))]
    ppermute x5 -> x6, waiting for transfers between devices: 3.15 us -> 3.65 us  [swap_cores(): lax.ppermute(value, 'proto', partners(lax.axis_size('proto'), 1, 2, 1))]
  transfers between devices with their start and end apart: 20 -> 21, of which waited for: 13 -> 16; matrix products, arithmetic and copies ran while one was open for 0% -> 0% of each run, Pallas kernels for 14% -> 14%
where the time goes in v7:
time: 50 us; the launch traced here: 49.9 us
  starting transfers between devices  21.5 us (43%)
  waiting for transfers between devices  15.3 us (31%)
  Pallas kernels  12.8 us (26%)
    ppermute x9, starting transfers between devices, from_others(): lax.ppermute(value, axis, partners(size, stride, count, step))  13.3 us
    pallas_call x9, Pallas kernels, call(): pl.pallas_call(kernel, out_shape=[VMEM(shape, dtype) for shape, dtype in...  9.94 us
    ppermute x6, starting transfers between devices, send(): return lax.ppermute(value, ('batch', 'proto'), by_core(steps))  7.3 us
    ppermute x9, waiting for transfers between devices, from_others(): lax.ppermute(value, axis, partners(size, stride, count, step))  7.22 us
    ppermute x6, waiting for transfers between devices, send(): return lax.ppermute(value, ('batch', 'proto'), by_core(steps))  4.43 us
    ppermute x6, waiting for transfers between devices, swap_cores(): lax.ppermute(value, 'proto', partners(lax.axis_size('proto'), 1, 2, 1))  3.65 us
    pallas_call x1, Pallas kernels, whole_plan(): pl.pallas_call(functools.partial(last_kernel, len(parts), block), out_sha...  1.51 us
    pallas_call x1, Pallas kernels, whole_plan(): pl.pallas_call(unit_kernel, out_shape=[VMEM((block, depth), bf16)] * 2, i...  1.31 us
  transfers between devices with their start and end apart: 21, of which 16 were waited for; matrix products, arithmetic and copies ran while one was open for 0% of the time, Pallas kernels for 14%

profile of v7, /device:TPU:0, one launch (start us, length us, event | category | flops | bytes accessed | tf_op | source)
XLA Modules:
  0.0 49.9 jit_solution(12136274322308928307)
XLA Ops:
  0.0 2.9 %collective-permute-start.2 = (bf16[512,256]{1,0:T(8,128)(2,1)}, bf16[512,256]{1,0:T(8,128)(2,1)S(1)}, u32[]{:S(2)}, u32[]{:S(2)}) collective-permute-start(bf16[512,256]{1,0:T(8,128)(2,1)} %feats.1), channel_id=1, source_target_pairs={{0,8},{1,17},{2,10},{3,19},{4,12},{5,21},{6,14},{7,23},{8,0},{9,25... | collective-permute-start | bytes 786440 | tf_op jit(solution)/shard_map/ppermute | solution.py:260
  2.9 1.3 %shard_map.28 = (bf16[512,256]{1,0:T(8,128)(2,1)S(1)}, bf16[512,256]{1,0:T(8,128)(2,1)S(1)}) custom-call(bf16[512,256]{1,0:T(8,128)(2,1)} %feats.1, bf16[512,256]{1,0:T(8,128)(2,1)} %protos.1), custom_call_target="tpu_custom_call" | custom-call | flops 1 | bytes 1 | tf_op jit(solution)/shard_map/pallas_call | solution.py:277
  4.3 3.2 %collective-permute-done.2.near = bf16[512,256]{1,0:T(8,128)(2,1)S(1)} collective-permute-done((bf16[512,256]{1,0:T(8,128)(2,1)}, bf16[512,256]{1,0:T(8,128)(2,1)S(1)}, u32[]{:S(2)}, u32[]{:S(2)}) %collective-permute-start.2) | collective-permute-done | bytes 262176 | tf_op jit(solution)/shard_map/ppermute | solution.py:260
  7.5 2.1 %collective-permute-start.3 = (bf16[256,256]{1,0:T(8,128)(2,1)S(1)}, bf16[256,256]{1,0:T(8,128)(2,1)S(1)}, u32[]{:S(2)}, u32[]{:S(2)}) collective-permute-start(bf16[256,256]{1,0:T(8,128)(2,1)S(1)} %constant_dynamic-slice_fusion), channel_id=1, source_target_pairs={{0,16},{1,9},{2,18},{3,11},{4,20},{5,13},{6,22},{7,15},{8,24},{9,1... | collective-permute-start | bytes 393224 | tf_op jit(solution)/shard_map/ppermute | solution.py:260
  9.7 1.0 %collective-permute-done.first = bf16[512,256]{1,0:T(8,128)(2,1)S(1)} collective-permute-done((bf16[512,256]{1,0:T(8,128)(2,1)S(1)}, bf16[512,256]{1,0:T(8,128)(2,1)S(1)}, u32[]{:S(2)}, u32[]{:S(2)}) %collective-permute-start) | collective-permute-done | bytes 262176 | tf_op jit(solution)/shard_map/ppermute | solution.py:260
  10.7 1.7 %collective-permute-start.7 = (bf16[352,256]{1,0:T(8,128)(2,1)S(1)}, bf16[352,256]{1,0:T(8,128)(2,1)S(1)}, u32[]{:S(2)}, u32[]{:S(2)}) collective-permute-start(bf16[352,256]{1,0:T(8,128)(2,1)S(1)} %slice.17), channel_id=1, source_target_pairs={{0,16},{1,9},{2,18},{3,11},{4,20},{5,13},{6,22},{7,15},{8,24},{9,1... | collective-permute-start | bytes 540680 | tf_op jit(solution)/shard_map/ppermute | solution.py:260
  12.8 0.8 %shard_map.29 = (bf16[2048,256]{1,0:T(8,128)(2,1)S(1)}, bf16[2048,256]{1,0:T(8,128)(2,1)S(1)}, f32[2048,2048]{1,0:T(8,128)S(1)}, f32[2048,128]{1,0:T(8,128)S(1)}) custom-call(bf16[512,256]{1,0:T(8,128)(2,1)S(1)} %get-tuple-element.36.own_feat, bf16[512,256]{1,0:T(8,128)(2,1)S(1)} %collective-permute-done.2.near, ...), custom_call_target="tpu_custom_call" | custom-call | flops 1 | bytes 1 | tf_op jit(solution)/shard_map/pallas_call | solution.py:84
  13.8 0.5 collective-permute-start.6
  14.3 0.6 %shard_map.30 = (f32[2048,128]{1,0:T(8,128)S(1)}, bf16[2048,256]{1,0:T(8,128)(2,1)S(1)}, f32[2048,2048]{1,0:T(8,128)S(1)}) custom-call(bf16[512,256]{1,0:T(8,128)(2,1)S(1)} %collective-permute-done.first, f32[2048,128]{1,0:T(8,128)S(1)} %get-tuple-element.40.sums_in, ...), custom_call_target="tpu_custom_call", output_to_operand_aliasing={{0}: (1, {}), {1}: (3, {}), {2}: (4, {})} | custom-call | flops 1 | bytes 1 | tf_op jit(solution)/shard_map/pallas_call | solution.py:84
  15.2 1.4 %shard_map.31 = (bf16[2048,256]{1,0:T(8,128)(2,1)S(1)}, f32[2048,2048]{1,0:T(8,128)S(1)}, f32[8,2048]{1,0:T(8,128)S(1)}) custom-call(bf16[256,256]{1,0:T(8,128)(2,1)S(1)} %collective-permute-done.3.far, bf16[128,256]{1,0:T(8,128)(2,1)S(1)} %collective-permute-done.5.refs_0_, ...), custom_call_target="tpu_custom_call", output_to_operand_aliasing={{0}: (5, {}), {1}: (6, {})} | custom-call | flops 1 | bytes 1 | tf_op jit(solution)/shard_map/pallas_call | solution.py:84
  16.6 1.1 %shard_map.32 = (bf16[2048,256]{1,0:T(8,128)(2,1)S(1)}, f32[2048,2048]{1,0:T(8,128)S(1)}, f32[8,2048]{1,0:T(8,128)S(1)}) custom-call(bf16[512,256]{1,0:T(8,128)(2,1)S(1)} %collective-permute-done.8.ready, bf16[2048,256]{1,0:T(8,128)(2,1)S(1)} %get-tuple-element.47.unit_feat, ...), custom_call_target="tpu_custom_call", output_to_operand_aliasing={{0}: (2, {}), {1}: (3, {}), {2}: (4, {})} | custom-call | flops 1 | bytes 1 | tf_op jit(solution)/shard_map/pallas_call | solution.py:84
  17.9 0.8 %shard_map.33 = (bf16[2048,256]{1,0:T(8,128)(2,1)S(1)}, f32[2048,2048]{1,0:T(8,128)S(1)}, f32[8,2048]{1,0:T(8,128)S(1)}) custom-call(bf16[352,256]{1,0:T(8,128)(2,1)S(1)} %collective-permute-done.7.ready, bf16[2048,256]{1,0:T(8,128)(2,1)S(1)} %get-tuple-element.47.unit_feat, ...), custom_call_target="tpu_custom_call", output_to_operand_aliasing={{0}: (2, {}), {1}: (3, {}), {2}: (4, {})} | custom-call | flops 1 | bytes 1 | tf_op jit(solution)/shard_map/pallas_call | solution.py:84
  18.8 0.7 %shard_map.34 = (bf16[2048,256]{1,0:T(8,128)(2,1)S(1)}, f32[2048,2048]{1,0:T(8,128)S(1)}, f32[8,2048]{1,0:T(8,128)S(1)}, f32[1,2048]{1,0:T(1,128)S(1)}) custom-call(bf16[160,256]{1,0:T(8,128)(2,1)S(1)} %collective-permute-done.1.ready, bf16[2048,256]{1,0:T(8,128)(2,1)S(1)} %get-tuple-element.47.unit_feat, ...), custom_call_target="tpu_custom_call", output_to_operand_aliasing={{0}: (2, {}), {1}: (3, {}), {2}: (4, {})} | custom-call | flops 1 | bytes 1 | tf_op jit(solution)/shard_map/pallas_call | solution.py:84
  19.7 1.1 %collective-permute-done.9 = f32[1,2048]{1,0:T(1,128)S(1)} collective-permute-done((f32[1,2048]{1,0:T(1,128)S(1)}, f32[1,2048]{1,0:T(1,128)S(1)}, u32[]{:S(2)}, u32[]{:S(2)}) %collective-permute-start.9) | collective-permute-done | bytes 8224 | tf_op jit(solution)/shard_map/ppermute | solution.py:40
  20.7 3.7 %collective-permute-start.10 = (f32[1,2048]{1,0:T(1,128)S(1)}, f32[1,2048]{1,0:T(1,128)S(1)}, u32[]{:S(2)}, u32[]{:S(2)}) collective-permute-start(f32[1,2048]{1,0:T(1,128)S(1)} %add.45), channel_id=1, source_target_pairs={{0,6},{1,7},{2,4},{3,5},{4,2},{5,3},{6,0},{7,1},{8,14},{9,15},{10,... | collective-permute-start | bytes 24584 | tf_op jit(solution)/shard_map/ppermute | solution.py:36
  24.4 0.8 %collective-permute-start.12 = (f32[1,2048]{1,0:T(1,128)S(1)}, f32[1,2048]{1,0:T(1,128)S(1)}, u32[]{:S(2)}, u32[]{:S(2)}) collective-permute-start(f32[1,2048]{1,0:T(1,128)S(1)} %add.45), channel_id=1, source_target_pairs={{0,2},{1,3},{2,0},{3,1},{4,6},{5,7},{6,4},{7,5},{8,10},{9,11},{10,... | collective-permute-start | bytes 24584 | tf_op jit(solution)/shard_map/ppermute | solution.py:36
  25.2 1.1 %collective-permute-done.10 = f32[1,2048]{1,0:T(1,128)S(1)} collective-permute-done((f32[1,2048]{1,0:T(1,128)S(1)}, f32[1,2048]{1,0:T(1,128)S(1)}, u32[]{:S(2)}, u32[]{:S(2)}) %collective-permute-start.10) | collective-permute-done | bytes 8224 | tf_op jit(solution)/shard_map/ppermute | solution.py:36
  26.3 2.7 %collective-permute-done.11 = f32[1,2048]{1,0:T(1,128)S(1)} collective-permute-done((f32[1,2048]{1,0:T(1,128)S(1)}, f32[1,2048]{1,0:T(1,128)S(1)}, u32[]{:S(2)}, u32[]{:S(2)}) %collective-permute-start.11) | collective-permute-done | bytes 8224 | tf_op jit(solution)/shard_map/ppermute | solution.py:36
  29.0 2.2 %shard_map.35 = f32[1,2048]{1,0:T(1,128)S(1)} custom-call(f32[1,2048]{1,0:T(1,128)S(1)} %add.48.refs_0_, f32[2048,2048]{1,0:T(8,128)S(1)} %get-tuple-element.57.refs_1_), custom_call_target="tpu_custom_call" | custom-call | flops 16777216 | bytes 1 | tf_op jit(solution)/shard_map/pallas_call | solution.py:84
  31.3 1.2 %collective-permute-done.13 = f32[1,2048]{1,0:T(1,128)S(1)} collective-permute-done((f32[1,2048]{1,0:T(1,128)S(1)}, f32[1,2048]{1,0:T(1,128)S(1)}, u32[]{:S(2)}, u32[]{:S(2)}) %collective-permute-start.13) | collective-permute-done | bytes 8224 | tf_op jit(solution)/shard_map/ppermute | solution.py:40
  32.5 1.5 %collective-permute-start.14 = (f32[1,2048]{1,0:T(1,128)S(1)}, f32[1,2048]{1,0:T(1,128)S(1)}, u32[]{:S(2)}, u32[]{:S(2)}) collective-permute-start(f32[1,2048]{1,0:T(1,128)S(1)} %add.49), channel_id=1, source_target_pairs={{0,6},{1,7},{2,4},{3,5},{4,2},{5,3},{6,0},{7,1},{8,14},{9,15},{10,... | collective-permute-start | bytes 24584 | tf_op jit(solution)/shard_map/ppermute | solution.py:36
  34.0 0.6 %collective-permute-start.15 = (f32[1,2048]{1,0:T(1,128)S(1)}, f32[1,2048]{1,0:T(1,128)S(1)}, u32[]{:S(2)}, u32[]{:S(2)}) collective-permute-start(f32[1,2048]{1,0:T(1,128)S(1)} %add.49), channel_id=1, source_target_pairs={{0,4},{1,5},{2,6},{3,7},{4,0},{5,1},{6,2},{7,3},{8,12},{9,13},{10,... | collective-permute-start | bytes 24584 | tf_op jit(solution)/shard_map/ppermute | solution.py:36
  34.6 2.3 %collective-permute-start.16 = (f32[1,2048]{1,0:T(1,128)S(1)}, f32[1,2048]{1,0:T(1,128)S(1)}, u32[]{:S(2)}, u32[]{:S(2)}) collective-permute-start(f32[1,2048]{1,0:T(1,128)S(1)} %add.49), channel_id=1, source_target_pairs={{0,2},{1,3},{2,0},{3,1},{4,6},{5,7},{6,4},{7,5},{8,10},{9,11},{10,... | collective-permute-start | bytes 24584 | tf_op jit(solution)/shard_map/ppermute | solution.py:36
  36.9 1.1 %collective-permute-done.14 = f32[1,2048]{1,0:T(1,128)S(1)} collective-permute-done((f32[1,2048]{1,0:T(1,128)S(1)}, f32[1,2048]{1,0:T(1,128)S(1)}, u32[]{:S(2)}, u32[]{:S(2)}) %collective-permute-start.14) | collective-permute-done | bytes 8224 | tf_op jit(solution)/shard_map/ppermute | solution.py:36
  38.6 1.4 %shard_map.36 = (f32[1,512]{1,0:T(1,128)S(1)}, f32[2048,128]{1,0:T(8,128)S(1)}) custom-call(f32[1,2048]{1,0:T(1,128)S(1)} %add.52.refs_0_, f32[2048,2048]{1,0:T(8,128)S(1)} %get-tuple-element.57.refs_1_), custom_call_target="tpu_custom_call" | custom-call | flops 16777216 | bytes 1 | tf_op jit(solution)/shard_map/pallas_call | solution.py:84
  40.2 1.1 %collective-permute-done.17 = f32[1,512]{1,0:T(1,128)S(1)} collective-permute-done((f32[1,512]{1,0:T(1,128)S(1)}, f32[1,512]{1,0:T(1,128)S(1)}, u32[]{:S(2)}, u32[]{:S(2)}) %collective-permute-start.17) | collective-permute-done | bytes 2080 | tf_op jit(solution)/shard_map/ppermute | solution.py:40
  41.3 2.5 %collective-permute-start.18 = (f32[1,512]{1,0:T(1,128)S(1)}, f32[1,512]{1,0:T(1,128)S(1)}, u32[]{:S(2)}, u32[]{:S(2)}) collective-permute-start(f32[1,512]{1,0:T(1,128)S(1)} %add.53), channel_id=1, source_target_pairs={{0,6},{1,7},{2,4},{3,5},{4,2},{5,3},{6,0},{7,1},{8,14},{9,15},{10,... | collective-permute-start | bytes 6152 | tf_op jit(solution)/shard_map/ppermute | solution.py:36
  43.8 0.9 %collective-permute-start.19 = (f32[1,512]{1,0:T(1,128)S(1)}, f32[1,512]{1,0:T(1,128)S(1)}, u32[]{:S(2)}, u32[]{:S(2)}) collective-permute-start(f32[1,512]{1,0:T(1,128)S(1)} %add.53), channel_id=1, source_target_pairs={{0,4},{1,5},{2,6},{3,7},{4,0},{5,1},{6,2},{7,3},{8,12},{9,13},{10,... | collective-permute-start | bytes 6152 | tf_op jit(solution)/shard_map/ppermute | solution.py:36
  44.8 1.0 %collective-permute-start.20 = (f32[1,512]{1,0:T(1,128)S(1)}, f32[1,512]{1,0:T(1,128)S(1)}, u32[]{:S(2)}, u32[]{:S(2)}) collective-permute-start(f32[1,512]{1,0:T(1,128)S(1)} %add.53), channel_id=1, source_target_pairs={{0,2},{1,3},{2,0},{3,1},{4,6},{5,7},{6,4},{7,5},{8,10},{9,11},{10,... | collective-permute-start | bytes 6152 | tf_op jit(solution)/shard_map/ppermute | solution.py:36
  45.7 0.8 %shard_map.37.refs_1_ = f32[512,2048]{1,0:T(8,128)S(1)} custom-call(bf16[2048,256]{1,0:T(8,128)(2,1)S(1)} %get-tuple-element.47.unit_feat, bf16[2048,256]{1,0:T(8,128)(2,1)S(1)} %get-tuple-element.59.unit_proto, f32[2048,128]{1,0:T(8,128)S(1)} %get-tuple-element.60.col_factor), custom_call_target="tpu_custom_call" | custom-call | flops 536870912 | bytes 1 | tf_op jit(solution)/shard_map/pallas_call | solution.py:84
  46.7 1.6 %collective-permute-done.19 = f32[1,512]{1,0:T(1,128)S(1)} collective-permute-done((f32[1,512]{1,0:T(1,128)S(1)}, f32[1,512]{1,0:T(1,128)S(1)}, u32[]{:S(2)}, u32[]{:S(2)}) %collective-permute-start.19) | collective-permute-done | bytes 2080 | tf_op jit(solution)/shard_map/ppermute | solution.py:36
  48.3 1.5 %shard_map.38 = bf16[512,2048]{1,0:T(8,128)(2,1)} custom-call(f32[1,512]{1,0:T(1,128)S(1)} %add.56.refs_0_, f32[512,2048]{1,0:T(8,128)S(1)} %shard_map.37.refs_1_), custom_call_target="tpu_custom_call" | custom-call | tf_op jit(solution)/shard_map/pallas_call | solution.py:356
  (37 shorter events, 2.3 us)
Async XLA Ops:
  0.0 7.5 %collective-permute-start.2 = (bf16[512,256]{1,0:T(8,128)(2,1)}, bf16[512,256]{1,0:T(8,128)(2,1)S(1)}, u32[]{:S(2)}, u32[]{:S(2)}) collective-permute-start(bf16[512,256]{1,0:T(8,128)(2,1)} %feats.1), channel_id=1, source_target_pairs={{0,8},{1,17},{2,10},{3,19},{4,12},{5,21},{6,14},{7,23},{8,0},{9,25... | collective-permute-start | bytes 786440 | tf_op jit(solution)/shard_map/ppermute | solution.py:260
  4.3 6.4 %collective-permute-start = (bf16[512,256]{1,0:T(8,128)(2,1)S(1)}, bf16[512,256]{1,0:T(8,128)(2,1)S(1)}, u32[]{:S(2)}, u32[]{:S(2)}) collective-permute-start(bf16[512,256]{1,0:T(8,128)(2,1)S(1)} %get-tuple-element.37.own_proto), channel_id=1, source_target_pairs={{0,8},{1,17},{2,10},{3,19},{4,12},{5,21},{6,14},{7,23},{8,0},{9,25... | collective-permute-start | bytes 786440 | tf_op jit(solution)/shard_map/ppermute | solution.py:260
  7.5 5.3 %collective-permute-start.4 = (bf16[512,256]{1,0:T(8,128)(2,1)S(1)}, bf16[512,256]{1,0:T(8,128)(2,1)S(1)}, u32[]{:S(2)}, u32[]{:S(2)}) collective-permute-start(bf16[512,256]{1,0:T(8,128)(2,1)S(1)} %collective-permute-done.2.near), channel_id=1, source_target_pairs={{0,1},{1,0},{2,3},{3,2},{4,5},{5,4},{6,7},{7,6},{8,9},{9,8},{10,11... | collective-permute-start | bytes 786440 | tf_op jit(solution)/shard_map/ppermute | solution.py:40
  7.5 6.1 %collective-permute-start.3 = (bf16[256,256]{1,0:T(8,128)(2,1)S(1)}, bf16[256,256]{1,0:T(8,128)(2,1)S(1)}, u32[]{:S(2)}, u32[]{:S(2)}) collective-permute-start(bf16[256,256]{1,0:T(8,128)(2,1)S(1)} %constant_dynamic-slice_fusion), channel_id=1, source_target_pairs={{0,16},{1,9},{2,18},{3,11},{4,20},{5,13},{6,22},{7,15},{8,24},{9,1... | collective-permute-start | bytes 393224 | tf_op jit(solution)/shard_map/ppermute | solution.py:260
  9.6 7.0 %collective-permute-start.8 = (bf16[512,256]{1,0:T(8,128)(2,1)S(1)}, bf16[512,256]{1,0:T(8,128)(2,1)S(1)}, u32[]{:S(2)}, u32[]{:S(2)}) collective-permute-start(bf16[512,256]{1,0:T(8,128)(2,1)S(1)} %get-tuple-element.37.own_proto), channel_id=1, source_target_pairs={{0,16},{1,9},{2,18},{3,11},{4,20},{5,13},{6,22},{7,15},{8,24},{9,1... | collective-permute-start | bytes 786440 | tf_op jit(solution)/shard_map/ppermute | solution.py:260
  10.7 7.2 %collective-permute-start.7 = (bf16[352,256]{1,0:T(8,128)(2,1)S(1)}, bf16[352,256]{1,0:T(8,128)(2,1)S(1)}, u32[]{:S(2)}, u32[]{:S(2)}) collective-permute-start(bf16[352,256]{1,0:T(8,128)(2,1)S(1)} %slice.17), channel_id=1, source_target_pairs={{0,16},{1,9},{2,18},{3,11},{4,20},{5,13},{6,22},{7,15},{8,24},{9,1... | collective-permute-start | bytes 540680 | tf_op jit(solution)/shard_map/ppermute | solution.py:260
  12.4 6.4 %collective-permute-start.1 = (bf16[160,256]{1,0:T(8,128)(2,1)S(1)}, bf16[160,256]{1,0:T(8,128)(2,1)S(1)}, u32[]{:S(2)}, u32[]{:S(2)}) collective-permute-start(bf16[160,256]{1,0:T(8,128)(2,1)S(1)} %slice.16), channel_id=1, source_target_pairs={{0,16},{1,9},{2,18},{3,11},{4,20},{5,13},{6,22},{7,15},{8,24},{9,1... | collective-permute-start | bytes 245768 | tf_op jit(solution)/shard_map/ppermute | solution.py:260
  13.7 1.3 %collective-permute-start.5 = (bf16[128,256]{1,0:T(8,128)(2,1)S(1)}, bf16[128,256]{1,0:T(8,128)(2,1)S(1)}, u32[]{:S(2)}, u32[]{:S(2)}) collective-permute-start(bf16[128,256]{1,0:T(8,128)(2,1)S(1)} %get-tuple-element.62), channel_id=1, source_target_pairs={{0,1},{1,0},{2,3},{3,2},{4,5},{5,4},{6,7},{7,6},{8,9},{9,8},{10,11... | collective-permute-start | bytes 196616 | tf_op jit(solution)/shard_map/ppermute | solution.py:40
  13.8 1.4 %collective-permute-start.6 = (bf16[128,256]{1,0:T(8,128)(2,1)S(1)}, bf16[128,256]{1,0:T(8,128)(2,1)S(1)}, u32[]{:S(2)}, u32[]{:S(2)}) collective-permute-start(bf16[128,256]{1,0:T(8,128)(2,1)S(1)} %get-tuple-element.61), channel_id=1, source_target_pairs={{0,1},{1,0},{2,3},{3,2},{4,5},{5,4},{6,7},{7,6},{8,9},{9,8},{10,11... | collective-permute-start | bytes 196616 | tf_op jit(solution)/shard_map/ppermute | solution.py:40
  19.5 1.2 %collective-permute-start.9 = (f32[1,2048]{1,0:T(1,128)S(1)}, f32[1,2048]{1,0:T(1,128)S(1)}, u32[]{:S(2)}, u32[]{:S(2)}) collective-permute-start(f32[1,2048]{1,0:T(1,128)S(1)} %get-tuple-element.56), channel_id=1, source_target_pairs={{0,1},{1,0},{2,3},{3,2},{4,5},{5,4},{6,7},{7,6},{8,9},{9,8},{10,11... | collective-permute-start | bytes 24584 | tf_op jit(solution)/shard_map/ppermute | solution.py:40
  20.7 5.5 %collective-permute-start.10 = (f32[1,2048]{1,0:T(1,128)S(1)}, f32[1,2048]{1,0:T(1,128)S(1)}, u32[]{:S(2)}, u32[]{:S(2)}) collective-permute-start(f32[1,2048]{1,0:T(1,128)S(1)} %add.45), channel_id=1, source_target_pairs={{0,6},{1,7},{2,4},{3,5},{4,2},{5,3},{6,0},{7,1},{8,14},{9,15},{10,... | collective-permute-start | bytes 24584 | tf_op jit(solution)/shard_map/ppermute | solution.py:36
  24.4 4.5 %collective-permute-start.11 = (f32[1,2048]{1,0:T(1,128)S(1)}, f32[1,2048]{1,0:T(1,128)S(1)}, u32[]{:S(2)}, u32[]{:S(2)}) collective-permute-start(f32[1,2048]{1,0:T(1,128)S(1)} %add.45), channel_id=1, source_target_pairs={{0,4},{1,5},{2,6},{3,7},{4,0},{5,1},{6,2},{7,3},{8,12},{9,13},{10,... | collective-permute-start | bytes 24584 | tf_op jit(solution)/shard_map/ppermute | solution.py:36
  24.4 4.6 %collective-permute-start.12 = (f32[1,2048]{1,0:T(1,128)S(1)}, f32[1,2048]{1,0:T(1,128)S(1)}, u32[]{:S(2)}, u32[]{:S(2)}) collective-permute-start(f32[1,2048]{1,0:T(1,128)S(1)} %add.45), channel_id=1, source_target_pairs={{0,2},{1,3},{2,0},{3,1},{4,6},{5,7},{6,4},{7,5},{8,10},{9,11},{10,... | collective-permute-start | bytes 24584 | tf_op jit(solution)/shard_map/ppermute | solution.py:36
  31.2 1.2 %collective-permute-start.13 = (f32[1,2048]{1,0:T(1,128)S(1)}, f32[1,2048]{1,0:T(1,128)S(1)}, u32[]{:S(2)}, u32[]{:S(2)}) collective-permute-start(f32[1,2048]{1,0:T(1,128)S(1)} %shard_map.35), channel_id=1, source_target_pairs={{0,1},{1,0},{2,3},{3,2},{4,5},{5,4},{6,7},{7,6},{8,9},{9,8},{10,11... | collective-permute-start | bytes 24584 | tf_op jit(solution)/shard_map/ppermute | solution.py:40
  32.5 5.6 %collective-permute-start.14 = (f32[1,2048]{1,0:T(1,128)S(1)}, f32[1,2048]{1,0:T(1,128)S(1)}, u32[]{:S(2)}, u32[]{:S(2)}) collective-permute-start(f32[1,2048]{1,0:T(1,128)S(1)} %add.49), channel_id=1, source_target_pairs={{0,6},{1,7},{2,4},{3,5},{4,2},{5,3},{6,0},{7,1},{8,14},{9,15},{10,... | collective-permute-start | bytes 24584 | tf_op jit(solution)/shard_map/ppermute | solution.py:36
  34.0 4.5 %collective-permute-start.15 = (f32[1,2048]{1,0:T(1,128)S(1)}, f32[1,2048]{1,0:T(1,128)S(1)}, u32[]{:S(2)}, u32[]{:S(2)}) collective-permute-start(f32[1,2048]{1,0:T(1,128)S(1)} %add.49), channel_id=1, source_target_pairs={{0,4},{1,5},{2,6},{3,7},{4,0},{5,1},{6,2},{7,3},{8,12},{9,13},{10,... | collective-permute-start | bytes 24584 | tf_op jit(solution)/shard_map/ppermute | solution.py:36
  34.6 4.0 %collective-permute-start.16 = (f32[1,2048]{1,0:T(1,128)S(1)}, f32[1,2048]{1,0:T(1,128)S(1)}, u32[]{:S(2)}, u32[]{:S(2)}) collective-permute-start(f32[1,2048]{1,0:T(1,128)S(1)} %add.49), channel_id=1, source_target_pairs={{0,2},{1,3},{2,0},{3,1},{4,6},{5,7},{6,4},{7,5},{8,10},{9,11},{10,... | collective-permute-start | bytes 24584 | tf_op jit(solution)/shard_map/ppermute | solution.py:36
  40.1 1.2 %collective-permute-start.17 = (f32[1,512]{1,0:T(1,128)S(1)}, f32[1,512]{1,0:T(1,128)S(1)}, u32[]{:S(2)}, u32[]{:S(2)}) collective-permute-start(f32[1,512]{1,0:T(1,128)S(1)} %get-tuple-element.58), channel_id=1, source_target_pairs={{0,1},{1,0},{2,3},{3,2},{4,5},{5,4},{6,7},{7,6},{8,9},{9,8},{10,11... | collective-permute-start | bytes 6152 | tf_op jit(solution)/shard_map/ppermute | solution.py:40
  41.3 5.4 %collective-permute-start.18 = (f32[1,512]{1,0:T(1,128)S(1)}, f32[1,512]{1,0:T(1,128)S(1)}, u32[]{:S(2)}, u32[]{:S(2)}) collective-permute-start(f32[1,512]{1,0:T(1,128)S(1)} %add.53), channel_id=1, source_target_pairs={{0,6},{1,7},{2,4},{3,5},{4,2},{5,3},{6,0},{7,1},{8,14},{9,15},{10,... | collective-permute-start | bytes 6152 | tf_op jit(solution)/shard_map/ppermute | solution.py:36
  43.8 4.5 %collective-permute-start.19 = (f32[1,512]{1,0:T(1,128)S(1)}, f32[1,512]{1,0:T(1,128)S(1)}, u32[]{:S(2)}, u32[]{:S(2)}) collective-permute-start(f32[1,512]{1,0:T(1,128)S(1)} %add.53), channel_id=1, source_target_pairs={{0,4},{1,5},{2,6},{3,7},{4,0},{5,1},{6,2},{7,3},{8,12},{9,13},{10,... | collective-permute-start | bytes 6152 | tf_op jit(solution)/shard_map/ppermute | solution.py:36
  44.8 3.6 %collective-permute-start.20 = (f32[1,512]{1,0:T(1,128)S(1)}, f32[1,512]{1,0:T(1,128)S(1)}, u32[]{:S(2)}, u32[]{:S(2)}) collective-permute-start(f32[1,512]{1,0:T(1,128)S(1)} %add.53), channel_id=1, source_target_pairs={{0,2},{1,3},{2,0},{3,1},{4,6},{5,7},{6,4},{7,5},{8,10},{9,11},{10,... | collective-permute-start | bytes 6152 | tf_op jit(solution)/shard_map/ppermute | solution.py:36

commit v8 on v6

--- a/solution.py
+++ b/solution.py
@@ -292,7 +292,7 @@
         16,
     )
     far, sums = lax.optimization_barrier((far, sums))
-    cut = 5 * block // 8
+    cut = 9 * block // 16
     last = [send(first[:cut], (2, 1)), send(first[cut:], (2, 1))]
     sums, unit_proto, weights = call(
         first_kernel,
@@ -323,9 +323,10 @@
 
     def around(value):
         total = value + swap_cores(value)
-        for other in reversed(from_others(total, "proto", 2, z_count)):
+        *others, nearest = reversed(from_others(total, "proto", 2, z_count))
+        for other in others:
             total = lax.optimization_barrier(total + other)
-        return [total]
+        return [total, nearest]
 
     parts = around(*row_sums)
     for step in range(1, ITERS):

time: 50 us -> 50 us (level)
  no operation moved by 1% of the time
where the time goes in v8:
time: 50 us; the launch traced here: 49.8 us
  starting transfers between devices  22.1 us (44%)
  waiting for transfers between devices  14.8 us (30%)
  Pallas kernels  12.7 us (25%)
    ppermute x9, starting transfers between devices, from_others(): lax.ppermute(value, axis, partners(size, stride, count, step))  13.3 us
    pallas_call x9, Pallas kernels, call(): pl.pallas_call(kernel, out_shape=[VMEM(shape, dtype) for shape, dtype in...  9.86 us
    ppermute x6, starting transfers between devices, send(): return lax.ppermute(value, ('batch', 'proto'), by_core(steps))  8.22 us
    ppermute x9, waiting for transfers between devices, from_others(): lax.ppermute(value, axis, partners(size, stride, count, step))  7.23 us
    ppermute x6, waiting for transfers between devices, send(): return lax.ppermute(value, ('batch', 'proto'), by_core(steps))  4.35 us
    ppermute x5, waiting for transfers between devices, swap_cores(): lax.ppermute(value, 'proto', partners(lax.axis_size('proto'), 1, 2, 1))  3.18 us
    pallas_call x1, Pallas kernels, whole_plan(): pl.pallas_call(functools.partial(last_kernel, len(parts), block), out_sha...  1.5 us
    pallas_call x1, Pallas kernels, whole_plan(): pl.pallas_call(unit_kernel, out_shape=[VMEM((block, depth), bf16)] * 2, i...  1.31 us
  transfers between devices with their start and end apart: 20, of which 13 were waited for; matrix products, arithmetic and copies ran while one was open for 0% of the time, Pallas kernels for 14%

profile of v8, /device:TPU:0, one launch (start us, length us, event | category | flops | bytes accessed | tf_op | source)
XLA Modules:
  0.0 49.8 jit_solution(2901112110386647772)
XLA Ops:
  0.0 2.9 %collective-permute-start.2 = (bf16[512,256]{1,0:T(8,128)(2,1)}, bf16[512,256]{1,0:T(8,128)(2,1)S(1)}, u32[]{:S(2)}, u32[]{:S(2)}) collective-permute-start(bf16[512,256]{1,0:T(8,128)(2,1)} %feats.1), channel_id=1, source_target_pairs={{0,8},{1,17},{2,10},{3,19},{4,12},{5,21},{6,14},{7,23},{8,0},{9,25... | collective-permute-start | bytes 786440 | tf_op jit(solution)/shard_map/ppermute | solution.py:256
  2.9 1.3 %shard_map.28 = (bf16[512,256]{1,0:T(8,128)(2,1)S(1)}, bf16[512,256]{1,0:T(8,128)(2,1)S(1)}) custom-call(bf16[512,256]{1,0:T(8,128)(2,1)} %feats.1, bf16[512,256]{1,0:T(8,128)(2,1)} %protos.1), custom_call_target="tpu_custom_call" | custom-call | flops 1 | bytes 1 | tf_op jit(solution)/shard_map/pallas_call | solution.py:273
  4.3 3.2 %collective-permute-done.2.near = bf16[512,256]{1,0:T(8,128)(2,1)S(1)} collective-permute-done((bf16[512,256]{1,0:T(8,128)(2,1)}, bf16[512,256]{1,0:T(8,128)(2,1)S(1)}, u32[]{:S(2)}, u32[]{:S(2)}) %collective-permute-start.2) | collective-permute-done | bytes 262176 | tf_op jit(solution)/shard_map/ppermute | solution.py:256
  7.5 2.1 %collective-permute-start.3 = (bf16[256,256]{1,0:T(8,128)(2,1)S(1)}, bf16[256,256]{1,0:T(8,128)(2,1)S(1)}, u32[]{:S(2)}, u32[]{:S(2)}) collective-permute-start(bf16[256,256]{1,0:T(8,128)(2,1)S(1)} %constant_dynamic-slice_fusion), channel_id=1, source_target_pairs={{0,16},{1,9},{2,18},{3,11},{4,20},{5,13},{6,22},{7,15},{8,24},{9,1... | collective-permute-start | bytes 393224 | tf_op jit(solution)/shard_map/ppermute | solution.py:256
  9.7 1.0 %collective-permute-done.first = bf16[512,256]{1,0:T(8,128)(2,1)S(1)} collective-permute-done((bf16[512,256]{1,0:T(8,128)(2,1)S(1)}, bf16[512,256]{1,0:T(8,128)(2,1)S(1)}, u32[]{:S(2)}, u32[]{:S(2)}) %collective-permute-start) | collective-permute-done | bytes 262176 | tf_op jit(solution)/shard_map/ppermute | solution.py:256
  10.7 1.7 %collective-permute-start.6 = (bf16[288,256]{1,0:T(8,128)(2,1)S(1)}, bf16[288,256]{1,0:T(8,128)(2,1)S(1)}, u32[]{:S(2)}, u32[]{:S(2)}) collective-permute-start(bf16[288,256]{1,0:T(8,128)(2,1)S(1)} %slice.9), channel_id=1, source_target_pairs={{0,16},{1,9},{2,18},{3,11},{4,20},{5,13},{6,22},{7,15},{8,24},{9,1... | collective-permute-start | bytes 442376 | tf_op jit(solution)/shard_map/ppermute | solution.py:256
  12.4 0.8 %shard_map.29 = (bf16[2048,256]{1,0:T(8,128)(2,1)S(1)}, bf16[2048,256]{1,0:T(8,128)(2,1)S(1)}, f32[2048,2048]{1,0:T(8,128)S(1)}, f32[2048,128]{1,0:T(8,128)S(1)}) custom-call(bf16[512,256]{1,0:T(8,128)(2,1)S(1)} %get-tuple-element.36.own_feat, bf16[512,256]{1,0:T(8,128)(2,1)S(1)} %collective-permute-done.2.near, ...), custom_call_target="tpu_custom_call" | custom-call | flops 1 | bytes 1 | tf_op jit(solution)/shard_map/pallas_call | solution.py:84
  13.4 1.3 %collective-permute-start.1 = (bf16[224,256]{1,0:T(8,128)(2,1)S(1)}, bf16[224,256]{1,0:T(8,128)(2,1)S(1)}, u32[]{:S(2)}, u32[]{:S(2)}) collective-permute-start(bf16[224,256]{1,0:T(8,128)(2,1)S(1)} %slice.8), channel_id=1, source_target_pairs={{0,16},{1,9},{2,18},{3,11},{4,20},{5,13},{6,22},{7,15},{8,24},{9,1... | collective-permute-start | bytes 344072 | tf_op jit(solution)/shard_map/ppermute | solution.py:256
  14.7 0.6 %shard_map.30 = (f32[2048,128]{1,0:T(8,128)S(1)}, bf16[2048,256]{1,0:T(8,128)(2,1)S(1)}, f32[2048,2048]{1,0:T(8,128)S(1)}) custom-call(bf16[512,256]{1,0:T(8,128)(2,1)S(1)} %collective-permute-done.first, f32[2048,128]{1,0:T(8,128)S(1)} %get-tuple-element.40.sums_in, ...), custom_call_target="tpu_custom_call", output_to_operand_aliasing={{0}: (1, {}), {1}: (3, {}), {2}: (4, {})} | custom-call | flops 1 | bytes 1 | tf_op jit(solution)/shard_map/pallas_call | solution.py:84
  15.3 1.4 %shard_map.31 = (bf16[2048,256]{1,0:T(8,128)(2,1)S(1)}, f32[2048,2048]{1,0:T(8,128)S(1)}, f32[8,2048]{1,0:T(8,128)S(1)}) custom-call(bf16[256,256]{1,0:T(8,128)(2,1)S(1)} %collective-permute-done.3.far, bf16[256,256]{1,0:T(8,128)(2,1)S(1)} %collective-permute-done.5.far_swapped, ...), custom_call_target="tpu_custom_call", output_to_operand_aliasing={{0}: (4, {}), {1}: (5, {})} | custom-call | flops 1 | bytes 1 | tf_op jit(solution)/shard_map/pallas_call | solution.py:84
  16.8 1.1 %shard_map.32 = (bf16[2048,256]{1,0:T(8,128)(2,1)S(1)}, f32[2048,2048]{1,0:T(8,128)S(1)}, f32[8,2048]{1,0:T(8,128)S(1)}) custom-call(bf16[512,256]{1,0:T(8,128)(2,1)S(1)} %collective-permute-done.7.ready, bf16[2048,256]{1,0:T(8,128)(2,1)S(1)} %get-tuple-element.47.unit_feat, ...), custom_call_target="tpu_custom_call", output_to_operand_aliasing={{0}: (2, {}), {1}: (3, {}), {2}: (4, {})} | custom-call | flops 1 | bytes 1 | tf_op jit(solution)/shard_map/pallas_call | solution.py:84
  17.9 0.7 %shard_map.33 = (bf16[2048,256]{1,0:T(8,128)(2,1)S(1)}, f32[2048,2048]{1,0:T(8,128)S(1)}, f32[8,2048]{1,0:T(8,128)S(1)}) custom-call(bf16[288,256]{1,0:T(8,128)(2,1)S(1)} %collective-permute-done.6.ready, bf16[2048,256]{1,0:T(8,128)(2,1)S(1)} %get-tuple-element.47.unit_feat, ...), custom_call_target="tpu_custom_call", output_to_operand_aliasing={{0}: (2, {}), {1}: (3, {}), {2}: (4, {})} | custom-call | flops 1 | bytes 1 | tf_op jit(solution)/shard_map/pallas_call | solution.py:84
  18.8 0.7 %shard_map.34 = (bf16[2048,256]{1,0:T(8,128)(2,1)S(1)}, f32[2048,2048]{1,0:T(8,128)S(1)}, f32[8,2048]{1,0:T(8,128)S(1)}, f32[1,2048]{1,0:T(1,128)S(1)}) custom-call(bf16[224,256]{1,0:T(8,128)(2,1)S(1)} %collective-permute-done.1.ready, bf16[2048,256]{1,0:T(8,128)(2,1)S(1)} %get-tuple-element.47.unit_feat, ...), custom_call_target="tpu_custom_call", output_to_operand_aliasing={{0}: (2, {}), {1}: (3, {}), {2}: (4, {})} | custom-call | flops 1 | bytes 1 | tf_op jit(solution)/shard_map/pallas_call | solution.py:84
  19.9 0.9 %collective-permute-done.8 = f32[1,2048]{1,0:T(1,128)S(1)} collective-permute-done((f32[1,2048]{1,0:T(1,128)S(1)}, f32[1,2048]{1,0:T(1,128)S(1)}, u32[]{:S(2)}, u32[]{:S(2)}) %collective-permute-start.8) | collective-permute-done | bytes 8224 | tf_op jit(solution)/shard_map/ppermute | solution.py:40
  20.7 3.7 %collective-permute-start.9 = (f32[1,2048]{1,0:T(1,128)S(1)}, f32[1,2048]{1,0:T(1,128)S(1)}, u32[]{:S(2)}, u32[]{:S(2)}) collective-permute-start(f32[1,2048]{1,0:T(1,128)S(1)} %add.36), channel_id=1, source_target_pairs={{0,6},{1,7},{2,4},{3,5},{4,2},{5,3},{6,0},{7,1},{8,14},{9,15},{10,... | collective-permute-start | bytes 24584 | tf_op jit(solution)/shard_map/ppermute | solution.py:36
  24.4 0.8 %collective-permute-start.11 = (f32[1,2048]{1,0:T(1,128)S(1)}, f32[1,2048]{1,0:T(1,128)S(1)}, u32[]{:S(2)}, u32[]{:S(2)}) collective-permute-start(f32[1,2048]{1,0:T(1,128)S(1)} %add.36), channel_id=1, source_target_pairs={{0,2},{1,3},{2,0},{3,1},{4,6},{5,7},{6,4},{7,5},{8,10},{9,11},{10,... | collective-permute-start | bytes 24584 | tf_op jit(solution)/shard_map/ppermute | solution.py:36
  25.2 1.1 %collective-permute-done.9 = f32[1,2048]{1,0:T(1,128)S(1)} collective-permute-done((f32[1,2048]{1,0:T(1,128)S(1)}, f32[1,2048]{1,0:T(1,128)S(1)}, u32[]{:S(2)}, u32[]{:S(2)}) %collective-permute-start.9) | collective-permute-done | bytes 8224 | tf_op jit(solution)/shard_map/ppermute | solution.py:36
  26.3 2.7 %collective-permute-done.10 = f32[1,2048]{1,0:T(1,128)S(1)} collective-permute-done((f32[1,2048]{1,0:T(1,128)S(1)}, f32[1,2048]{1,0:T(1,128)S(1)}, u32[]{:S(2)}, u32[]{:S(2)}) %collective-permute-start.10) | collective-permute-done | bytes 8224 | tf_op jit(solution)/shard_map/ppermute | solution.py:36
  29.0 2.2 %shard_map.35 = f32[1,2048]{1,0:T(1,128)S(1)} custom-call(f32[1,2048]{1,0:T(1,128)S(1)} %add.38.refs_0_, f32[1,2048]{1,0:T(1,128)S(1)} %collective-permute-done.11.refs_1_, f32[2048,2048]{1,0:T(8,128)S(1)} %get-tuple-element.57.refs_2_), custom_call_target="tpu_custom_call" | custom-call | flops 16777216 | bytes 1 | tf_op jit(solution)/shard_map/pallas_call | solution.py:84
  31.3 1.2 %collective-permute-done.12 = f32[1,2048]{1,0:T(1,128)S(1)} collective-permute-done((f32[1,2048]{1,0:T(1,128)S(1)}, f32[1,2048]{1,0:T(1,128)S(1)}, u32[]{:S(2)}, u32[]{:S(2)}) %collective-permute-start.12) | collective-permute-done | bytes 8224 | tf_op jit(solution)/shard_map/ppermute | solution.py:40
  32.5 1.5 %collective-permute-start.13 = (f32[1,2048]{1,0:T(1,128)S(1)}, f32[1,2048]{1,0:T(1,128)S(1)}, u32[]{:S(2)}, u32[]{:S(2)}) collective-permute-start(f32[1,2048]{1,0:T(1,128)S(1)} %add.39), channel_id=1, source_target_pairs={{0,6},{1,7},{2,4},{3,5},{4,2},{5,3},{6,0},{7,1},{8,14},{9,15},{10,... | collective-permute-start | bytes 24584 | tf_op jit(solution)/shard_map/ppermute | solution.py:36
  34.0 0.6 %collective-permute-start.14 = (f32[1,2048]{1,0:T(1,128)S(1)}, f32[1,2048]{1,0:T(1,128)S(1)}, u32[]{:S(2)}, u32[]{:S(2)}) collective-permute-start(f32[1,2048]{1,0:T(1,128)S(1)} %add.39), channel_id=1, source_target_pairs={{0,4},{1,5},{2,6},{3,7},{4,0},{5,1},{6,2},{7,3},{8,12},{9,13},{10,... | collective-permute-start | bytes 24584 | tf_op jit(solution)/shard_map/ppermute | solution.py:36
  34.6 2.3 %collective-permute-start.15 = (f32[1,2048]{1,0:T(1,128)S(1)}, f32[1,2048]{1,0:T(1,128)S(1)}, u32[]{:S(2)}, u32[]{:S(2)}) collective-permute-start(f32[1,2048]{1,0:T(1,128)S(1)} %add.39), channel_id=1, source_target_pairs={{0,2},{1,3},{2,0},{3,1},{4,6},{5,7},{6,4},{7,5},{8,10},{9,11},{10,... | collective-permute-start | bytes 24584 | tf_op jit(solution)/shard_map/ppermute | solution.py:36
  36.9 1.1 %collective-permute-done.13 = f32[1,2048]{1,0:T(1,128)S(1)} collective-permute-done((f32[1,2048]{1,0:T(1,128)S(1)}, f32[1,2048]{1,0:T(1,128)S(1)}, u32[]{:S(2)}, u32[]{:S(2)}) %collective-permute-start.13) | collective-permute-done | bytes 8224 | tf_op jit(solution)/shard_map/ppermute | solution.py:36
  38.6 1.4 %shard_map.36 = (f32[1,512]{1,0:T(1,128)S(1)}, f32[2048,128]{1,0:T(8,128)S(1)}) custom-call(f32[1,2048]{1,0:T(1,128)S(1)} %add.41.refs_0_, f32[1,2048]{1,0:T(1,128)S(1)} %collective-permute-done.15.refs_1_, f32[2048,2048]{1,0:T(8,128)S(1)} %get-tuple-element.57.refs_2_), custom_call_target="tpu_custom_call" | custom-call | flops 16777216 | bytes 1 | tf_op jit(solution)/shard_map/pallas_call | solution.py:84
  40.2 1.1 %collective-permute-done.16 = f32[1,512]{1,0:T(1,128)S(1)} collective-permute-done((f32[1,512]{1,0:T(1,128)S(1)}, f32[1,512]{1,0:T(1,128)S(1)}, u32[]{:S(2)}, u32[]{:S(2)}) %collective-permute-start.16) | collective-permute-done | bytes 2080 | tf_op jit(solution)/shard_map/ppermute | solution.py:40
  41.3 2.5 %collective-permute-start.17 = (f32[1,512]{1,0:T(1,128)S(1)}, f32[1,512]{1,0:T(1,128)S(1)}, u32[]{:S(2)}, u32[]{:S(2)}) collective-permute-start(f32[1,512]{1,0:T(1,128)S(1)} %add.42), channel_id=1, source_target_pairs={{0,6},{1,7},{2,4},{3,5},{4,2},{5,3},{6,0},{7,1},{8,14},{9,15},{10,... | collective-permute-start | bytes 6152 | tf_op jit(solution)/shard_map/ppermute | solution.py:36
  43.8 0.9 %collective-permute-start.18 = (f32[1,512]{1,0:T(1,128)S(1)}, f32[1,512]{1,0:T(1,128)S(1)}, u32[]{:S(2)}, u32[]{:S(2)}) collective-permute-start(f32[1,512]{1,0:T(1,128)S(1)} %add.42), channel_id=1, source_target_pairs={{0,4},{1,5},{2,6},{3,7},{4,0},{5,1},{6,2},{7,3},{8,12},{9,13},{10,... | collective-permute-start | bytes 6152 | tf_op jit(solution)/shard_map/ppermute | solution.py:36
  44.7 1.0 %collective-permute-start.19 = (f32[1,512]{1,0:T(1,128)S(1)}, f32[1,512]{1,0:T(1,128)S(1)}, u32[]{:S(2)}, u32[]{:S(2)}) collective-permute-start(f32[1,512]{1,0:T(1,128)S(1)} %add.42), channel_id=1, source_target_pairs={{0,2},{1,3},{2,0},{3,1},{4,6},{5,7},{6,4},{7,5},{8,10},{9,11},{10,... | collective-permute-start | bytes 6152 | tf_op jit(solution)/shard_map/ppermute | solution.py:36
  45.7 0.8 %shard_map.37.refs_2_ = f32[512,2048]{1,0:T(8,128)S(1)} custom-call(bf16[2048,256]{1,0:T(8,128)(2,1)S(1)} %get-tuple-element.47.unit_feat, bf16[2048,256]{1,0:T(8,128)(2,1)S(1)} %get-tuple-element.59.unit_proto, f32[2048,128]{1,0:T(8,128)S(1)} %get-tuple-element.60.col_factor), custom_call_target="tpu_custom_call" | custom-call | flops 536870912 | bytes 1 | tf_op jit(solution)/shard_map/pallas_call | solution.py:84
  46.7 1.6 %collective-permute-done.18 = f32[1,512]{1,0:T(1,128)S(1)} collective-permute-done((f32[1,512]{1,0:T(1,128)S(1)}, f32[1,512]{1,0:T(1,128)S(1)}, u32[]{:S(2)}, u32[]{:S(2)}) %collective-permute-start.18) | collective-permute-done | bytes 2080 | tf_op jit(solution)/shard_map/ppermute | solution.py:36
  48.3 1.5 %shard_map.38 = bf16[512,2048]{1,0:T(8,128)(2,1)} custom-call(f32[1,512]{1,0:T(1,128)S(1)} %add.44.refs_0_, f32[1,512]{1,0:T(1,128)S(1)} %collective-permute-done.19.refs_1_, f32[512,2048]{1,0:T(8,128)S(1)} %shard_map.37.refs_2_), custom_call_target="tpu_custom_call" | custom-call | tf_op jit(solution)/shard_map/pallas_call | solution.py:352
  (31 shorter events, 1.8 us)
Async XLA Ops:
  0.0 7.5 %collective-permute-start.2 = (bf16[512,256]{1,0:T(8,128)(2,1)}, bf16[512,256]{1,0:T(8,128)(2,1)S(1)}, u32[]{:S(2)}, u32[]{:S(2)}) collective-permute-start(bf16[512,256]{1,0:T(8,128)(2,1)} %feats.1), channel_id=1, source_target_pairs={{0,8},{1,17},{2,10},{3,19},{4,12},{5,21},{6,14},{7,23},{8,0},{9,25... | collective-permute-start | bytes 786440 | tf_op jit(solution)/shard_map/ppermute | solution.py:256
  4.3 6.4 %collective-permute-start = (bf16[512,256]{1,0:T(8,128)(2,1)S(1)}, bf16[512,256]{1,0:T(8,128)(2,1)S(1)}, u32[]{:S(2)}, u32[]{:S(2)}) collective-permute-start(bf16[512,256]{1,0:T(8,128)(2,1)S(1)} %get-tuple-element.37.own_proto), channel_id=1, source_target_pairs={{0,8},{1,17},{2,10},{3,19},{4,12},{5,21},{6,14},{7,23},{8,0},{9,25... | collective-permute-start | bytes 786440 | tf_op jit(solution)/shard_map/ppermute | solution.py:256
  7.5 4.9 %collective-permute-start.4 = (bf16[512,256]{1,0:T(8,128)(2,1)S(1)}, bf16[512,256]{1,0:T(8,128)(2,1)S(1)}, u32[]{:S(2)}, u32[]{:S(2)}) collective-permute-start(bf16[512,256]{1,0:T(8,128)(2,1)S(1)} %collective-permute-done.2.near), channel_id=1, source_target_pairs={{0,1},{1,0},{2,3},{3,2},{4,5},{5,4},{6,7},{7,6},{8,9},{9,8},{10,11... | collective-permute-start | bytes 786440 | tf_op jit(solution)/shard_map/ppermute | solution.py:40
  7.5 5.8 %collective-permute-start.3 = (bf16[256,256]{1,0:T(8,128)(2,1)S(1)}, bf16[256,256]{1,0:T(8,128)(2,1)S(1)}, u32[]{:S(2)}, u32[]{:S(2)}) collective-permute-start(bf16[256,256]{1,0:T(8,128)(2,1)S(1)} %constant_dynamic-slice_fusion), channel_id=1, source_target_pairs={{0,16},{1,9},{2,18},{3,11},{4,20},{5,13},{6,22},{7,15},{8,24},{9,1... | collective-permute-start | bytes 393224 | tf_op jit(solution)/shard_map/ppermute | solution.py:256
  9.6 7.1 %collective-permute-start.7 = (bf16[512,256]{1,0:T(8,128)(2,1)S(1)}, bf16[512,256]{1,0:T(8,128)(2,1)S(1)}, u32[]{:S(2)}, u32[]{:S(2)}) collective-permute-start(bf16[512,256]{1,0:T(8,128)(2,1)S(1)} %get-tuple-element.37.own_proto), channel_id=1, source_target_pairs={{0,16},{1,9},{2,18},{3,11},{4,20},{5,13},{6,22},{7,15},{8,24},{9,1... | collective-permute-start | bytes 786440 | tf_op jit(solution)/shard_map/ppermute | solution.py:256
  10.7 7.2 %collective-permute-start.6 = (bf16[288,256]{1,0:T(8,128)(2,1)S(1)}, bf16[288,256]{1,0:T(8,128)(2,1)S(1)}, u32[]{:S(2)}, u32[]{:S(2)}) collective-permute-start(bf16[288,256]{1,0:T(8,128)(2,1)S(1)} %slice.9), channel_id=1, source_target_pairs={{0,16},{1,9},{2,18},{3,11},{4,20},{5,13},{6,22},{7,15},{8,24},{9,1... | collective-permute-start | bytes 442376 | tf_op jit(solution)/shard_map/ppermute | solution.py:256
  13.3 2.0 %collective-permute-start.5 = (bf16[256,256]{1,0:T(8,128)(2,1)S(1)}, bf16[256,256]{1,0:T(8,128)(2,1)S(1)}, u32[]{:S(2)}, u32[]{:S(2)}) collective-permute-start(bf16[256,256]{1,0:T(8,128)(2,1)S(1)} %collective-permute-done.3.far), channel_id=1, source_target_pairs={{0,1},{1,0},{2,3},{3,2},{4,5},{5,4},{6,7},{7,6},{8,9},{9,8},{10,11... | collective-permute-start | bytes 393224 | tf_op jit(solution)/shard_map/ppermute | solution.py:40
  13.4 5.4 %collective-permute-start.1 = (bf16[224,256]{1,0:T(8,128)(2,1)S(1)}, bf16[224,256]{1,0:T(8,128)(2,1)S(1)}, u32[]{:S(2)}, u32[]{:S(2)}) collective-permute-start(bf16[224,256]{1,0:T(8,128)(2,1)S(1)} %slice.8), channel_id=1, source_target_pairs={{0,16},{1,9},{2,18},{3,11},{4,20},{5,13},{6,22},{7,15},{8,24},{9,1... | collective-permute-start | bytes 344072 | tf_op jit(solution)/shard_map/ppermute | solution.py:256
  19.5 1.2 %collective-permute-start.8 = (f32[1,2048]{1,0:T(1,128)S(1)}, f32[1,2048]{1,0:T(1,128)S(1)}, u32[]{:S(2)}, u32[]{:S(2)}) collective-permute-start(f32[1,2048]{1,0:T(1,128)S(1)} %get-tuple-element.56), channel_id=1, source_target_pairs={{0,1},{1,0},{2,3},{3,2},{4,5},{5,4},{6,7},{7,6},{8,9},{9,8},{10,11... | collective-permute-start | bytes 24584 | tf_op jit(solution)/shard_map/ppermute | solution.py:40
  20.7 5.5 %collective-permute-start.9 = (f32[1,2048]{1,0:T(1,128)S(1)}, f32[1,2048]{1,0:T(1,128)S(1)}, u32[]{:S(2)}, u32[]{:S(2)}) collective-permute-start(f32[1,2048]{1,0:T(1,128)S(1)} %add.36), channel_id=1, source_target_pairs={{0,6},{1,7},{2,4},{3,5},{4,2},{5,3},{6,0},{7,1},{8,14},{9,15},{10,... | collective-permute-start | bytes 24584 | tf_op jit(solution)/shard_map/ppermute | solution.py:36
  24.4 4.5 %collective-permute-start.10 = (f32[1,2048]{1,0:T(1,128)S(1)}, f32[1,2048]{1,0:T(1,128)S(1)}, u32[]{:S(2)}, u32[]{:S(2)}) collective-permute-start(f32[1,2048]{1,0:T(1,128)S(1)} %add.36), channel_id=1, source_target_pairs={{0,4},{1,5},{2,6},{3,7},{4,0},{5,1},{6,2},{7,3},{8,12},{9,13},{10,... | collective-permute-start | bytes 24584 | tf_op jit(solution)/shard_map/ppermute | solution.py:36
  24.4 4.6 %collective-permute-start.11 = (f32[1,2048]{1,0:T(1,128)S(1)}, f32[1,2048]{1,0:T(1,128)S(1)}, u32[]{:S(2)}, u32[]{:S(2)}) collective-permute-start(f32[1,2048]{1,0:T(1,128)S(1)} %add.36), channel_id=1, source_target_pairs={{0,2},{1,3},{2,0},{3,1},{4,6},{5,7},{6,4},{7,5},{8,10},{9,11},{10,... | collective-permute-start | bytes 24584 | tf_op jit(solution)/shard_map/ppermute | solution.py:36
  31.2 1.2 %collective-permute-start.12 = (f32[1,2048]{1,0:T(1,128)S(1)}, f32[1,2048]{1,0:T(1,128)S(1)}, u32[]{:S(2)}, u32[]{:S(2)}) collective-permute-start(f32[1,2048]{1,0:T(1,128)S(1)} %shard_map.35), channel_id=1, source_target_pairs={{0,1},{1,0},{2,3},{3,2},{4,5},{5,4},{6,7},{7,6},{8,9},{9,8},{10,11... | collective-permute-start | bytes 24584 | tf_op jit(solution)/shard_map/ppermute | solution.py:40
  32.5 5.6 %collective-permute-start.13 = (f32[1,2048]{1,0:T(1,128)S(1)}, f32[1,2048]{1,0:T(1,128)S(1)}, u32[]{:S(2)}, u32[]{:S(2)}) collective-permute-start(f32[1,2048]{1,0:T(1,128)S(1)} %add.39), channel_id=1, source_target_pairs={{0,6},{1,7},{2,4},{3,5},{4,2},{5,3},{6,0},{7,1},{8,14},{9,15},{10,... | collective-permute-start | bytes 24584 | tf_op jit(solution)/shard_map/ppermute | solution.py:36
  34.0 4.6 %collective-permute-start.14 = (f32[1,2048]{1,0:T(1,128)S(1)}, f32[1,2048]{1,0:T(1,128)S(1)}, u32[]{:S(2)}, u32[]{:S(2)}) collective-permute-start(f32[1,2048]{1,0:T(1,128)S(1)} %add.39), channel_id=1, source_target_pairs={{0,4},{1,5},{2,6},{3,7},{4,0},{5,1},{6,2},{7,3},{8,12},{9,13},{10,... | collective-permute-start | bytes 24584 | tf_op jit(solution)/shard_map/ppermute | solution.py:36
  34.6 4.0 %collective-permute-start.15 = (f32[1,2048]{1,0:T(1,128)S(1)}, f32[1,2048]{1,0:T(1,128)S(1)}, u32[]{:S(2)}, u32[]{:S(2)}) collective-permute-start(f32[1,2048]{1,0:T(1,128)S(1)} %add.39), channel_id=1, source_target_pairs={{0,2},{1,3},{2,0},{3,1},{4,6},{5,7},{6,4},{7,5},{8,10},{9,11},{10,... | collective-permute-start | bytes 24584 | tf_op jit(solution)/shard_map/ppermute | solution.py:36
  40.1 1.2 %collective-permute-start.16 = (f32[1,512]{1,0:T(1,128)S(1)}, f32[1,512]{1,0:T(1,128)S(1)}, u32[]{:S(2)}, u32[]{:S(2)}) collective-permute-start(f32[1,512]{1,0:T(1,128)S(1)} %get-tuple-element.58), channel_id=1, source_target_pairs={{0,1},{1,0},{2,3},{3,2},{4,5},{5,4},{6,7},{7,6},{8,9},{9,8},{10,11... | collective-permute-start | bytes 6152 | tf_op jit(solution)/shard_map/ppermute | solution.py:40
  41.3 5.4 %collective-permute-start.17 = (f32[1,512]{1,0:T(1,128)S(1)}, f32[1,512]{1,0:T(1,128)S(1)}, u32[]{:S(2)}, u32[]{:S(2)}) collective-permute-start(f32[1,512]{1,0:T(1,128)S(1)} %add.42), channel_id=1, source_target_pairs={{0,6},{1,7},{2,4},{3,5},{4,2},{5,3},{6,0},{7,1},{8,14},{9,15},{10,... | collective-permute-start | bytes 6152 | tf_op jit(solution)/shard_map/ppermute | solution.py:36
  43.8 4.5 %collective-permute-start.18 = (f32[1,512]{1,0:T(1,128)S(1)}, f32[1,512]{1,0:T(1,128)S(1)}, u32[]{:S(2)}, u32[]{:S(2)}) collective-permute-start(f32[1,512]{1,0:T(1,128)S(1)} %add.42), channel_id=1, source_target_pairs={{0,4},{1,5},{2,6},{3,7},{4,0},{5,1},{6,2},{7,3},{8,12},{9,13},{10,... | collective-permute-start | bytes 6152 | tf_op jit(solution)/shard_map/ppermute | solution.py:36
  44.7 3.6 %collective-permute-start.19 = (f32[1,512]{1,0:T(1,128)S(1)}, f32[1,512]{1,0:T(1,128)S(1)}, u32[]{:S(2)}, u32[]{:S(2)}) collective-permute-start(f32[1,512]{1,0:T(1,128)S(1)} %add.42), channel_id=1, source_target_pairs={{0,2},{1,3},{2,0},{3,1},{4,6},{5,7},{6,4},{7,5},{8,10},{9,11},{10,... | collective-permute-start | bytes 6152 | tf_op jit(solution)/shard_map/ppermute | solution.py:36

commit v9 on v7

--- a/solution.py
+++ b/solution.py
@@ -296,7 +296,7 @@
         16,
     )
     far, sums = lax.optimization_barrier((far, sums))
-    cut = 11 * block // 16
+    cut = 5 * block // 8
     last = [send(first[:cut], (2, 1)), send(first[cut:], (2, 1))]
     sums, unit_proto, weights = call(
         first_kernel,
@@ -328,9 +328,11 @@
 
     def around(value):
         total = value + swap_cores(value)
-        for other in reversed(from_others(total, "proto", 2, z_count)):
+        far, *others = reversed(from_others(total, "proto", 2, z_count))
+        total = lax.optimization_barrier(total + far)
+        for other in others[:-1]:
             total = lax.optimization_barrier(total + other)
-        return [total]
+        return [total, others[-1]]
 
     parts = around(*row_sums)
     for step in range(1, ITERS):

time: 50 us -> 50 us (level)
  transfers between devices with their start and end apart: 21 -> 21, of which waited for: 16 -> 15; matrix products, arithmetic and copies ran while one was open for 0% -> 0% of each run, Pallas kernels for 14% -> 14%
where the time goes in v9:
time: 50 us; the launch traced here: 49.8 us
  starting transfers between devices  21.5 us (43%)
  waiting for transfers between devices  15.3 us (31%)
  Pallas kernels  12.7 us (25%)
    ppermute x9, starting transfers between devices, from_others(): lax.ppermute(value, axis, partners(size, stride, count, step))  13.3 us
    pallas_call x9, Pallas kernels, call(): pl.pallas_call(kernel, out_shape=[VMEM(shape, dtype) for shape, dtype in...  9.91 us
    ppermute x6, starting transfers between devices, send(): return lax.ppermute(value, ('batch', 'proto'), by_core(steps))  7.36 us
    ppermute x9, waiting for transfers between devices, from_others(): lax.ppermute(value, axis, partners(size, stride, count, step))  7.22 us
    ppermute x6, waiting for transfers between devices, send(): return lax.ppermute(value, ('batch', 'proto'), by_core(steps))  4.41 us
    ppermute x6, waiting for transfers between devices, swap_cores(): lax.ppermute(value, 'proto', partners(lax.axis_size('proto'), 1, 2, 1))  3.64 us
    pallas_call x1, Pallas kernels, whole_plan(): pl.pallas_call(functools.partial(last_kernel, len(parts), block), out_sha...  1.5 us
    pallas_call x1, Pallas kernels, whole_plan(): pl.pallas_call(unit_kernel, out_shape=[VMEM((block, depth), bf16)] * 2, i...  1.31 us
  transfers between devices with their start and end apart: 21, of which 15 were waited for; matrix products, arithmetic and copies ran while one was open for 0% of the time, Pallas kernels for 14%

profile of v9, /device:TPU:0, one launch (start us, length us, event | category | flops | bytes accessed | tf_op | source)
XLA Modules:
  0.0 49.8 jit_solution(1869562176395339347)
XLA Ops:
  0.0 2.9 %collective-permute-start.2 = (bf16[512,256]{1,0:T(8,128)(2,1)}, bf16[512,256]{1,0:T(8,128)(2,1)S(1)}, u32[]{:S(2)}, u32[]{:S(2)}) collective-permute-start(bf16[512,256]{1,0:T(8,128)(2,1)} %feats.1), channel_id=1, source_target_pairs={{0,8},{1,17},{2,10},{3,19},{4,12},{5,21},{6,14},{7,23},{8,0},{9,25... | collective-permute-start | bytes 786440 | tf_op jit(solution)/shard_map/ppermute | solution.py:260
  2.9 1.3 %shard_map.28 = (bf16[512,256]{1,0:T(8,128)(2,1)S(1)}, bf16[512,256]{1,0:T(8,128)(2,1)S(1)}) custom-call(bf16[512,256]{1,0:T(8,128)(2,1)} %feats.1, bf16[512,256]{1,0:T(8,128)(2,1)} %protos.1), custom_call_target="tpu_custom_call" | custom-call | flops 1 | bytes 1 | tf_op jit(solution)/shard_map/pallas_call | solution.py:277
  4.3 3.2 %collective-permute-done.2.near = bf16[512,256]{1,0:T(8,128)(2,1)S(1)} collective-permute-done((bf16[512,256]{1,0:T(8,128)(2,1)}, bf16[512,256]{1,0:T(8,128)(2,1)S(1)}, u32[]{:S(2)}, u32[]{:S(2)}) %collective-permute-start.2) | collective-permute-done | bytes 262176 | tf_op jit(solution)/shard_map/ppermute | solution.py:260
  7.5 2.1 %collective-permute-start.3 = (bf16[256,256]{1,0:T(8,128)(2,1)S(1)}, bf16[256,256]{1,0:T(8,128)(2,1)S(1)}, u32[]{:S(2)}, u32[]{:S(2)}) collective-permute-start(bf16[256,256]{1,0:T(8,128)(2,1)S(1)} %constant_dynamic-slice_fusion), channel_id=1, source_target_pairs={{0,16},{1,9},{2,18},{3,11},{4,20},{5,13},{6,22},{7,15},{8,24},{9,1... | collective-permute-start | bytes 393224 | tf_op jit(solution)/shard_map/ppermute | solution.py:260
  9.7 1.0 %collective-permute-done.first = bf16[512,256]{1,0:T(8,128)(2,1)S(1)} collective-permute-done((bf16[512,256]{1,0:T(8,128)(2,1)S(1)}, bf16[512,256]{1,0:T(8,128)(2,1)S(1)}, u32[]{:S(2)}, u32[]{:S(2)}) %collective-permute-start) | collective-permute-done | bytes 262176 | tf_op jit(solution)/shard_map/ppermute | solution.py:260
  10.7 1.7 %collective-permute-start.7 = (bf16[320,256]{1,0:T(8,128)(2,1)S(1)}, bf16[320,256]{1,0:T(8,128)(2,1)S(1)}, u32[]{:S(2)}, u32[]{:S(2)}) collective-permute-start(bf16[320,256]{1,0:T(8,128)(2,1)S(1)} %slice.17), channel_id=1, source_target_pairs={{0,16},{1,9},{2,18},{3,11},{4,20},{5,13},{6,22},{7,15},{8,24},{9,1... | collective-permute-start | bytes 491528 | tf_op jit(solution)/shard_map/ppermute | solution.py:260
  12.9 0.8 %shard_map.29 = (bf16[2048,256]{1,0:T(8,128)(2,1)S(1)}, bf16[2048,256]{1,0:T(8,128)(2,1)S(1)}, f32[2048,2048]{1,0:T(8,128)S(1)}, f32[2048,128]{1,0:T(8,128)S(1)}) custom-call(bf16[512,256]{1,0:T(8,128)(2,1)S(1)} %get-tuple-element.36.own_feat, bf16[512,256]{1,0:T(8,128)(2,1)S(1)} %collective-permute-done.2.near, ...), custom_call_target="tpu_custom_call" | custom-call | flops 1 | bytes 1 | tf_op jit(solution)/shard_map/pallas_call | solution.py:84
  13.8 0.5 collective-permute-start.6
  14.3 0.6 %shard_map.30 = (f32[2048,128]{1,0:T(8,128)S(1)}, bf16[2048,256]{1,0:T(8,128)(2,1)S(1)}, f32[2048,2048]{1,0:T(8,128)S(1)}) custom-call(bf16[512,256]{1,0:T(8,128)(2,1)S(1)} %collective-permute-done.first, f32[2048,128]{1,0:T(8,128)S(1)} %get-tuple-element.40.sums_in, ...), custom_call_target="tpu_custom_call", output_to_operand_aliasing={{0}: (1, {}), {1}: (3, {}), {2}: (4, {})} | custom-call | flops 1 | bytes 1 | tf_op jit(solution)/shard_map/pallas_call | solution.py:84
  15.2 1.4 %shard_map.31 = (bf16[2048,256]{1,0:T(8,128)(2,1)S(1)}, f32[2048,2048]{1,0:T(8,128)S(1)}, f32[8,2048]{1,0:T(8,128)S(1)}) custom-call(bf16[256,256]{1,0:T(8,128)(2,1)S(1)} %collective-permute-done.3.far, bf16[128,256]{1,0:T(8,128)(2,1)S(1)} %collective-permute-done.5.refs_0_, ...), custom_call_target="tpu_custom_call", output_to_operand_aliasing={{0}: (5, {}), {1}: (6, {})} | custom-call | flops 1 | bytes 1 | tf_op jit(solution)/shard_map/pallas_call | solution.py:84
  16.7 1.1 %shard_map.32 = (bf16[2048,256]{1,0:T(8,128)(2,1)S(1)}, f32[2048,2048]{1,0:T(8,128)S(1)}, f32[8,2048]{1,0:T(8,128)S(1)}) custom-call(bf16[512,256]{1,0:T(8,128)(2,1)S(1)} %collective-permute-done.8.ready, bf16[2048,256]{1,0:T(8,128)(2,1)S(1)} %get-tuple-element.47.unit_feat, ...), custom_call_target="tpu_custom_call", output_to_operand_aliasing={{0}: (2, {}), {1}: (3, {}), {2}: (4, {})} | custom-call | flops 1 | bytes 1 | tf_op jit(solution)/shard_map/pallas_call | solution.py:84
  17.8 0.7 %shard_map.33 = (bf16[2048,256]{1,0:T(8,128)(2,1)S(1)}, f32[2048,2048]{1,0:T(8,128)S(1)}, f32[8,2048]{1,0:T(8,128)S(1)}) custom-call(bf16[320,256]{1,0:T(8,128)(2,1)S(1)} %collective-permute-done.7.ready, bf16[2048,256]{1,0:T(8,128)(2,1)S(1)} %get-tuple-element.47.unit_feat, ...), custom_call_target="tpu_custom_call", output_to_operand_aliasing={{0}: (2, {}), {1}: (3, {}), {2}: (4, {})} | custom-call | flops 1 | bytes 1 | tf_op jit(solution)/shard_map/pallas_call | solution.py:84
  18.8 0.7 %shard_map.34 = (bf16[2048,256]{1,0:T(8,128)(2,1)S(1)}, f32[2048,2048]{1,0:T(8,128)S(1)}, f32[8,2048]{1,0:T(8,128)S(1)}, f32[1,2048]{1,0:T(1,128)S(1)}) custom-call(bf16[192,256]{1,0:T(8,128)(2,1)S(1)} %collective-permute-done.1.ready, bf16[2048,256]{1,0:T(8,128)(2,1)S(1)} %get-tuple-element.47.unit_feat, ...), custom_call_target="tpu_custom_call", output_to_operand_aliasing={{0}: (2, {}), {1}: (3, {}), {2}: (4, {})} | custom-call | flops 1 | bytes 1 | tf_op jit(solution)/shard_map/pallas_call | solution.py:84
  19.7 1.1 %collective-permute-done.9 = f32[1,2048]{1,0:T(1,128)S(1)} collective-permute-done((f32[1,2048]{1,0:T(1,128)S(1)}, f32[1,2048]{1,0:T(1,128)S(1)}, u32[]{:S(2)}, u32[]{:S(2)}) %collective-permute-start.9) | collective-permute-done | bytes 8224 | tf_op jit(solution)/shard_map/ppermute | solution.py:40
  20.8 3.7 %collective-permute-start.10 = (f32[1,2048]{1,0:T(1,128)S(1)}, f32[1,2048]{1,0:T(1,128)S(1)}, u32[]{:S(2)}, u32[]{:S(2)}) collective-permute-start(f32[1,2048]{1,0:T(1,128)S(1)} %add.36), channel_id=1, source_target_pairs={{0,6},{1,7},{2,4},{3,5},{4,2},{5,3},{6,0},{7,1},{8,14},{9,15},{10,... | collective-permute-start | bytes 24584 | tf_op jit(solution)/shard_map/ppermute | solution.py:36
  24.4 0.8 %collective-permute-start.12 = (f32[1,2048]{1,0:T(1,128)S(1)}, f32[1,2048]{1,0:T(1,128)S(1)}, u32[]{:S(2)}, u32[]{:S(2)}) collective-permute-start(f32[1,2048]{1,0:T(1,128)S(1)} %add.36), channel_id=1, source_target_pairs={{0,2},{1,3},{2,0},{3,1},{4,6},{5,7},{6,4},{7,5},{8,10},{9,11},{10,... | collective-permute-start | bytes 24584 | tf_op jit(solution)/shard_map/ppermute | solution.py:36
  25.2 1.1 %collective-permute-done.10 = f32[1,2048]{1,0:T(1,128)S(1)} collective-permute-done((f32[1,2048]{1,0:T(1,128)S(1)}, f32[1,2048]{1,0:T(1,128)S(1)}, u32[]{:S(2)}, u32[]{:S(2)}) %collective-permute-start.10) | collective-permute-done | bytes 8224 | tf_op jit(solution)/shard_map/ppermute | solution.py:36
  26.3 2.7 %collective-permute-done.11 = f32[1,2048]{1,0:T(1,128)S(1)} collective-permute-done((f32[1,2048]{1,0:T(1,128)S(1)}, f32[1,2048]{1,0:T(1,128)S(1)}, u32[]{:S(2)}, u32[]{:S(2)}) %collective-permute-start.11) | collective-permute-done | bytes 8224 | tf_op jit(solution)/shard_map/ppermute | solution.py:36
  29.0 2.2 %shard_map.35 = f32[1,2048]{1,0:T(1,128)S(1)} custom-call(f32[1,2048]{1,0:T(1,128)S(1)} %add.38.refs_0_, f32[1,2048]{1,0:T(1,128)S(1)} %collective-permute-done.12.refs_1_, f32[2048,2048]{1,0:T(8,128)S(1)} %get-tuple-element.57.refs_2_), custom_call_target="tpu_custom_call" | custom-call | flops 16777216 | bytes 1 | tf_op jit(solution)/shard_map/pallas_call | solution.py:84
  31.3 1.2 %collective-permute-done.13 = f32[1,2048]{1,0:T(1,128)S(1)} collective-permute-done((f32[1,2048]{1,0:T(1,128)S(1)}, f32[1,2048]{1,0:T(1,128)S(1)}, u32[]{:S(2)}, u32[]{:S(2)}) %collective-permute-start.13) | collective-permute-done | bytes 8224 | tf_op jit(solution)/shard_map/ppermute | solution.py:40
  32.5 1.5 %collective-permute-start.14 = (f32[1,2048]{1,0:T(1,128)S(1)}, f32[1,2048]{1,0:T(1,128)S(1)}, u32[]{:S(2)}, u32[]{:S(2)}) collective-permute-start(f32[1,2048]{1,0:T(1,128)S(1)} %add.39), channel_id=1, source_target_pairs={{0,6},{1,7},{2,4},{3,5},{4,2},{5,3},{6,0},{7,1},{8,14},{9,15},{10,... | collective-permute-start | bytes 24584 | tf_op jit(solution)/shard_map/ppermute | solution.py:36
  34.0 0.6 %collective-permute-start.15 = (f32[1,2048]{1,0:T(1,128)S(1)}, f32[1,2048]{1,0:T(1,128)S(1)}, u32[]{:S(2)}, u32[]{:S(2)}) collective-permute-start(f32[1,2048]{1,0:T(1,128)S(1)} %add.39), channel_id=1, source_target_pairs={{0,4},{1,5},{2,6},{3,7},{4,0},{5,1},{6,2},{7,3},{8,12},{9,13},{10,... | collective-permute-start | bytes 24584 | tf_op jit(solution)/shard_map/ppermute | solution.py:36
  34.6 2.3 %collective-permute-start.16 = (f32[1,2048]{1,0:T(1,128)S(1)}, f32[1,2048]{1,0:T(1,128)S(1)}, u32[]{:S(2)}, u32[]{:S(2)}) collective-permute-start(f32[1,2048]{1,0:T(1,128)S(1)} %add.39), channel_id=1, source_target_pairs={{0,2},{1,3},{2,0},{3,1},{4,6},{5,7},{6,4},{7,5},{8,10},{9,11},{10,... | collective-permute-start | bytes 24584 | tf_op jit(solution)/shard_map/ppermute | solution.py:36
  36.9 1.1 %collective-permute-done.14 = f32[1,2048]{1,0:T(1,128)S(1)} collective-permute-done((f32[1,2048]{1,0:T(1,128)S(1)}, f32[1,2048]{1,0:T(1,128)S(1)}, u32[]{:S(2)}, u32[]{:S(2)}) %collective-permute-start.14) | collective-permute-done | bytes 8224 | tf_op jit(solution)/shard_map/ppermute | solution.py:36
  38.6 1.4 %shard_map.36 = (f32[1,512]{1,0:T(1,128)S(1)}, f32[2048,128]{1,0:T(8,128)S(1)}) custom-call(f32[1,2048]{1,0:T(1,128)S(1)} %add.41.refs_0_, f32[1,2048]{1,0:T(1,128)S(1)} %collective-permute-done.16.refs_1_, f32[2048,2048]{1,0:T(8,128)S(1)} %get-tuple-element.57.refs_2_), custom_call_target="tpu_custom_call" | custom-call | flops 16777216 | bytes 1 | tf_op jit(solution)/shard_map/pallas_call | solution.py:84
  40.2 1.1 %collective-permute-done.17 = f32[1,512]{1,0:T(1,128)S(1)} collective-permute-done((f32[1,512]{1,0:T(1,128)S(1)}, f32[1,512]{1,0:T(1,128)S(1)}, u32[]{:S(2)}, u32[]{:S(2)}) %collective-permute-start.17) | collective-permute-done | bytes 2080 | tf_op jit(solution)/shard_map/ppermute | solution.py:40
  41.3 2.5 %collective-permute-start.18 = (f32[1,512]{1,0:T(1,128)S(1)}, f32[1,512]{1,0:T(1,128)S(1)}, u32[]{:S(2)}, u32[]{:S(2)}) collective-permute-start(f32[1,512]{1,0:T(1,128)S(1)} %add.42), channel_id=1, source_target_pairs={{0,6},{1,7},{2,4},{3,5},{4,2},{5,3},{6,0},{7,1},{8,14},{9,15},{10,... | collective-permute-start | bytes 6152 | tf_op jit(solution)/shard_map/ppermute | solution.py:36
  43.8 0.9 %collective-permute-start.19 = (f32[1,512]{1,0:T(1,128)S(1)}, f32[1,512]{1,0:T(1,128)S(1)}, u32[]{:S(2)}, u32[]{:S(2)}) collective-permute-start(f32[1,512]{1,0:T(1,128)S(1)} %add.42), channel_id=1, source_target_pairs={{0,4},{1,5},{2,6},{3,7},{4,0},{5,1},{6,2},{7,3},{8,12},{9,13},{10,... | collective-permute-start | bytes 6152 | tf_op jit(solution)/shard_map/ppermute | solution.py:36
  44.7 1.0 %collective-permute-start.20 = (f32[1,512]{1,0:T(1,128)S(1)}, f32[1,512]{1,0:T(1,128)S(1)}, u32[]{:S(2)}, u32[]{:S(2)}) collective-permute-start(f32[1,512]{1,0:T(1,128)S(1)} %add.42), channel_id=1, source_target_pairs={{0,2},{1,3},{2,0},{3,1},{4,6},{5,7},{6,4},{7,5},{8,10},{9,11},{10,... | collective-permute-start | bytes 6152 | tf_op jit(solution)/shard_map/ppermute | solution.py:36
  45.7 0.8 %shard_map.37.refs_2_ = f32[512,2048]{1,0:T(8,128)S(1)} custom-call(bf16[2048,256]{1,0:T(8,128)(2,1)S(1)} %get-tuple-element.47.unit_feat, bf16[2048,256]{1,0:T(8,128)(2,1)S(1)} %get-tuple-element.59.unit_proto, f32[2048,128]{1,0:T(8,128)S(1)} %get-tuple-element.60.col_factor), custom_call_target="tpu_custom_call" | custom-call | flops 536870912 | bytes 1 | tf_op jit(solution)/shard_map/pallas_call | solution.py:84
  46.7 1.6 %collective-permute-done.19 = f32[1,512]{1,0:T(1,128)S(1)} collective-permute-done((f32[1,512]{1,0:T(1,128)S(1)}, f32[1,512]{1,0:T(1,128)S(1)}, u32[]{:S(2)}, u32[]{:S(2)}) %collective-permute-start.19) | collective-permute-done | bytes 2080 | tf_op jit(solution)/shard_map/ppermute | solution.py:36
  48.3 1.5 %shard_map.38 = bf16[512,2048]{1,0:T(8,128)(2,1)} custom-call(f32[1,512]{1,0:T(1,128)S(1)} %add.44.refs_0_, f32[1,512]{1,0:T(1,128)S(1)} %collective-permute-done.20.refs_1_, f32[512,2048]{1,0:T(8,128)S(1)} %shard_map.37.refs_2_), custom_call_target="tpu_custom_call" | custom-call | tf_op jit(solution)/shard_map/pallas_call | solution.py:358
  (34 shorter events, 2.4 us)
Async XLA Ops:
  0.0 7.5 %collective-permute-start.2 = (bf16[512,256]{1,0:T(8,128)(2,1)}, bf16[512,256]{1,0:T(8,128)(2,1)S(1)}, u32[]{:S(2)}, u32[]{:S(2)}) collective-permute-start(bf16[512,256]{1,0:T(8,128)(2,1)} %feats.1), channel_id=1, source_target_pairs={{0,8},{1,17},{2,10},{3,19},{4,12},{5,21},{6,14},{7,23},{8,0},{9,25... | collective-permute-start | bytes 786440 | tf_op jit(solution)/shard_map/ppermute | solution.py:260
  4.3 6.4 %collective-permute-start = (bf16[512,256]{1,0:T(8,128)(2,1)S(1)}, bf16[512,256]{1,0:T(8,128)(2,1)S(1)}, u32[]{:S(2)}, u32[]{:S(2)}) collective-permute-start(bf16[512,256]{1,0:T(8,128)(2,1)S(1)} %get-tuple-element.37.own_proto), channel_id=1, source_target_pairs={{0,8},{1,17},{2,10},{3,19},{4,12},{5,21},{6,14},{7,23},{8,0},{9,25... | collective-permute-start | bytes 786440 | tf_op jit(solution)/shard_map/ppermute | solution.py:260
  7.5 5.4 %collective-permute-start.4 = (bf16[512,256]{1,0:T(8,128)(2,1)S(1)}, bf16[512,256]{1,0:T(8,128)(2,1)S(1)}, u32[]{:S(2)}, u32[]{:S(2)}) collective-permute-start(bf16[512,256]{1,0:T(8,128)(2,1)S(1)} %collective-permute-done.2.near), channel_id=1, source_target_pairs={{0,1},{1,0},{2,3},{3,2},{4,5},{5,4},{6,7},{7,6},{8,9},{9,8},{10,11... | collective-permute-start | bytes 786440 | tf_op jit(solution)/shard_map/ppermute | solution.py:40
  7.5 6.2 %collective-permute-start.3 = (bf16[256,256]{1,0:T(8,128)(2,1)S(1)}, bf16[256,256]{1,0:T(8,128)(2,1)S(1)}, u32[]{:S(2)}, u32[]{:S(2)}) collective-permute-start(bf16[256,256]{1,0:T(8,128)(2,1)S(1)} %constant_dynamic-slice_fusion), channel_id=1, source_target_pairs={{0,16},{1,9},{2,18},{3,11},{4,20},{5,13},{6,22},{7,15},{8,24},{9,1... | collective-permute-start | bytes 393224 | tf_op jit(solution)/shard_map/ppermute | solution.py:260
  9.6 7.0 %collective-permute-start.8 = (bf16[512,256]{1,0:T(8,128)(2,1)S(1)}, bf16[512,256]{1,0:T(8,128)(2,1)S(1)}, u32[]{:S(2)}, u32[]{:S(2)}) collective-permute-start(bf16[512,256]{1,0:T(8,128)(2,1)S(1)} %get-tuple-element.37.own_proto), channel_id=1, source_target_pairs={{0,16},{1,9},{2,18},{3,11},{4,20},{5,13},{6,22},{7,15},{8,24},{9,1... | collective-permute-start | bytes 786440 | tf_op jit(solution)/shard_map/ppermute | solution.py:260
  10.7 7.1 %collective-permute-start.7 = (bf16[320,256]{1,0:T(8,128)(2,1)S(1)}, bf16[320,256]{1,0:T(8,128)(2,1)S(1)}, u32[]{:S(2)}, u32[]{:S(2)}) collective-permute-start(bf16[320,256]{1,0:T(8,128)(2,1)S(1)} %slice.17), channel_id=1, source_target_pairs={{0,16},{1,9},{2,18},{3,11},{4,20},{5,13},{6,22},{7,15},{8,24},{9,1... | collective-permute-start | bytes 491528 | tf_op jit(solution)/shard_map/ppermute | solution.py:260
  12.4 6.4 %collective-permute-start.1 = (bf16[192,256]{1,0:T(8,128)(2,1)S(1)}, bf16[192,256]{1,0:T(8,128)(2,1)S(1)}, u32[]{:S(2)}, u32[]{:S(2)}) collective-permute-start(bf16[192,256]{1,0:T(8,128)(2,1)S(1)} %slice.16), channel_id=1, source_target_pairs={{0,16},{1,9},{2,18},{3,11},{4,20},{5,13},{6,22},{7,15},{8,24},{9,1... | collective-permute-start | bytes 294920 | tf_op jit(solution)/shard_map/ppermute | solution.py:260
  13.8 1.3 %collective-permute-start.5 = (bf16[128,256]{1,0:T(8,128)(2,1)S(1)}, bf16[128,256]{1,0:T(8,128)(2,1)S(1)}, u32[]{:S(2)}, u32[]{:S(2)}) collective-permute-start(bf16[128,256]{1,0:T(8,128)(2,1)S(1)} %get-tuple-element.62), channel_id=1, source_target_pairs={{0,1},{1,0},{2,3},{3,2},{4,5},{5,4},{6,7},{7,6},{8,9},{9,8},{10,11... | collective-permute-start | bytes 196616 | tf_op jit(solution)/shard_map/ppermute | solution.py:40
  13.8 1.4 %collective-permute-start.6 = (bf16[128,256]{1,0:T(8,128)(2,1)S(1)}, bf16[128,256]{1,0:T(8,128)(2,1)S(1)}, u32[]{:S(2)}, u32[]{:S(2)}) collective-permute-start(bf16[128,256]{1,0:T(8,128)(2,1)S(1)} %get-tuple-element.61), channel_id=1, source_target_pairs={{0,1},{1,0},{2,3},{3,2},{4,5},{5,4},{6,7},{7,6},{8,9},{9,8},{10,11... | collective-permute-start | bytes 196616 | tf_op jit(solution)/shard_map/ppermute | solution.py:40
  19.5 1.2 %collective-permute-start.9 = (f32[1,2048]{1,0:T(1,128)S(1)}, f32[1,2048]{1,0:T(1,128)S(1)}, u32[]{:S(2)}, u32[]{:S(2)}) collective-permute-start(f32[1,2048]{1,0:T(1,128)S(1)} %get-tuple-element.56), channel_id=1, source_target_pairs={{0,1},{1,0},{2,3},{3,2},{4,5},{5,4},{6,7},{7,6},{8,9},{9,8},{10,11... | collective-permute-start | bytes 24584 | tf_op jit(solution)/shard_map/ppermute | solution.py:40
  20.8 5.5 %collective-permute-start.10 = (f32[1,2048]{1,0:T(1,128)S(1)}, f32[1,2048]{1,0:T(1,128)S(1)}, u32[]{:S(2)}, u32[]{:S(2)}) collective-permute-start(f32[1,2048]{1,0:T(1,128)S(1)} %add.36), channel_id=1, source_target_pairs={{0,6},{1,7},{2,4},{3,5},{4,2},{5,3},{6,0},{7,1},{8,14},{9,15},{10,... | collective-permute-start | bytes 24584 | tf_op jit(solution)/shard_map/ppermute | solution.py:36
  24.4 4.5 %collective-permute-start.11 = (f32[1,2048]{1,0:T(1,128)S(1)}, f32[1,2048]{1,0:T(1,128)S(1)}, u32[]{:S(2)}, u32[]{:S(2)}) collective-permute-start(f32[1,2048]{1,0:T(1,128)S(1)} %add.36), channel_id=1, source_target_pairs={{0,4},{1,5},{2,6},{3,7},{4,0},{5,1},{6,2},{7,3},{8,12},{9,13},{10,... | collective-permute-start | bytes 24584 | tf_op jit(solution)/shard_map/ppermute | solution.py:36
  24.4 4.6 %collective-permute-start.12 = (f32[1,2048]{1,0:T(1,128)S(1)}, f32[1,2048]{1,0:T(1,128)S(1)}, u32[]{:S(2)}, u32[]{:S(2)}) collective-permute-start(f32[1,2048]{1,0:T(1,128)S(1)} %add.36), channel_id=1, source_target_pairs={{0,2},{1,3},{2,0},{3,1},{4,6},{5,7},{6,4},{7,5},{8,10},{9,11},{10,... | collective-permute-start | bytes 24584 | tf_op jit(solution)/shard_map/ppermute | solution.py:36
  31.2 1.2 %collective-permute-start.13 = (f32[1,2048]{1,0:T(1,128)S(1)}, f32[1,2048]{1,0:T(1,128)S(1)}, u32[]{:S(2)}, u32[]{:S(2)}) collective-permute-start(f32[1,2048]{1,0:T(1,128)S(1)} %shard_map.35), channel_id=1, source_target_pairs={{0,1},{1,0},{2,3},{3,2},{4,5},{5,4},{6,7},{7,6},{8,9},{9,8},{10,11... | collective-permute-start | bytes 24584 | tf_op jit(solution)/shard_map/ppermute | solution.py:40
  32.5 5.6 %collective-permute-start.14 = (f32[1,2048]{1,0:T(1,128)S(1)}, f32[1,2048]{1,0:T(1,128)S(1)}, u32[]{:S(2)}, u32[]{:S(2)}) collective-permute-start(f32[1,2048]{1,0:T(1,128)S(1)} %add.39), channel_id=1, source_target_pairs={{0,6},{1,7},{2,4},{3,5},{4,2},{5,3},{6,0},{7,1},{8,14},{9,15},{10,... | collective-permute-start | bytes 24584 | tf_op jit(solution)/shard_map/ppermute | solution.py:36
  34.0 4.6 %collective-permute-start.15 = (f32[1,2048]{1,0:T(1,128)S(1)}, f32[1,2048]{1,0:T(1,128)S(1)}, u32[]{:S(2)}, u32[]{:S(2)}) collective-permute-start(f32[1,2048]{1,0:T(1,128)S(1)} %add.39), channel_id=1, source_target_pairs={{0,4},{1,5},{2,6},{3,7},{4,0},{5,1},{6,2},{7,3},{8,12},{9,13},{10,... | collective-permute-start | bytes 24584 | tf_op jit(solution)/shard_map/ppermute | solution.py:36
  34.6 4.0 %collective-permute-start.16 = (f32[1,2048]{1,0:T(1,128)S(1)}, f32[1,2048]{1,0:T(1,128)S(1)}, u32[]{:S(2)}, u32[]{:S(2)}) collective-permute-start(f32[1,2048]{1,0:T(1,128)S(1)} %add.39), channel_id=1, source_target_pairs={{0,2},{1,3},{2,0},{3,1},{4,6},{5,7},{6,4},{7,5},{8,10},{9,11},{10,... | collective-permute-start | bytes 24584 | tf_op jit(solution)/shard_map/ppermute | solution.py:36
  40.1 1.2 %collective-permute-start.17 = (f32[1,512]{1,0:T(1,128)S(1)}, f32[1,512]{1,0:T(1,128)S(1)}, u32[]{:S(2)}, u32[]{:S(2)}) collective-permute-start(f32[1,512]{1,0:T(1,128)S(1)} %get-tuple-element.58), channel_id=1, source_target_pairs={{0,1},{1,0},{2,3},{3,2},{4,5},{5,4},{6,7},{7,6},{8,9},{9,8},{10,11... | collective-permute-start | bytes 6152 | tf_op jit(solution)/shard_map/ppermute | solution.py:40
  41.3 5.4 %collective-permute-start.18 = (f32[1,512]{1,0:T(1,128)S(1)}, f32[1,512]{1,0:T(1,128)S(1)}, u32[]{:S(2)}, u32[]{:S(2)}) collective-permute-start(f32[1,512]{1,0:T(1,128)S(1)} %add.42), channel_id=1, source_target_pairs={{0,6},{1,7},{2,4},{3,5},{4,2},{5,3},{6,0},{7,1},{8,14},{9,15},{10,... | collective-permute-start | bytes 6152 | tf_op jit(solution)/shard_map/ppermute | solution.py:36
  43.8 4.5 %collective-permute-start.19 = (f32[1,512]{1,0:T(1,128)S(1)}, f32[1,512]{1,0:T(1,128)S(1)}, u32[]{:S(2)}, u32[]{:S(2)}) collective-permute-start(f32[1,512]{1,0:T(1,128)S(1)} %add.42), channel_id=1, source_target_pairs={{0,4},{1,5},{2,6},{3,7},{4,0},{5,1},{6,2},{7,3},{8,12},{9,13},{10,... | collective-permute-start | bytes 6152 | tf_op jit(solution)/shard_map/ppermute | solution.py:36
  44.7 3.6 %collective-permute-start.20 = (f32[1,512]{1,0:T(1,128)S(1)}, f32[1,512]{1,0:T(1,128)S(1)}, u32[]{:S(2)}, u32[]{:S(2)}) collective-permute-start(f32[1,512]{1,0:T(1,128)S(1)} %add.42), channel_id=1, source_target_pairs={{0,2},{1,3},{2,0},{3,1},{4,6},{5,7},{6,4},{7,5},{8,10},{9,11},{10,... | collective-permute-start | bytes 6152 | tf_op jit(solution)/shard_map/ppermute | solution.py:36
